TPU v7x, 32 devices: a whole 2x2x4 slice. The times are simulated.
32 devices in a mesh: dp: 8 (over z, y), shard: 4 (over x, core).
Axes of the slice: x: 2, y: 2, z: 4, core: 2. Of those that a mesh axis runs over, the one named last changes fastest.
Arguments:
- images: bfloat16 [2, 160, 12, 12, 256], P(None, ('dp', 'shard')), may hold values from -6 to 6
- bucket: int32 [8], P('dp'), may hold values from 0 to 2
- counts: int32 [2, 32], P(None, ('dp', 'shard')), may hold values from 2 to 5, as said below
- balance: int32 [2, 160], P(None, ('dp', 'shard')), may hold values from 1 to 4
- labels: int32 [2, 160], P(None, ('dp', 'shard')), may hold values from 0 to 999
- step: int32 [1], replicated, may hold values from 2 to 20
- expand_w: float32 [2, 256, 3072], P(None, 'shard'), may hold values from -0.375 to 0.375
- expand_m: float32 [2, 256, 3072], P(None, 'shard'), may hold values from -6.1035156e-05 to 6.1035156e-05
- expand_v: float32 [2, 256, 3072], P(None, 'shard'), may hold values from 3.4375e-11 to 5.625e-10
- expand_e: float32 [2, 256, 3072], P(None, 'shard'), may hold values from -0.375 to 0.375
- chan_w: float32 [2, 137, 1536], P(None, None, 'shard'), may hold values from -0.75 to 0.75
- chan_m: float32 [2, 137, 1536], P(None, None, 'shard'), may hold values from -6.1035156e-05 to 6.1035156e-05
- chan_v: float32 [2, 137, 1536], P(None, None, 'shard'), may hold values from 3.4375e-11 to 5.625e-10
- chan_e: float32 [2, 137, 1536], P(None, None, 'shard'), may hold values from -0.75 to 0.75
- head_w: float32 [256, 1280], P(None, 'shard'), may hold values from -0.375 to 0.375
- head_m: float32 [256, 1280], P(None, 'shard'), may hold values from -6.1035156e-05 to 6.1035156e-05
- head_v: float32 [256, 1280], P(None, 'shard'), may hold values from 5e-11 to 8.125e-10
- head_e: float32 [256, 1280], P(None, 'shard'), may hold values from -0.375 to 0.375
- class_w: float32 [1280, 1000], P('shard'), may hold values from -0.3125 to 0.3125
- class_m: float32 [1280, 1000], P('shard'), may hold values from -0.0007324219 to 0.0007324219
- class_v: float32 [1280, 1000], P('shard'), may hold values from 6.25e-09 to 1e-07
- class_e: float32 [1280, 1000], P('shard'), may hold values from -0.3125 to 0.3125
- gain_w: float32 [4, 5018], P('shard'), may hold values from 0.25 to 1.75
- gain_m: float32 [4, 5018], P('shard'), may hold values from -0.00010681152 to 0.00010681152
- gain_v: float32 [4, 5018], P('shard'), may hold values from 1.40625e-10 to 2.25e-09
- gain_e: float32 [4, 5018], P('shard'), may hold values from 0.25 to 1.75
Outputs:
- loss: float32 [], replicated
- expand_new: float32 [2, 256, 3072], P(None, 'shard')
- expand_first: float32 [2, 256, 3072], P(None, 'shard')
- expand_second: float32 [2, 256, 3072], P(None, 'shard')
- expand_avg: float32 [2, 256, 3072], P(None, 'shard')
- chan_new: float32 [2, 137, 1536], P(None, None, 'shard')
- chan_first: float32 [2, 137, 1536], P(None, None, 'shard')
- chan_second: float32 [2, 137, 1536], P(None, None, 'shard')
- chan_avg: float32 [2, 137, 1536], P(None, None, 'shard')
- head_new: float32 [256, 1280], P(None, 'shard')
- head_first: float32 [256, 1280], P(None, 'shard')
- head_second: float32 [256, 1280], P(None, 'shard')
- head_avg: float32 [256, 1280], P(None, 'shard')
- class_new: float32 [1280, 1000], P('shard')
- class_first: float32 [1280, 1000], P('shard')
- class_second: float32 [1280, 1000], P('shard')
- class_avg: float32 [1280, 1000], P('shard')
- gain_new: float32 [4, 5018], P('shard')
- gain_first: float32 [4, 5018], P('shard')
- gain_second: float32 [4, 5018], P('shard')
- gain_avg: float32 [4, 5018], P('shard')
- norms: float32 [2, 12], replicated
Inputs may be any that keep to these rules, and one draw needn't show every extreme that they name: `bucket`: 0, 1, 2 stand for images of 7 x 7, 10 x 10 and 12 x 12 pixels at the upper left of each slot. A device's valid images are its first counts slots; in every micro-batch some device holds 5 images.
All inputs are finite; a program needn't handle non-finite values.
Results may differ from a plain program's by a relative error of at most 0.01065.
The roundings to bfloat16 on the way count: a program that leaves them out, or rounds other values in their place, can miss the bound.
Values may be sent and summed in bfloat16 or wider, within the bound.
A program may use at most 448 MiB of HBM per device.

v0:
```python
import jax
import jax.numpy as jnp
from jax import lax
from jax.sharding import PartitionSpec as P

C = 256
E = 1536
SE = 64
HEAD = 1280
CLASSES = 1000
L = 2
S = 12


EPS_NORM = 1e-05
BETA_ONE = 0.9
BETA_TWO = 0.99
EPS_ADAM = 1e-08
DECAY = 0.01
RATE = 0.3
KEEP = 0.9


def contract(left, right, left_dim, right_dim):
    return lax.dot_general(
        left, right, (((left_dim,), (right_dim,)), ((), ())), preferred_element_type=jnp.float32
    )


def matmul(left, right):
    return jnp.dot(left, right, precision=lax.Precision.HIGHEST, preferred_element_type=jnp.float32)


def matmul_bt(left, right):
    return lax.dot_general(
        left,
        right,
        (((1,), (1,)), ((), ())),
        precision=lax.Precision.HIGHEST,
        preferred_element_type=jnp.float32,
    )


def norm_stats(values, masks, counts):
    sums_first = jnp.stack([jnp.sum(masks[0] * values[0], 0)])
    sums_second = jnp.stack([jnp.sum(masks[0] * values[0] * values[0], 0)])
    sums = lax.psum((sums_first, sums_second), ("dp", "shard"))
    mean = sums[0][0] / counts[0]
    scale = lax.rsqrt(sums[1][0] / counts[0] - mean * mean + EPS_NORM)
    result = [(mean, scale)]
    return result


def norm_apply(value, mask, gain, shift, mean, scale):
    return mask * (gain * ((value - mean) * scale) + shift)


def norm_back(grads, values, masks, gains, stats, counts):
    units = (values[0] - stats[0][0]) * stats[0][1]
    inners = masks[0] * grads[0] * gains[0]
    sums_first = jnp.stack([jnp.sum(inners, 0)])
    sums_second = jnp.stack([jnp.sum(inners * units, 0)])
    sums = lax.psum((sums_first, sums_second), ("dp", "shard"))
    gain_grad = jnp.sum(masks[0] * grads[0] * units, 0)
    shift_grad = jnp.sum(masks[0] * grads[0], 0)
    back = (
        masks[0] * stats[0][1] * (inners - sums[0][0] / counts[0] - units * sums[1][0] / counts[0])
    )
    result = [(back, gain_grad, shift_grad)]
    return result


def spread(first, taps):
    image = jax.nn.silu(first).reshape(-1, S, S, first.shape[-1])
    padded = jnp.pad(image, ((0, 0), (1, 1), (1, 1), (0, 0)))
    total = jnp.zeros_like(image)
    for offset in range(9):
        total = (
            total
            + padded[:, offset // 3 : offset // 3 + S, offset % 3 : offset % 3 + S, :]
            * taps[offset]
        )
    return total.reshape(first.shape)


def pool(value, area):
    return jnp.sum(value.reshape(area.shape[0], S * S, value.shape[-1]), 1) / area[:, None]


def excite(second, se_part, excite_bias, squeeze_bias, area):
    active = jax.nn.silu(second)
    pooled = pool(active, area)
    squeezed = jax.nn.silu(matmul_bt(pooled, se_part[:SE]) + squeeze_bias)
    gate = jax.nn.sigmoid(matmul(squeezed, se_part[SE:]) + excite_bias)
    shaped = active.reshape(area.shape[0], S * S, active.shape[-1])
    return (shaped * gate[:, None, :]).reshape(second.shape)


def unpack_gains(gains):
    rows = gains.shape[0]
    widths = []
    for layer in range(L):
        widths = widths + [E, E, E, E, E, C, C, SE]
    widths = widths + [HEAD, HEAD, CLASSES]
    parts = []
    start = 0
    for width in widths:
        piece = width // rows
        parts.append(gains[:, start : start + piece].reshape(-1))
        start = start + piece
    return parts


def pack_gains(vectors, rows):
    return jnp.concatenate([vector.reshape(rows, -1) for vector in vectors], 1)


def block_forward(hiddens, mats, chans, gainsets, masks, area, counts):
    width = mats[0].shape[1] // 2
    hidden_lows = [h.astype(jnp.bfloat16) for h in hiddens]
    pres = [jnp.dot(hidden_lows[0], mats[0][:, :width], preferred_element_type=jnp.float32)]
    stats_one = norm_stats(pres, masks, counts)
    firsts = norm_apply(
        pres[0], masks[0], gainsets[0][0], gainsets[0][1], stats_one[0][0], stats_one[0][1]
    )
    mixeds = [spread(firsts, chans[0][:9].astype(jnp.float32))]
    stats_two = norm_stats(mixeds, masks, counts)
    seconds = norm_apply(
        mixeds[0], masks[0], gainsets[0][2], gainsets[0][3], stats_two[0][0], stats_two[0][1]
    )
    scaleds = excite(
        seconds, chans[0][9:].astype(jnp.float32), gainsets[0][4], gainsets[0][7], area
    ).astype(jnp.bfloat16)
    outs = [contract(scaleds, mats[0][:, width:], 1, 1)]
    stats_three = norm_stats(outs, masks, counts)
    fresh = [
        hiddens[0]
        + norm_apply(
            outs[0], masks[0], gainsets[0][5], gainsets[0][6], stats_three[0][0], stats_three[0][1]
        )
    ]
    kept = [
        (
            hidden_lows[0],
            pres[0],
            stats_one[0],
            mixeds[0],
            stats_two[0],
            scaleds,
            outs[0],
            stats_three[0],
        )
    ]
    return (fresh, kept)


def block_backward(grad_hiddens, mats, chans, gainsets, kepts, masks, area, counts):
    width = mats[0].shape[1] // 2
    backs_three = norm_back(
        grad_hiddens, [kepts[0][6]], masks, [gainsets[0][5]], [kepts[0][7]], counts
    )
    k = 0
    hidden_low, pre, stats_one, mixed, stats_two, scaled, out, stats_three = kepts[k]
    grad_out_low = backs_three[k][0].astype(jnp.bfloat16)
    grad_project = contract(grad_out_low, scaled, 0, 0)
    grad_scaled = jnp.dot(grad_out_low, mats[k][:, width:], preferred_element_type=jnp.float32)
    second = norm_apply(mixed, masks[k], gainsets[k][2], gainsets[k][3], stats_two[0], stats_two[1])
    excite_part = lambda value, se_part, bias_x, bias_r: excite(
        value, se_part, bias_x, bias_r, area
    )
    unused, pull = jax.vjp(
        excite_part, second, chans[k][9:].astype(jnp.float32), gainsets[k][4], gainsets[k][7]
    )
    grad_second, grad_se, grad_excite_bias, grad_squeeze_bias = pull(grad_scaled)
    grad_seconds = [grad_second]
    middle = [(grad_project, grad_se, grad_excite_bias, grad_squeeze_bias)]
    backs_two = norm_back(
        grad_seconds, [kepts[0][3]], masks, [gainsets[0][2]], [kepts[0][4]], counts
    )
    k = 0
    pre = kepts[k][1]
    stats_one = kepts[k][2]
    first = norm_apply(pre, masks[k], gainsets[k][0], gainsets[k][1], stats_one[0], stats_one[1])
    unused, pull = jax.vjp(spread, first, chans[k][:9].astype(jnp.float32))
    grad_first, grad_taps = pull(backs_two[k][0])
    grad_firsts = [grad_first]
    taps_grads = [grad_taps]
    backs_one = norm_back(
        grad_firsts, [kepts[0][1]], masks, [gainsets[0][0]], [kepts[0][2]], counts
    )
    k = 0
    grad_pre_low = backs_one[k][0].astype(jnp.bfloat16)
    grad_expand = contract(kepts[k][0], grad_pre_low, 0, 0)
    grad_below = grad_hiddens[k] + contract(grad_pre_low, mats[k][:, :width], 1, 1)
    grad_project, grad_se, grad_excite_bias, grad_squeeze_bias = middle[k]
    grad_mats = jnp.concatenate([grad_expand, grad_project], 1)
    grad_chan = jnp.concatenate([taps_grads[k], grad_se], 0)
    grad_gains = [
        backs_one[k][1],
        backs_one[k][2],
        backs_two[k][1],
        backs_two[k][2],
        grad_excite_bias,
        backs_three[k][1],
        backs_three[k][2],
        grad_squeeze_bias,
    ]
    result = [(grad_below, grad_mats, grad_chan, grad_gains)]
    return result


def run_forward(models, rows_list, masks, area, counts):
    gainsets_all = [unpack_gains(m[4].astype(jnp.float32)) for m in models]
    layers = models[0][0].shape[0]
    hiddens = rows_list
    kept_blocks = []
    for layer in range(layers):
        hiddens, kept = block_forward(
            hiddens,
            [m[0][layer] for m in models],
            [m[1][layer] for m in models],
            [g[8 * layer : 8 * layer + 8] for g in gainsets_all],
            masks,
            area,
            counts,
        )
        kept_blocks.append(kept)
    heads = [g[8 * layers : 8 * layers + 3] for g in gainsets_all]
    hidden_lows = [h.astype(jnp.bfloat16) for h in hiddens]
    feats = [jnp.dot(hidden_lows[0], models[0][2], preferred_element_type=jnp.float32)]
    stats_head = norm_stats(feats, masks, counts)
    normed = norm_apply(
        feats[0], masks[0], heads[0][0], heads[0][1], stats_head[0][0], stats_head[0][1]
    )
    pooled_low = pool(jax.nn.silu(normed), area).astype(jnp.bfloat16)
    logits_all = [
        jnp.dot(pooled_low, models[0][3], preferred_element_type=jnp.float32) + heads[0][2]
    ]
    kept_heads = [(hidden_lows[0], feats[0], stats_head[0], pooled_low)]
    return (logits_all, kept_blocks, kept_heads)


def head_backward(grad_logits_all, model, kept_heads, masks, area, counts):
    count_all = len(grad_logits_all)
    layers = model[0].shape[0]
    gains = unpack_gains(model[4].astype(jnp.float32))
    head_gain, head_shift, class_bias = gains[8 * layers : 8 * layers + 3]
    k = 0
    hidden_low, feat, stats_head, pooled_low = kept_heads[k]
    grad_low = grad_logits_all[k].astype(jnp.bfloat16)
    grad_classes = contract(pooled_low, grad_low, 0, 0)
    grad_class_bias = jnp.sum(grad_low.astype(jnp.float32), 0)
    grad_pooled = contract(grad_low, model[3], 1, 1)
    normed = norm_apply(feat, masks[k], head_gain, head_shift, stats_head[0], stats_head[1])
    unused, pull = jax.vjp(lambda value: pool(jax.nn.silu(value), area), normed)
    (grad_normed,) = pull(grad_pooled)
    grad_normeds = [grad_normed]
    partial_heads = [(grad_classes, grad_class_bias)]
    backs = norm_back(
        grad_normeds, [kept_heads[0][1]], masks, [head_gain] * count_all, [kept_heads[0][2]], counts
    )
    k = 0
    grad_feat_low = backs[k][0].astype(jnp.bfloat16)
    grad_head = contract(kept_heads[k][0], grad_feat_low, 0, 0)
    grad_hidden = contract(grad_feat_low, model[2], 1, 1)
    head_tail = [backs[k][1], backs[k][2], partial_heads[k][1]]
    result = [(grad_hidden, grad_head, partial_heads[k][0], head_tail)]
    return result


def objective(logits, target, onehot, coef):
    logp = jax.nn.log_softmax(logits)
    per = -jnp.sum(onehot * logp, 1) + jnp.sum(jnp.exp(target) * (target - logp), 1)
    return jnp.sum(coef * per)


def own_slice(value, dim, parts, place):
    width = value.shape[dim] // parts
    return lax.dynamic_slice_in_dim(value, place * width, width, dim)


def mats_groups(value):
    rows = jnp.sum(value * value, 1)
    half = rows.shape[1] // 2
    return jnp.stack([jnp.sum(rows[:, :half], 1), jnp.sum(rows[:, half:], 1)], 1).reshape(-1)


def chan_groups(value):
    rows = jnp.sum(value * value, 2)
    return jnp.stack(
        [jnp.sum(rows[:, :9], 1), jnp.sum(rows[:, 9 : 9 + SE], 1), jnp.sum(rows[:, 9 + SE :], 1)], 1
    ).reshape(-1)


def mats_factor(ratio, value):
    paired = ratio.reshape(-1, 2)
    column = jnp.arange(value.shape[2])
    return jnp.where(column[None, :] < value.shape[2] // 2, paired[:, 0:1], paired[:, 1:2])[
        :, None, :
    ]


def chan_factor(ratio, value):
    triple = ratio.reshape(-1, 3)
    row = jnp.arange(value.shape[1])[None, :]
    return jnp.where(
        row < 9, triple[:, 0:1], jnp.where(row < 9 + SE, triple[:, 1:2], triple[:, 2:3])
    )[:, :, None]


def adapt(first, second, grad, first_fix, second_fix):
    new_first = BETA_ONE * first + (1.0 - BETA_ONE) * grad
    new_second = BETA_TWO * second + (1.0 - BETA_TWO) * grad * grad
    update = new_first / first_fix / (jnp.sqrt(new_second / second_fix) + EPS_ADAM)
    return (new_first, new_second, update)


def per_device(
    images,
    bucket,
    counts,
    balance,
    labels,
    step,
    expand_w,
    expand_m,
    expand_v,
    expand_e,
    chan_w,
    chan_m,
    chan_v,
    chan_e,
    head_w,
    head_m,
    head_v,
    head_e,
    class_w,
    class_m,
    class_v,
    class_e,
    gain_w,
    gain_m,
    gain_v,
    gain_e,
):
    full = (
        lax.all_gather(expand_w.astype(jnp.bfloat16), "shard", axis=1, tiled=True),
        lax.all_gather(chan_w.astype(jnp.bfloat16), "shard", axis=2, tiled=True),
        lax.all_gather(head_w.astype(jnp.bfloat16), "shard", axis=1, tiled=True),
        lax.all_gather(class_w.astype(jnp.bfloat16), "shard", axis=0, tiled=True),
        lax.all_gather(gain_w.astype(jnp.bfloat16), "shard", axis=0, tiled=True),
        lax.all_gather(expand_e.astype(jnp.bfloat16), "shard", axis=1, tiled=True),
        lax.all_gather(chan_e.astype(jnp.bfloat16), "shard", axis=2, tiled=True),
        lax.all_gather(head_e.astype(jnp.bfloat16), "shard", axis=1, tiled=True),
        lax.all_gather(class_e.astype(jnp.bfloat16), "shard", axis=0, tiled=True),
        lax.all_gather(gain_e.astype(jnp.bfloat16), "shard", axis=0, tiled=True),
    )
    model = full[:5]
    shadow = full[5:]
    batches = images.shape[0]
    slots = images.shape[1]
    code = bucket[0]
    side = jnp.where(code == 0, 7, jnp.where(code == 1, 10, 12))
    spot = jnp.arange(S * S)
    inside = ((spot // S < side) & (spot % S < side)).astype(jnp.float32)
    area_value = (side * side).astype(jnp.float32)
    area = jnp.full((slots,), area_value)
    valid = (jnp.arange(slots)[None, :] < counts).astype(jnp.float32)
    weighted = valid * balance.astype(jnp.float32)
    pixels, weight_sums = lax.psum(
        (jnp.sum(valid, 1) * area_value, jnp.sum(weighted, 1)), ("dp", "shard")
    )
    total_weight = jnp.sum(weight_sums)
    layers = model[0].shape[0]
    rows_all = [
        images[index].astype(jnp.float32).reshape(-1, images.shape[-1]) for index in range(batches)
    ]
    masks_all = [
        (valid[index][:, None] * inside[None, :]).reshape(-1, 1) for index in range(batches)
    ]
    counts_all = [pixels[index] for index in range(batches)]
    forward_groups = []
    for index in range(batches):
        forward_groups = forward_groups + [[(0, index)], [(1, index)]]
    backward_groups = [[index] for index in range(batches)]
    targets = [None] * batches
    main_logits = [None] * batches
    main_blocks = [None] * batches
    main_heads = [None] * batches
    for group in forward_groups:
        models = [shadow if kind == 0 else model for kind, index in group]
        logits_all, kept_blocks, kept_heads = run_forward(
            models,
            [rows_all[index] for kind, index in group],
            [masks_all[index] for kind, index in group],
            area,
            [counts_all[index] for kind, index in group],
        )
        place = 0
        kind, index = group[place]
        if kind == 0:
            targets[index] = jax.nn.log_softmax(logits_all[place])
        else:
            main_logits[index] = logits_all[place]
            main_blocks[index] = [kept_blocks[layer][place] for layer in range(layers)]
            main_heads[index] = kept_heads[place]
    grad_mats = jnp.zeros(model[0].shape, jnp.float32)
    grad_chan = jnp.zeros(model[1].shape, jnp.float32)
    grad_head = jnp.zeros(model[2].shape, jnp.float32)
    grad_class = jnp.zeros(model[3].shape, jnp.float32)
    grad_gain = jnp.zeros(model[4].shape, jnp.float32)
    loss = jnp.float32(0.0)
    gain_list = unpack_gains(model[4].astype(jnp.float32))
    for group in backward_groups:
        grad_logits_all = []
        for index in group:
            onehot = (
                labels[index][:, None] == jnp.arange(main_logits[index].shape[1])[None, :]
            ).astype(jnp.float32)
            coef = weighted[index] / total_weight
            target = targets[index]
            part, pull = jax.vjp(
                lambda value: objective(value, target, onehot, coef), main_logits[index]
            )
            (grad_logits,) = pull(jnp.float32(1.0))
            loss = loss + part
            grad_logits_all.append(grad_logits)
        masks = [masks_all[index] for index in group]
        group_counts = [counts_all[index] for index in group]
        head_parts = head_backward(
            grad_logits_all,
            model,
            [main_heads[index] for index in group],
            masks,
            area,
            group_counts,
        )
        grad_hiddens = [item[0] for item in head_parts]
        mats_parts = [[None] * layers for index in group]
        chan_parts = [[None] * layers for index in group]
        gain_parts = [[None] * layers for index in group]
        for layer in reversed(range(layers)):
            size = len(group)
            backs = block_backward(
                grad_hiddens,
                [model[0][layer]] * size,
                [model[1][layer]] * size,
                [gain_list[8 * layer : 8 * layer + 8]] * size,
                [main_blocks[index][layer] for index in group],
                masks,
                area,
                group_counts,
            )
            grad_hiddens = [item[0] for item in backs]
            place = 0
            mats_parts[place][layer] = backs[place][1]
            chan_parts[place][layer] = backs[place][2]
            gain_parts[place][layer] = backs[place][3]
        place = 0
        grad_mats = grad_mats + jnp.stack(mats_parts[place])
        grad_chan = grad_chan + jnp.stack(chan_parts[place])
        grad_head = grad_head + head_parts[place][1]
        grad_class = grad_class + head_parts[place][2]
        vectors = []
        for layer in range(layers):
            vectors = vectors + gain_parts[place][layer]
        vectors = vectors + head_parts[place][3]
        grad_gain = grad_gain + pack_gains(vectors, grad_gain.shape[0])
    shards = lax.axis_size("shard")
    loss_spread = jnp.full((shards,), loss)
    summed = lax.psum(
        (loss_spread, grad_mats, grad_chan, grad_head, grad_class, grad_gain), ("dp", "shard")
    )
    place = lax.axis_index("shard")
    owned = (
        summed[0][0:1],
        own_slice(summed[1], 1, shards, place),
        own_slice(summed[2], 2, shards, place),
        own_slice(summed[3], 1, shards, place),
        own_slice(summed[4], 0, shards, place),
        own_slice(summed[5], 0, shards, place),
    )
    total_loss = owned[0][0]
    power = step[0].astype(jnp.float32)
    first_fix = 1.0 - jnp.power(jnp.float32(BETA_ONE), power)
    second_fix = 1.0 - jnp.power(jnp.float32(BETA_TWO), power)
    weights = (expand_w, chan_w, head_w, class_w, gain_w)
    firsts = (expand_m, chan_m, head_m, class_m, gain_m)
    seconds = (expand_v, chan_v, head_v, class_v, gain_v)
    averaged = (expand_e, chan_e, head_e, class_e, gain_e)
    states = [
        adapt(firsts[item], seconds[item], owned[item + 1], first_fix, second_fix)
        for item in range(5)
    ]
    updates = [states[item][2] + DECAY * weights[item] for item in range(4)]
    local_weight_sq = jnp.concatenate(
        [
            mats_groups(expand_w),
            chan_groups(chan_w),
            jnp.sum(head_w * head_w)[None],
            jnp.sum(class_w * class_w)[None],
        ]
    )
    local_update_sq = jnp.concatenate(
        [
            mats_groups(updates[0]),
            chan_groups(updates[1]),
            jnp.sum(updates[2] * updates[2])[None],
            jnp.sum(updates[3] * updates[3])[None],
        ]
    )
    weight_sq, update_sq = lax.psum((local_weight_sq, local_update_sq), "shard")
    ratio = jnp.sqrt(weight_sq) / jnp.sqrt(update_sq)
    count_mats = 2 * layers
    count_chan = 3 * layers
    factors = [
        mats_factor(ratio[:count_mats], expand_w),
        chan_factor(ratio[count_mats : count_mats + count_chan], chan_w),
        ratio[count_mats + count_chan],
        ratio[count_mats + count_chan + 1],
    ]
    result = [total_loss]
    for item in range(5):
        if item < 4:
            fresh = weights[item] - RATE * factors[item] * updates[item]
        else:
            fresh = weights[item] - RATE * states[item][2]
        result = result + [
            fresh,
            states[item][0],
            states[item][1],
            KEEP * averaged[item] + (1.0 - KEEP) * fresh,
        ]
    norms = jnp.stack([jnp.sqrt(weight_sq), jnp.sqrt(update_sq)])
    return tuple(result + [norms])


def solution(mesh):
    in_specs = (
        P(None, ("dp", "shard"), None, None, None),
        P("dp"),
        P(None, ("dp", "shard")),
        P(None, ("dp", "shard")),
        P(None, ("dp", "shard")),
        P(),
        P(None, "shard", None),
        P(None, "shard", None),
        P(None, "shard", None),
        P(None, "shard", None),
        P(None, None, "shard"),
        P(None, None, "shard"),
        P(None, None, "shard"),
        P(None, None, "shard"),
        P(None, "shard"),
        P(None, "shard"),
        P(None, "shard"),
        P(None, "shard"),
        P("shard", None),
        P("shard", None),
        P("shard", None),
        P("shard", None),
        P("shard", None),
        P("shard", None),
        P("shard", None),
        P("shard", None),
    )
    out_specs = (
        P(),
        P(None, "shard", None),
        P(None, "shard", None),
        P(None, "shard", None),
        P(None, "shard", None),
        P(None, None, "shard"),
        P(None, None, "shard"),
        P(None, None, "shard"),
        P(None, None, "shard"),
        P(None, "shard"),
        P(None, "shard"),
        P(None, "shard"),
        P(None, "shard"),
        P("shard", None),
        P("shard", None),
        P("shard", None),
        P("shard", None),
        P("shard", None),
        P("shard", None),
        P("shard", None),
        P("shard", None),
        P(),
    )
    return jax.shard_map(
        per_device, mesh=mesh, in_specs=in_specs, out_specs=out_specs, check_vma=False
    )
```

profile of v0, /device:TPU:0, one launch (start us, length us, event | category | flops | bytes accessed | tf_op | source)
XLA Modules:
  0.0 2149.2 jit_solution(11912719452517257703)
XLA Ops:
  17.2 6.2 all-gather.1
  24.4 6.2 all-gather
  31.2 13.9 all_gather.37
  48.3 9.1 all_gather.32
  83.5 11.0 all_gather.33
  94.5 13.2 all_gather.38
  135.1 41.4 %all-reduce.104 = (f32[1,1536]{1,0:T(1,128)S(1)}, f32[2]{0:T(128)S(1)}, f32[1,1536]{1,0:T(1,128)S(1)}, f32[1,1536]{1,0:T(1,128)S(1)}, f32[1,1536]{1,0:T(1,128)S(1)}) all-reduce(f32[1,1536]{1,0:T(1,128)S(1)} %stack.339, f32[2]{0:T(128)S(1)} %broadcast_multiply_fusion.40, ...), channel_id=1, replica_groups=mesh['dp'=8,'shard'=4] {'dp','shard'}, use_global_device_ids=true, to_apply=%region_4.5 | all-reduce | flops 6146 | bytes 49168 | tf_op jit(solution)/shard_map/psum | solution.py:47
  178.7 7.6 fusion.117
  197.6 41.3 %fusion.68 = (f32[1536]{0:T(1024)S(1)}, f32[1536]{0:T(1024)S(1)}, f32[5,12,12,1536]{3,2,1,0:T(8,128)}, f32[1536]{0:T(1024)S(1)}, f32[1536]{0:T(1024)S(1)}, /*index=5*/f32[5,12,12,1536]{3,2,1,0:T(8,128)}) fusion(f32[5,12,12]{2,1,0:T(8,128)S(1)} %get-tuple-element.741, f32[1536]{0:T(1024)S(1)} %get-tuple-element.303, f32[1536]{0:T(1024)S(1)} %get-tuple-element.304, ...), kind=kLoop, calls=%fused_computation.185 | loop fusion | flops 46442496 | bytes 17780352 | tf_op jit(solution)/shard_map/reduce_sum | solution.py:46
  244.9 5.9 reshape.1370
  250.8 41.1 %all-reduce.103 = (f32[1,1536]{1,0:T(1,128)S(1)}, f32[1,1536]{1,0:T(1,128)S(1)}, f32[1,1536]{1,0:T(1,128)S(1)}, f32[1,1536]{1,0:T(1,128)S(1)}) all-reduce(f32[1,1536]{1,0:T(1,128)S(1)} %stack.369, f32[1,1536]{1,0:T(1,128)S(1)} %stack.370, f32[1,1536]{1,0:T(1,128)S(1)} %stack.341, ...), channel_id=1, replica_groups=mesh['dp'=8,'shard'=4] {'dp','shard'}, use_global_device_ids=true, to_apply=%region_79.82 | all-reduce | flops 6144 | bytes 49152 | tf_op jit(solution)/shard_map/psum | solution.py:47
  293.5 7.8 multiply_reduce_fusion.51
  310.1 39.8 %all-reduce.102 = (f32[1,256]{1,0:T(1,128)S(1)}, f32[1,256]{1,0:T(1,128)S(1)}, f32[1,256]{1,0:T(1,128)S(1)}, f32[1,256]{1,0:T(1,128)S(1)}) all-reduce(f32[1,256]{1,0:T(1,128)S(1)} %bitcast.488, f32[1,256]{1,0:T(1,128)S(1)} %bitcast.487, f32[1,256]{1,0:T(1,128)S(1)} %bitcast.486, ...), channel_id=1, replica_groups=mesh['dp'=8,'shard'=4] {'dp','shard'}, use_global_device_ids=true, to_apply=%region_15.16 | all-reduce | flops 1024 | bytes 8192 | tf_op jit(solution)/shard_map/psum | solution.py:47
  360.0 41.5 %all-reduce.101 = (f32[1,1536]{1,0:T(1,128)S(1)}, f32[1,1536]{1,0:T(1,128)S(1)}, f32[1,1536]{1,0:T(1,128)S(1)}, f32[1,1536]{1,0:T(1,128)S(1)}, f32[1,1536]{1,0:T...) all-reduce(f32[1,1536]{1,0:T(1,128)S(1)} %stack.353, ...), channel_id=1, replica_groups=mesh['dp'=8,'shard'=4] {'dp','shard'}, use_global_device_ids=true, to_apply=%region_40.42 | all-reduce | flops 12288 | bytes 98304 | tf_op jit(solution)/shard_map/psum | solution.py:47
  404.5 15.3 divide_multiply_fusion.1
  442.4 41.8 %fusion.65 = (f32[1536]{0:T(1024)S(1)}, f32[1536]{0:T(1024)S(1)}, f32[1536]{0:T(1024)S(1)}, f32[1536]{0:T(1024)S(1)}, f32[5,12,12,1536]{3,2,1,0:T(8,128)}, /*index=5*/f32[5,12,12,1536]{3,2,1,0:T(8,128)}) fusion(f32[5,12,12]{2,1,0:T(8,128)S(1)} %get-tuple-element.742, f32[1536]{0:T(1024)S(1)} %copy-done.206, f32[1536]{0:T(1024)S(1)} %copy-done.207, ...), kind=kLoop, calls=%fused_computation.182 | loop fusion | flops 46442496 | bytes 17832768 | tf_op jit(solution)/shard_map/reduce_sum | solution.py:46
  496.0 42.0 %fusion.69 = (f32[1536]{0:T(1024)S(1)}, f32[1536]{0:T(1024)S(1)}, f32[1536]{0:T(1024)S(1)}, f32[1536]{0:T(1024)S(1)}, f32[5,12,12,1536]{3,2,1,0:T(8,128)}, /*index=5*/f32[5,12,12,1536]{3,2,1,0:T(8,128)}) fusion(f32[5,12,12]{2,1,0:T(8,128)S(1)} %get-tuple-element.741, f32[1536]{0:T(1024)S(1)} %copy-done.206, f32[1536]{0:T(1024)S(1)} %copy-done.207, ...), kind=kLoop, calls=%fused_computation.186 | loop fusion | flops 46442496 | bytes 17832768 | tf_op jit(solution)/shard_map/reduce_sum | solution.py:46
  538.0 5.9 reshape.1385
  549.8 40.8 %all-reduce.100 = (f32[1,1536]{1,0:T(1,128)S(1)}, f32[1,1536]{1,0:T(1,128)S(1)}, f32[1,1536]{1,0:T(1,128)S(1)}, f32[1,1536]{1,0:T(1,128)S(1)}, f32[1,1536]{1,0:T...) all-reduce(f32[1,1536]{1,0:T(1,128)S(1)} %stack.347, ...), channel_id=1, replica_groups=mesh['dp'=8,'shard'=4] {'dp','shard'}, use_global_device_ids=true, to_apply=%region_23.24 | all-reduce | flops 12288 | bytes 98304 | tf_op jit(solution)/shard_map/psum | solution.py:47
  593.7 14.1 multiply_reduce_fusion.54
  616.2 40.9 %all-reduce.99 = (f32[1,256]{1,0:T(1,128)S(1)}, f32[1,256]{1,0:T(1,128)S(1)}, f32[1,256]{1,0:T(1,128)}, f32[1,256]{1,0:T(1,128)}) all-reduce(f32[1,256]{1,0:T(1,128)S(1)} %bitcast.482, f32[1,256]{1,0:T(1,128)S(1)} %bitcast.481, f32[1,256]{1,0:T(1,128)S(1)} %bitcast.478, ...), channel_id=1, replica_groups=mesh['dp'=8,'shard'=4] {'dp','shard'}, use_global_device_ids=true, to_apply=%region_49.51 | all-reduce | flops 1024 | bytes 8192 | tf_op jit(solution)/shard_map/psum | solution.py:47
  663.7 8.7 fusion.110
  672.5 40.2 %all-reduce.98 = (f32[1,1536]{1,0:T(1,128)S(1)}, f32[1,1536]{1,0:T(1,128)S(1)}, f32[1,1536]{1,0:T(1,128)S(1)}, f32[1,1536]{1,0:T(1,128)S(1)}) all-reduce(f32[1,1536]{1,0:T(1,128)S(1)} %stack.359, f32[1,1536]{1,0:T(1,128)S(1)} %stack.360, f32[1,1536]{1,0:T(1,128)S(1)} %stack.387, ...), channel_id=1, replica_groups=mesh['dp'=8,'shard'=4] {'dp','shard'}, use_global_device_ids=true, to_apply=%region_53.55 | all-reduce | flops 6144 | bytes 49152 | tf_op jit(solution)/shard_map/psum | solution.py:47
  714.1 7.6 divide_multiply_fusion
  733.0 39.8 %fusion.71 = (f32[1536]{0:T(1024)S(1)}, f32[1536]{0:T(1024)S(1)}, f32[5,12,12,1536]{3,2,1,0:T(8,128)}, f32[1536]{0:T(1024)S(1)}, f32[1536]{0:T(1024)S(1)}, /*index=5*/f32[5,12,12,1536]{3,2,1,0:T(8,128)}) fusion(f32[5,12,12]{2,1,0:T(8,128)S(1)} %get-tuple-element.741, f32[1536]{0:T(1024)S(1)} %copy-done.231, f32[1536]{0:T(1024)S(1)} %copy-done.232, ...), kind=kLoop, calls=%fused_computation.188 | loop fusion | flops 46442496 | bytes 17780352 | tf_op jit(solution)/shard_map/reduce_sum | solution.py:46
  772.9 5.9 reshape.1377
  784.7 41.1 %all-reduce.97 = (f32[1,1536]{1,0:T(1,128)S(1)}, f32[1,1536]{1,0:T(1,128)S(1)}, f32[1,1536]{1,0:T(1,128)S(1)}, f32[1,1536]{1,0:T(1,128)S(1)}) all-reduce(f32[1,1536]{1,0:T(1,128)S(1)} %stack.389, f32[1,1536]{1,0:T(1,128)S(1)} %stack.390, f32[1,1536]{1,0:T(1,128)S(1)} %stack.361, ...), channel_id=1, replica_groups=mesh['dp'=8,'shard'=4] {'dp','shard'}, use_global_device_ids=true, to_apply=%region_124.127 | all-reduce | flops 6144 | bytes 49152 | tf_op jit(solution)/shard_map/psum | solution.py:47
  827.3 7.8 multiply_reduce_fusion.48
  846.9 39.5 %all-reduce.96 = (f32[1,256]{1,0:T(1,128)S(1)}, f32[1,256]{1,0:T(1,128)S(1)}, f32[1,256]{1,0:T(1,128)S(1)}, f32[1,256]{1,0:T(1,128)S(1)}, f32[1,256]{1,0:T(1,128...) all-reduce(f32[1,256]{1,0:T(1,128)S(1)} %bitcast.491, ...), channel_id=1, replica_groups=mesh['dp'=8,'shard'=4] {'dp','shard'}, use_global_device_ids=true, to_apply=%region_62.64 | all-reduce | flops 2048 | bytes 16384 | tf_op jit(solution)/shard_map/psum | solution.py:47
  901.4 41.9 %all-reduce.95 = (f32[2]{0:T(128)S(1)}, f32[1,1280]{1,0:T(1,128)S(1)}, f32[1,1280]{1,0:T(1,128)S(1)}, f32[1,1280]{1,0:T(1,128)S(1)}, f32[1,1280]{1,0:T(1,128)S(1...) all-reduce(f32[2]{0:T(128)S(1)} %copy-done.319, ...), channel_id=1, replica_groups=mesh['dp'=8,'shard'=4] {'dp','shard'}, use_global_device_ids=true, to_apply=%region_1.2 | all-reduce | flops 10242 | bytes 81936 | tf_op jit(solution)/shard_map/psum | solution.py:370
  944.1 5.9 reshape.1408
  969.7 8.5 divide_multiply_fusion.4
  999.8 6.9 multiply_reduce_fusion.93
  1017.1 39.9 %all-reduce.94 = (f32[1280]{0:T(1024)S(1)}, f32[1,1280]{1,0:T(1,128)S(1)}, f32[1280]{0:T(1024)S(1)}, f32[1,1280]{1,0:T(1,128)S(1)}) all-reduce(f32[1280]{0:T(1024)S(1)} %get-tuple-element.196, f32[1,1280]{1,0:T(1,128)S(1)} %stack.402, f32[1280]{0:T(1024)S(1)} %get-tuple-element.194, ...), channel_id=1, replica_groups=mesh['dp'=8,'shard'=4] {'dp','shard'}, use_global_device_ids=true, to_apply=%region_154.157 | all-reduce | flops 5120 | bytes 40960 | tf_op jit(solution)/shard_map/psum | solution.py:63
  1058.4 8.0 multiply_convert_fusion.5
  1072.0 40.6 %all-reduce.93 = (f32[256]{0:T(256)S(1)}, f32[1,256]{1,0:T(1,128)S(1)}, f32[256]{0:T(256)S(1)}, f32[1,256]{1,0:T(1,128)S(1)}) all-reduce(f32[256]{0:T(256)S(1)} %get-tuple-element.758, f32[1,256]{1,0:T(1,128)S(1)} %bitcast.484, f32[256]{0:T(256)S(1)} %get-tuple-element.258, ...), channel_id=1, replica_groups=mesh['dp'=8,'shard'=4] {'dp','shard'}, use_global_device_ids=true, to_apply=%region_158.161 | all-reduce | flops 1024 | bytes 8192 | tf_op jit(solution)/shard_map/psum | solution.py:63
  1138.4 9.7 multiply_reduce_fusion.60
  1148.1 40.3 %all-reduce.92 = (f32[1536]{0:T(1024)S(1)}, f32[1,1536]{1,0:T(1,128)S(1)}, f32[1536]{0:T(1024)S(1)}, f32[1,1536]{1,0:T(1,128)S(1)}) all-reduce(f32[1536]{0:T(1024)S(1)} %get-tuple-element.709, f32[1,1536]{1,0:T(1,128)S(1)} %stack.406, f32[1536]{0:T(1024)S(1)} %get-tuple-element.178, ...), channel_id=1, replica_groups=mesh['dp'=8,'shard'=4] {'dp','shard'}, use_global_device_ids=true, to_apply=%region_163.166 | all-reduce | flops 6144 | bytes 49152 | tf_op jit(solution)/shard_map/psum | solution.py:63
  1189.8 15.6 multiply_reduce_fusion.70
  1216.8 38.0 %multiply_reduce_fusion.23 = (f32[1536]{0:T(1024)S(1)}, f32[1536]{0:T(1024)S(1)}, f32[1536]{0:T(1024)S(1)}, f32[1536]{0:T(1024)S(1)}, f32[1536]{0:T(1024)S(1)}, ...) fusion(f32[5,12,12,1536]{3,2,1,0:T(8,128)} %reshape.1406, ...), kind=kLoop, calls=%fused_computation.220 | loop fusion | flops 27635712 | bytes 48764928 | tf_op jit(solution)/shard_map/transpose(jvp())/reduce_sum | solution.py:80
  1254.8 10.5 pad_add_fusion.1
  1265.3 17.3 pad_add_fusion.10
  1288.5 37.9 %multiply_reduce_fusion.39 = (f32[1536]{0:T(1024)S(1)}, f32[1536]{0:T(1024)S(1)}, f32[1536]{0:T(1024)S(1)}, f32[1536]{0:T(1024)S(1)}, f32[1536]{0:T(1024)S(1)}, ...) fusion(f32[5,12,12,1536]{3,2,1,0:T(8,128)} %reshape.1395, ...), kind=kLoop, calls=%fused_computation.236 | loop fusion | flops 27635712 | bytes 48764928 | tf_op jit(solution)/shard_map/transpose(jvp())/reduce_sum | solution.py:80
  1326.4 10.5 pad_add_fusion.3
  1336.9 17.5 pad_add_fusion.22
  1360.4 13.7 multiply_reduce_fusion.65
  1374.2 41.1 %all-reduce.91 = (f32[1536]{0:T(1024)S(1)}, f32[1,1536]{1,0:T(1,128)S(1)}, f32[1536]{0:T(1024)S(1)}, f32[1,1536]{1,0:T(1,128)S(1)}) all-reduce(f32[1536]{0:T(1024)S(1)} %get-tuple-element.188, f32[1,1536]{1,0:T(1,128)S(1)} %stack.408, f32[1536]{0:T(1024)S(1)} %get-tuple-element.704, ...), channel_id=1, replica_groups=mesh['dp'=8,'shard'=4] {'dp','shard'}, use_global_device_ids=true, to_apply=%region_167.170 | all-reduce | flops 6144 | bytes 49152 | tf_op jit(solution)/shard_map/psum | solution.py:63
  1416.8 9.2 multiply_convert_fusion.3
  1434.0 39.8 %all-reduce.90 = (f32[256]{0:T(256)S(1)}, f32[1,256]{1,0:T(1,128)S(1)}, f32[256]{0:T(256)S(1)}, f32[1,256]{1,0:T(1,128)S(1)}) all-reduce(f32[256]{0:T(256)S(1)} %get-tuple-element.752, f32[1,256]{1,0:T(1,128)S(1)} %bitcast.480, f32[256]{0:T(256)S(1)} %get-tuple-element.262, ...), channel_id=1, replica_groups=mesh['dp'=8,'shard'=4] {'dp','shard'}, use_global_device_ids=true, to_apply=%region_171.174 | all-reduce | flops 1024 | bytes 8192 | tf_op jit(solution)/shard_map/psum | solution.py:63
  1523.9 13.9 multiply_reduce_fusion.62
  1537.9 41.3 %all-reduce.89 = (f32[1536]{0:T(1024)S(1)}, f32[1,1536]{1,0:T(1,128)S(1)}, f32[1536]{0:T(1024)S(1)}, f32[1,1536]{1,0:T(1,128)S(1)}) all-reduce(f32[1536]{0:T(1024)S(1)} %get-tuple-element.699, f32[1,1536]{1,0:T(1,128)S(1)} %stack.412, f32[1536]{0:T(1024)S(1)} %get-tuple-element.182, ...), channel_id=1, replica_groups=mesh['dp'=8,'shard'=4] {'dp','shard'}, use_global_device_ids=true, to_apply=%region_176.179 | all-reduce | flops 6144 | bytes 49152 | tf_op jit(solution)/shard_map/psum | solution.py:63
  1580.6 15.7 multiply_reduce_fusion.69
  1607.7 37.8 %multiply_reduce_fusion.47 = (f32[1536]{0:T(1024)S(1)}, f32[1536]{0:T(1024)S(1)}, f32[1536]{0:T(1024)S(1)}, f32[1536]{0:T(1024)S(1)}, f32[1536]{0:T(1024)S(1)}, ...) fusion(f32[5,12,12,1536]{3,2,1,0:T(8,128)} %reshape.1400, ...), kind=kLoop, calls=%fused_computation.244 | loop fusion | flops 27635712 | bytes 48764928 | tf_op jit(solution)/shard_map/transpose(jvp())/reduce_sum | solution.py:80
  1645.6 10.6 pad_add_fusion.2
  1656.1 17.3 pad_add_fusion.16
  1679.4 37.8 %multiply_reduce_fusion.31 = (f32[1536]{0:T(1024)S(1)}, f32[1536]{0:T(1024)S(1)}, f32[1536]{0:T(1024)S(1)}, f32[1536]{0:T(1024)S(1)}, f32[1536]{0:T(1024)S(1)}, ...) fusion(f32[5,12,12,1536]{3,2,1,0:T(8,128)} %reshape.1411, ...), kind=kLoop, calls=%fused_computation.228 | loop fusion | flops 27635712 | bytes 48764928 | tf_op jit(solution)/shard_map/transpose(jvp())/reduce_sum | solution.py:80
  1717.3 10.5 pad_add_fusion
  1727.8 17.4 pad_add_fusion.4
  1751.3 13.8 multiply_reduce_fusion.63
  1767.2 40.8 %all-reduce.88 = (f32[4]{0:T(128)}, f32[1536]{0:T(1024)}, f32[1,1536]{1,0:T(1,128)S(1)}, f32[1536]{0:T(1024)}, f32[1,1536]{1,0:T(1,128)S(1)}) all-reduce(f32[4]{0:T(128)S(1)} %broadcast_in_dim.157, f32[1536]{0:T(1024)S(1)} %get-tuple-element.694, f32[1,1536]{1,0:T(1,128)S(1)} %stack.414, ...), channel_id=1, replica_groups=mesh['dp'=8,'shard'=4] {'dp','shard'}, use_global_device_ids=true, to_apply=%region_139.142 | all-reduce | flops 6148 | bytes 49184 | tf_op jit(solution)/shard_map/psum | solution.py:471
  1817.7 6.2 convolution_bitcast_fusion.1
  1824.6 6.3 convolution_bitcast_fusion
  1841.6 257.7 %all-reduce.109.cloned.1.call-done = (f32[2,256,3072]{2,1,0:T(8,128)}, f32[1280,1000]{1,0:T(8,128)}, f32[256,1280]{0,1:T(8,128)}, f32[2,137,1536]{2,1,0:T(8,128)}, f32[4,5018]{1,0:T(4,128)}) async-done(((f32[2,256,3072]{2,1,0:T(8,128)}, f32[1280,1000]{1,0:T(8,128)}, f32[256,1280]{0,1:T(8,128)}, f32[2,137,1536]{2,1,0:T(8,128)}, f32[4,5018]{1,0:T(4,128)}), (f32[2,256,3072]{2,1,0:T(8,128)}, ...) | async-done | bytes 14485936 | tf_op jit(solution)/shard_map/psum | solution.py:471
  2117.7 7.1 all-reduce.106
  (1204 shorter events, 460.2 us)
Async XLA Ops:
  7.2 109.7 %all-gather.11.cloned.1.call-start = ((), (), s32[]{:S(2)}) async-start(), calls=%async_computation.2 | async-start | bytes 3932160 | tf_op jit(solution)/shard_map/all_gather | solution.py:352
  9.8 116.2 %all-gather.7.cloned.1.call-start = ((), (), s32[]{:S(2)}) async-start(), calls=%async_computation | async-start | bytes 3932160 | tf_op jit(solution)/shard_map/all_gather | solution.py:347
  13.5 969.2 %all-gather.13.cloned.1.call-start = ((), (), s32[]{:S(2)}) async-start(), calls=%async_computation.3 | async-start | bytes 3276800 | tf_op jit(solution)/shard_map/all_gather | solution.py:355
  14.6 975.5 %all-gather.9.cloned.1.call-start = ((), (), s32[]{:S(2)}) async-start(), calls=%async_computation.1 | async-start | bytes 3276800 | tf_op jit(solution)/shard_map/all_gather | solution.py:350
  16.4 2082.9 %all-reduce.109.cloned.1.call-start = ((), (), s32[]{:S(2)}) async-start(), calls=%async_computation.4 | async-start | bytes 29392896 | tf_op jit(solution)/shard_map/psum | solution.py:471
  57.5 56.1 %copy-start.62 = (bf16[2,5,12,12,256]{4,0,3,2,1:T(2,128)(2,1)S(1)}, bf16[2,5,12,12,256]{4,0,3,2,1:T(2,128)(2,1)}, u32[]{:S(2)}) copy-start(bf16[2,5,12,12,256]{4,0,3,2,1:T(2,128)(2,1)} %param.28) | copy-start | bytes 2211844
  60.6 56.2 %copy-start.172 = (f32[5,144]{1,0:T(8,128)}, f32[5,144]{1,0:T(8,128)S(1)}, u32[]{:S(2)}) copy-start(f32[5,144]{1,0:T(8,128)S(1)} %get-tuple-element.764) | copy-start | bytes 8644
  60.6 56.2 %copy-start.174 = (f32[5,144]{1,0:T(8,128)}, f32[5,144]{1,0:T(8,128)S(1)}, u32[]{:S(2)}) copy-start(f32[5,144]{1,0:T(8,128)S(1)} %get-tuple-element.765) | copy-start | bytes 8644
  77.8 224.8 %copy-start.108 = (f32[1536]{0:T(1024)}, f32[1536]{0:T(1024)S(1)}, u32[]{:S(2)}) copy-start(f32[1536]{0:T(1024)S(1)} %mul.3962) | copy-start | bytes 18436
  108.5 387.4 %copy-start.119 = (f32[1536]{0:T(1024)}, f32[1536]{0:T(1024)S(1)}, u32[]{:S(2)}) copy-start(f32[1536]{0:T(1024)S(1)} %get-tuple-element.293) | copy-start | bytes 18436
  108.5 387.4 %copy-start.121 = (f32[1536]{0:T(1024)}, f32[1536]{0:T(1024)S(1)}, u32[]{:S(2)}) copy-start(f32[1536]{0:T(1024)S(1)} %get-tuple-element.294) | copy-start | bytes 18436
  108.5 387.4 %copy-start.123 = (f32[1536]{0:T(1024)}, f32[1536]{0:T(1024)S(1)}, u32[]{:S(2)}) copy-start(f32[1536]{0:T(1024)S(1)} %get-tuple-element.295) | copy-start | bytes 18436
  108.5 387.4 %copy-start.125 = (f32[1536]{0:T(1024)}, f32[1536]{0:T(1024)S(1)}, u32[]{:S(2)}) copy-start(f32[1536]{0:T(1024)S(1)} %get-tuple-element.296) | copy-start | bytes 18436
  108.5 387.5 %copy-start.127 = (f32[1536]{0:T(1024)}, f32[1536]{0:T(1024)S(1)}, u32[]{:S(2)}) copy-start(f32[1536]{0:T(1024)S(1)} %get-tuple-element.297) | copy-start | bytes 18436
  108.5 387.5 %copy-start.129 = (f32[1536]{0:T(1024)}, f32[1536]{0:T(1024)S(1)}, u32[]{:S(2)}) copy-start(f32[1536]{0:T(1024)S(1)} %get-tuple-element.298) | copy-start | bytes 18436
  109.3 88.3 %copy-start.154 = (f32[1536]{0:T(1024)}, f32[1536]{0:T(1024)S(1)}, u32[]{:S(2)}) copy-start(f32[1536]{0:T(1024)S(1)} %get-tuple-element.302) | copy-start | bytes 18436
  109.3 88.3 %copy-start.156 = (f32[1536]{0:T(1024)}, f32[1536]{0:T(1024)S(1)}, u32[]{:S(2)}) copy-start(f32[1536]{0:T(1024)S(1)} %get-tuple-element.303) | copy-start | bytes 18436
  109.3 88.3 %copy-start.158 = (f32[1536]{0:T(1024)}, f32[1536]{0:T(1024)S(1)}, u32[]{:S(2)}) copy-start(f32[1536]{0:T(1024)S(1)} %get-tuple-element.304) | copy-start | bytes 18436
  109.3 88.3 %copy-start.160 = (f32[1536]{0:T(1024)}, f32[1536]{0:T(1024)S(1)}, u32[]{:S(2)}) copy-start(f32[1536]{0:T(1024)S(1)} %get-tuple-element.305) | copy-start | bytes 18436
  109.3 88.3 %copy-start.162 = (f32[1536]{0:T(1024)}, f32[1536]{0:T(1024)S(1)}, u32[]{:S(2)}) copy-start(f32[1536]{0:T(1024)S(1)} %get-tuple-element.306) | copy-start | bytes 18436
  109.3 88.3 %copy-start.164 = (f32[1536]{0:T(1024)}, f32[1536]{0:T(1024)S(1)}, u32[]{:S(2)}) copy-start(f32[1536]{0:T(1024)S(1)} %get-tuple-element.307) | copy-start | bytes 18436
  109.3 88.3 %copy-start.166 = (f32[1536]{0:T(1024)}, f32[1536]{0:T(1024)S(1)}, u32[]{:S(2)}) copy-start(f32[1536]{0:T(1024)S(1)} %get-tuple-element.308) | copy-start | bytes 18436
  116.8 781.1 %copy-start.8 = (bf16[720,256]{1,0:T(8,128)(2,1)}, bf16[720,256]{1,0:T(8,128)(2,1)S(1)}, u32[]{:S(2)}) copy-start(bf16[720,256]{1,0:T(8,128)(2,1)S(1)} %squeeze.24) | copy-start | bytes 1105924
  116.9 772.7 %copy-start.10 = (bf16[720,256]{1,0:T(8,128)(2,1)}, bf16[720,256]{1,0:T(8,128)(2,1)S(1)}, u32[]{:S(2)}) copy-start(bf16[720,256]{1,0:T(8,128)(2,1)S(1)} %squeeze.18) | copy-start | bytes 1105924
  129.3 177.2 %copy-start.35 = (bf16[256,3072]{1,0:T(8,128)(2,1)}, bf16[256,3072]{1,0:T(8,128)(2,1)S(1)}, u32[]{:S(2)}) copy-start(bf16[256,3072]{1,0:T(8,128)(2,1)S(1)} %get-tuple-element.628) | copy-start | bytes 4718596
  132.3 46.4 %copy-start.193 = (f32[1536]{0:T(1024)S(1)}, f32[1536]{0:T(1024)}, u32[]{:S(2)}) copy-start(f32[1536]{0:T(1024)} %mul.3964) | copy-start | bytes 18436
  132.3 46.4 %copy-start.199 = (f32[1536]{0:T(1024)S(1)}, f32[1536]{0:T(1024)}, u32[]{:S(2)}) copy-start(f32[1536]{0:T(1024)} %add.1547) | copy-start | bytes 18436
  244.9 48.5 %copy-start.137 = (f32[1536]{0:T(1024)S(1)}, f32[1536]{0:T(1024)}, u32[]{:S(2)}) copy-start(f32[1536]{0:T(1024)} %add.1561) | copy-start | bytes 18436
  244.9 57.8 %slice-start.6 = ((s8[4423680]{0:T(1024)(128)(4,1)}), s8[229376]{0:T(1024)(128)(4,1)S(1)}, s32[]{:S(2)}) async-start(s8[4423680]{0:T(1024)(128)(4,1)} %bitcast.381), calls=%async_computation.11 | async-start | bytes 458752
  307.4 48.4 %copy-start.27 = (f32[720,256]{1,0:T(8,128)}, f32[720,256]{1,0:T(8,128)S(1)}, u32[]{:S(2)}) copy-start(f32[720,256]{1,0:T(8,128)S(1)} %get-tuple-element.779) | copy-start | bytes 2211844
  307.4 49.2 %slice-start.8 = ((s8[4423680]{0:T(1024)(128)(4,1)}), s8[229376]{0:T(1024)(128)(4,1)S(1)}, s32[]{:S(2)}) async-start(s8[4423680]{0:T(1024)(128)(4,1)} %bitcast.387), calls=%async_computation.13 | async-start | bytes 458752
  310.1 46.5 %copy-start.30 = (f32[720,256]{1,0:T(8,128)}, f32[720,256]{1,0:T(8,128)S(1)}, u32[]{:S(2)}) copy-start(f32[720,256]{1,0:T(8,128)S(1)} %get-tuple-element.778) | copy-start | bytes 2211844
  356.6 47.8 %copy-start.176 = (f32[1536]{0:T(1024)S(1)}, f32[1536]{0:T(1024)}, u32[]{:S(2)}) copy-start(f32[1536]{0:T(1024)} %mul.4040) | copy-start | bytes 18436
  356.6 47.8 %copy-start.216 = (f32[1536]{0:T(1024)S(1)}, f32[1536]{0:T(1024)}, u32[]{:S(2)}) copy-start(f32[1536]{0:T(1024)} %add.1582) | copy-start | bytes 18436
  356.6 47.8 %copy-start.245 = (f32[1536]{0:T(1024)S(1)}, f32[1536]{0:T(1024)}, u32[]{:S(2)}) copy-start(f32[1536]{0:T(1024)} %add.1624) | copy-start | bytes 18436
  356.7 47.8 %copy-start.246 = (f32[1536]{0:T(1024)S(1)}, f32[1536]{0:T(1024)}, u32[]{:S(2)}) copy-start(f32[1536]{0:T(1024)} %mul.4121) | copy-start | bytes 18436
  544.0 49.6 %copy-start.191 = (f32[1536]{0:T(1024)S(1)}, f32[1536]{0:T(1024)}, u32[]{:S(2)}) copy-start(f32[1536]{0:T(1024)} %add.1637) | copy-start | bytes 18436
  544.0 49.6 %copy-start.192 = (f32[1536]{0:T(1024)S(1)}, f32[1536]{0:T(1024)}, u32[]{:S(2)}) copy-start(f32[1536]{0:T(1024)} %mul.4119) | copy-start | bytes 18436
  608.6 522.0 %copy-start.274 = (f32[5,64]{1,0:T(8,128)}, f32[5,64]{1,0:T(8,128)S(1)}, u32[]{:S(2)}) copy-start(f32[5,64]{1,0:T(8,128)S(1)} %convolution_add_fusion.22) | copy-start | bytes 3844
  608.9 520.8 %copy-start.273 = (f32[5,64]{1,0:T(8,128)}, f32[5,64]{1,0:T(8,128)S(1)}, u32[]{:S(2)}) copy-start(f32[5,64]{1,0:T(8,128)S(1)} %convolution_add_fusion.18) | copy-start | bytes 3844
  614.1 45.2 %copy-start.52 = (f32[720,256]{1,0:T(8,128)}, f32[720,256]{1,0:T(8,128)S(1)}, u32[]{:S(2)}) copy-start(f32[720,256]{1,0:T(8,128)S(1)} %get-tuple-element.783) | copy-start | bytes 2211844
  614.1 45.2 %copy-start.32 = (bf16[256,3072]{1,0:T(8,128)(2,1)S(1)}, bf16[256,3072]{1,0:T(8,128)(2,1)}, u32[]{:S(2)}) copy-start(bf16[256,3072]{1,0:T(8,128)(2,1)} %get-tuple-element.626) | copy-start | bytes 4718596
  614.1 45.2 %copy-start.226 = (f32[256]{0:T(256)S(1)}, f32[256]{0:T(256)}, u32[]{:S(2)}) copy-start(f32[256]{0:T(256)} %add.1653) | copy-start | bytes 3076
  614.1 45.2 %copy-start.227 = (f32[256]{0:T(256)S(1)}, f32[256]{0:T(256)}, u32[]{:S(2)}) copy-start(f32[256]{0:T(256)} %mul.4117) | copy-start | bytes 3076
  614.1 46.0 %slice-start = ((s8[4423680]{0:T(1024)(128)(4,1)}), s8[229376]{0:T(1024)(128)(4,1)S(1)}, s32[]{:S(2)}) async-start(s8[4423680]{0:T(1024)(128)(4,1)} %bitcast.375), calls=%async_computation.5 | async-start | bytes 458752
  663.7 50.3 %copy-start.241 = (f32[1536]{0:T(1024)S(1)}, f32[1536]{0:T(1024)}, u32[]{:S(2)}) copy-start(f32[1536]{0:T(1024)} %add.1658) | copy-start | bytes 18436
  663.7 50.4 %copy-start.242 = (f32[1536]{0:T(1024)S(1)}, f32[1536]{0:T(1024)}, u32[]{:S(2)}) copy-start(f32[1536]{0:T(1024)} %mul.4190) | copy-start | bytes 18436
  672.4 172.7 %copy-start.21 = (bf16[720,1536]{1,0:T(8,128)(2,1)}, bf16[720,1536]{1,0:T(8,128)(2,1)S(1)}, u32[]{:S(2)}) copy-start(bf16[720,1536]{1,0:T(8,128)(2,1)S(1)} %get-tuple-element.717) | copy-start | bytes 6635524
  778.8 48.5 %copy-start.214 = (f32[1536]{0:T(1024)S(1)}, f32[1536]{0:T(1024)}, u32[]{:S(2)}) copy-start(f32[1536]{0:T(1024)} %mul.4188) | copy-start | bytes 18436
  778.8 48.5 %copy-start.215 = (f32[1536]{0:T(1024)S(1)}, f32[1536]{0:T(1024)}, u32[]{:S(2)}) copy-start(f32[1536]{0:T(1024)} %add.1671) | copy-start | bytes 18436
  845.2 44.4 %copy-start.285 = (f32[1,256]{1,0:T(1,128)S(1)}, f32[1,256]{1,0:T(1,128)}, u32[]{:S(2)}) copy-start(f32[1,256]{1,0:T(1,128)} %copy-done.284) | copy-start | bytes 3076
  845.2 44.4 %copy-start.287 = (f32[1,256]{1,0:T(1,128)S(1)}, f32[1,256]{1,0:T(1,128)}, u32[]{:S(2)}) copy-start(f32[1,256]{1,0:T(1,128)} %copy-done.286) | copy-start | bytes 3076
  846.9 45.3 %copy-start.95 = (bf16[256,1280]{0,1:T(8,128)(2,1)S(1)}, bf16[256,1280]{0,1:T(8,128)(2,1)}, u32[]{:S(2)}) copy-start(bf16[256,1280]{0,1:T(8,128)(2,1)} %all_gather.33) | copy-start | bytes 1966084
  898.3 51.7 %copy-start.80 = (bf16[720,256]{1,0:T(8,128)(2,1)}, bf16[720,256]{1,0:T(8,128)(2,1)S(1)}, u32[]{:S(2)}) copy-start(bf16[720,256]{1,0:T(8,128)(2,1)S(1)} %add_convert_fusion.1) | copy-start | bytes 1105924
  1069.6 48.0 %copy-start.24 = (bf16[720,1536]{1,0:T(8,128)(2,1)S(1)}, bf16[720,1536]{1,0:T(8,128)(2,1)}, u32[]{:S(2)}) copy-start(bf16[720,1536]{1,0:T(8,128)(2,1)} %get-tuple-element.718) | copy-start | bytes 6635524
  1431.4 47.7 %copy-start.20 = (bf16[720,1536]{1,0:T(8,128)(2,1)S(1)}, bf16[720,1536]{1,0:T(8,128)(2,1)}, u32[]{:S(2)}) copy-start(bf16[720,1536]{1,0:T(8,128)(2,1)} %copy-done.19) | copy-start | bytes 6635524
  1751.3 59.3 %copy-start.74 = (f32[64,1536]{1,0:T(8,128)S(1)}, f32[64,1536]{1,0:T(8,128)}, u32[]{:S(2)}) copy-start(f32[64,1536]{1,0:T(8,128)} %fusion.358) | copy-start | bytes 1179652
  1751.3 59.3 %copy-start.76 = (f32[64,1536]{1,0:T(8,128)S(1)}, f32[64,1536]{1,0:T(8,128)}, u32[]{:S(2)}) copy-start(f32[64,1536]{1,0:T(8,128)} %fusion.294) | copy-start | bytes 1179652
  1751.3 60.2 %copy-start.75 = (f32[64,1536]{1,0:T(8,128)S(1)}, f32[64,1536]{1,0:T(8,128)}, u32[]{:S(2)}) copy-start(f32[64,1536]{1,0:T(8,128)} %fusion.364) | copy-start | bytes 1179652
  1751.3 60.2 %copy-start.77 = (f32[64,1536]{1,0:T(8,128)S(1)}, f32[64,1536]{1,0:T(8,128)}, u32[]{:S(2)}) copy-start(f32[64,1536]{1,0:T(8,128)} %fusion.296) | copy-start | bytes 1179652
  1838.8 260.5 %copy-start.58 = (f32[2,137,384]{2,0,1:T(2,128)S(1)}, f32[2,137,384]{2,0,1:T(2,128)}, u32[]{:S(2)}) copy-start(f32[2,137,384]{2,0,1:T(2,128)} %param.38) | copy-start | bytes 1262596
  1838.8 260.5 %copy-start.97 = (f32[2,137,384]{2,0,1:T(2,128)S(1)}, f32[2,137,384]{2,0,1:T(2,128)}, u32[]{:S(2)}) copy-start(f32[2,137,384]{2,0,1:T(2,128)} %param.40) | copy-start | bytes 1262596
  1838.8 260.5 %copy-start.98 = (f32[2,137,384]{2,0,1:T(2,128)S(1)}, f32[2,137,384]{2,0,1:T(2,128)}, u32[]{:S(2)}) copy-start(f32[2,137,384]{2,0,1:T(2,128)} %param.39) | copy-start | bytes 1262596
  1838.8 263.2 %copy-start.14 = (f32[2,64,3072]{2,1,0:T(8,128)S(1)}, f32[2,64,3072]{2,1,0:T(8,128)}, u32[]{:S(2)}) copy-start(f32[2,64,3072]{2,1,0:T(8,128)} %param.34) | copy-start | bytes 4718596
  (304 other events, 2524.9 us)
Sparse Core Ops, SparseCore 0:
  10.2 36.1 all-gather.10
  48.5 28.7 all-gather.6
  78.9 30.9 all-gather.12
  111.3 26.6 all-gather.8
  1838.9 260.2 all-reduce.108
where the time goes:
time: 2160 us; the launch traced here: 2150 us
  blocking collectives  759 us (35%)
  other arithmetic  735 us (34%)
  waiting for transfers between devices  258 us (12%)
  local copies, waits for them, and re-layouts  247 us (11%)
  matrix products  125 us (6%)
  between operations  24.5 us (1%)
    psum x9, blocking collectives, norm_stats(): sums = lax.psum((sums_first, sums_second), ('dp', 'shard'))  366 us
    psum x1, waiting for transfers between devices, per_device(): lax.psum((loss_spread, grad_mats, grad_chan, grad_head, grad_class, grad_...  258 us
    psum x6, blocking collectives, norm_back(): sums = lax.psum((sums_first, sums_second), ('dp', 'shard'))  243 us
    reduce_sum x6, other arithmetic, spread(): padded[:, offset // 3:offset // 3 + S, offset % 3:offset % 3 + S, :]  183 us
    reduce_sum x4, other arithmetic, norm_stats(): sums_second = jnp.stack([jnp.sum(masks[0] * values[0] * values[0], 0)])  165 us
    add_any x8, other arithmetic, spread(): padded[:, offset // 3:offset // 3 + S, offset % 3:offset % 3 + S, :]  112 us
    reshape x16, local copies, waits for them, and re-layouts, spread(): return total.reshape(first.shape)  93.1 us
    reshape x12, local copies, waits for them, and re-layouts, spread(): image = jax.nn.silu(first).reshape(-1, S, S, first.shape[-1])  68.3 us
  transfers between devices with their start and end apart: 5, of which 1 were waited for; matrix products, arithmetic and copies ran while one was open for 23% of the time, Pallas kernels for 0%

commit v1 on v0

--- a/solution.py
+++ b/solution.py
@@ -1,6 +1,10 @@
+import functools
+
 import jax
 import jax.numpy as jnp
 from jax import lax
+from jax.experimental import pallas as pl
+from jax.experimental.pallas import tpu as pltpu
 from jax.sharding import PartitionSpec as P
 
 C = 256
@@ -266,6 +270,438 @@
     head_tail = [backs[k][1], backs[k][2], partial_heads[k][1]]
     result = [(grad_hidden, grad_head, partial_heads[k][0], head_tail)]
     return result
+
+
+IMGS = 5
+ROWS = S * S
+BATCHES = 2
+HALF = IMGS * ROWS
+FULL = BATCHES * HALF
+SLOTS = BATCHES * IMGS
+LANES = 128
+EC = E // LANES
+HC = HEAD // LANES
+GAP = 16
+TILE = 48
+OFFSETS = [S * (a - 1) + (c - 1) for a in range(3) for c in range(3)]
+MESH = pl.DeviceIdType.MESH
+F32 = jnp.float32
+BF16 = jnp.bfloat16
+
+
+class Sum:
+    def __init__(self, near, far, total, sems, sizes, rows):
+        self.near, self.far, self.total = near, far, total
+        self.sems = sems
+        self.n_dp, self.n_sh = sizes
+        self.rows = rows
+
+    def copy_near(self, step, slot, target):
+        d = lax.axis_index("dp")
+        return pltpu.make_async_remote_copy(
+            self.near.at[slot], self.near.at[slot],
+            self.sems[0].at[step], self.sems[1].at[slot],
+            device_id=(d, target), device_id_type=MESH)
+
+    def copy_far(self, step, slot, target):
+        s = lax.axis_index("shard")
+        return pltpu.make_async_remote_copy(
+            self.far.at[slot], self.far.at[slot],
+            self.sems[2].at[step], self.sems[3].at[slot],
+            device_id=(target, s), device_id_type=MESH)
+
+    def start(self, stage):
+        s = lax.axis_index("shard")
+        self.near[s] = stage[0 : self.rows]
+        for j in range(1, self.n_sh):
+            self.copy_near(j, s, lax.rem(s + j, self.n_sh)).start()
+
+    def middle(self):
+        s, d = lax.axis_index("shard"), lax.axis_index("dp")
+        for j in range(1, self.n_sh):
+            self.copy_near(j, lax.rem(s + j, self.n_sh), s).wait_recv()
+        for j in range(1, self.n_sh):
+            self.copy_near(j, s, s).wait_send()
+        part = self.near[0]
+        for j in range(1, self.n_sh):
+            part = part + self.near[j]
+        self.far[d] = part
+
+        def send(j, carry):
+            self.copy_far(j, d, lax.rem(d + j, self.n_dp)).start()
+            return carry
+
+        lax.fori_loop(1, self.n_dp, send, 0)
+
+    def finish(self):
+        d = lax.axis_index("dp")
+
+        def arrive(j, carry):
+            self.copy_far(j, lax.rem(d + j, self.n_dp), d).wait_recv()
+            self.copy_far(j, d, d).wait_send()
+            return carry
+
+        lax.fori_loop(1, self.n_dp, arrive, 0)
+        part = self.far[0]
+        for j in range(1, self.n_dp):
+            part = part + self.far[j]
+        self.total[0 : self.rows] = part
+
+
+def sum_scratch(sizes, rows):
+    n_dp, n_sh = sizes
+    return [
+        pltpu.VMEM((n_sh, rows, LANES), F32),
+        pltpu.VMEM((n_dp, rows, LANES), F32),
+        pltpu.SemaphoreType.DMA((n_sh,)),
+        pltpu.SemaphoreType.DMA((n_sh,)),
+        pltpu.SemaphoreType.DMA((n_dp,)),
+        pltpu.SemaphoreType.DMA((n_dp,)),
+    ]
+
+
+def greet(sizes):
+    n_dp, n_sh = sizes
+    d, s = lax.axis_index("dp"), lax.axis_index("shard")
+    gate = pltpu.get_barrier_semaphore()
+    for j in range(1, n_sh):
+        pl.semaphore_signal(gate, inc=1, device_id=(d, lax.rem(s + j, n_sh)), device_id_type=MESH)
+
+    def signal(j, carry):
+        pl.semaphore_signal(gate, inc=1, device_id=(lax.rem(d + j, n_dp), s), device_id_type=MESH)
+        return carry
+
+    lax.fori_loop(1, n_dp, signal, 0)
+    pl.semaphore_wait(gate, n_sh + n_dp - 2)
+
+
+def repeat(count, body, hook=None):
+    def step(i, carry):
+        if hook is not None:
+
+            @pl.when(i == hook[0])
+            def _():
+                hook[1]()
+
+        body(i)
+        return carry
+
+    lax.fori_loop(0, count, step, 0)
+
+
+def lanes(c, width=LANES):
+    return pl.ds(pl.multiple_of(c * width, width), width)
+
+
+def coefs(total, row, count, gain, shift):
+    mean = total[pl.ds(row, 1), :] / count
+    square = total[pl.ds(row + 1, 1), :] / count
+    scale = gain * lax.rsqrt(square - mean * mean + EPS_NORM)
+    return scale, shift - mean * scale
+
+
+def act_half(half):
+    return half + half * jnp.tanh(half)
+
+
+def forward_kernel(sizes, *refs):
+    (images, mask, edge_l, edge_r, area, firstrow, wexp, headt, taps, squeeze, excite, gain_e, gain_c, gain_h, gain_s,
+     pre_s, mixed_s, feat_s, out_s, low_s, pool_s, unit_s, gate_s, tot_e, tot_c, tot_h, pooled_h,
+     pre, hid, out_t, low_t, scaled, pads, stages, totals, cnt, pool_t, gate_t) = refs[:38]
+    rest = list(refs[38:])
+    save_sems = rest.pop(0)
+    sums = []
+    for m in range(2):
+        group = []
+        for rows in (56, 48, 8, 40):
+            near, far = rest[0], rest[1]
+            group.append((near, far, rest[2:6], rows))
+            rest = rest[6:]
+        sums.append(group)
+
+    greet(sizes)
+
+    def low(m, layer):
+        return low_s.at[layer] if m == 0 else low_t
+
+    def out(m, layer):
+        return out_s.at[layer] if m == 0 else out_t
+
+    def total_ref(m, kind, layer):
+        if m == 0:
+            return (tot_e.at[layer, 0], tot_e.at[layer, 1], tot_c.at[layer], tot_h)[kind]
+        return totals.at[kind]
+
+    def summer(m, kind, layer):
+        near, far, sems, rows = sums[m][kind]
+        if kind == 0 and layer == 1:
+            pass
+        return Sum(near, far, total_ref(m, kind, layer), sems, sizes, rows)
+
+    def save(src, dst, index):
+        return pltpu.make_async_copy(src, dst, save_sems.at[index])
+
+    for slot in range(SLOTS):
+        pads[slot, 0:GAP, :] = jnp.zeros((GAP, LANES), F32)
+        pads[slot, GAP + ROWS : 2 * GAP + ROWS, :] = jnp.zeros((GAP, LANES), F32)
+
+    def load_rows(i):
+        rows = pl.ds(pl.multiple_of(i * ROWS, ROWS), ROWS)
+        for half in range(2):
+            cols = slice(half * LANES, half * LANES + LANES)
+            value = images[rows, cols].astype(F32) * mask[rows, :]
+            hid[0, rows, cols] = value
+            hid[1, rows, cols] = value
+            low_s[0, rows, cols] = value.astype(BF16)
+            low_t[rows, cols] = value.astype(BF16)
+
+    repeat(SLOTS, load_rows)
+
+    def update(m, layer):
+        tot = total_ref(m, 2, layer)
+        for half in range(2):
+            cols = slice(half * LANES, half * LANES + LANES)
+            for b in range(BATCHES):
+                scale, shift = coefs(tot, 4 * half + 2 * b, cnt[b : b + 1, :], gain_c[m, layer, 0:1, cols], gain_c[m, layer, 1:2, cols])
+
+                def one(i):
+                    rows = pl.ds(pl.multiple_of(b * HALF + i * ROWS, ROWS), ROWS)
+                    value = hid[m, rows, cols] + mask[rows, :] * (out(m, layer)[rows, cols] * scale + shift)
+                    hid[m, rows, cols] = value
+                    low(m, layer + 1)[rows, cols] = value.astype(BF16)
+
+                repeat(IMGS, one)
+
+    def put_sums(stage, chunk, b, value):
+        stage[pl.ds(4 * chunk + 2 * b, 1), :] = jnp.sum(value, 0, keepdims=True)
+        stage[pl.ds(4 * chunk + 2 * b + 1, 1), :] = jnp.sum(value * value, 0, keepdims=True)
+
+    def expand(m, layer, hook=None):
+        stage = stages.at[m]
+
+        def body(c):
+            weight = wexp[m, layer, :, lanes(c, 256)]
+            for b in range(BATCHES):
+                value = jnp.dot(low(m, layer)[b * HALF : (b + 1) * HALF, :], weight, preferred_element_type=F32)
+                for half in range(2):
+                    piece = value[:, half * LANES : (half + 1) * LANES]
+                    pre[m, 2 * c + half, b * HALF : (b + 1) * HALF, :] = piece
+                    put_sums(stage, 2 * c + half, b, piece)
+            if m == 0:
+                for half in range(2):
+                    save(pre.at[0, 2 * c + half], pre_s.at[layer, 2 * c + half], 2 * c + half).start()
+
+        repeat(E // 256, body, hook)
+
+    def depthwise(m, layer, hook=None):
+        stage = stages.at[m]
+        tot = total_ref(m, 0, layer)
+
+        def body(c):
+            if m == 0:
+                save(pre.at[0, c], pre_s.at[layer, c], c).wait()
+            tap = [taps[m, layer, k : k + 1, lanes(c)] for k in range(9)]
+            for b in range(BATCHES):
+                scale, shift = coefs(tot, 4 * c + 2 * b, cnt[b : b + 1, :], gain_e[m, layer, 0:1, lanes(c)], gain_e[m, layer, 1:2, lanes(c)])
+                scale, shift = 0.5 * scale, 0.5 * shift
+                for i in range(IMGS):
+                    slot = b * IMGS + i
+                    rows = slice(slot * ROWS, (slot + 1) * ROWS)
+                    half = mask[rows, :] * (pre[m, c, rows, :] * scale + shift)
+                    pads[slot, GAP : GAP + ROWS, :] = act_half(half)
+                first = jnp.zeros((8, LANES), F32)
+                second = jnp.zeros((8, LANES), F32)
+                for i in range(IMGS):
+                    slot = b * IMGS + i
+                    for t in range(ROWS // TILE):
+                        start = GAP + t * TILE
+                        near = [pads[slot, start + o : start + o + TILE, :] for o in OFFSETS]
+                        left = near[0] * tap[0] + near[3] * tap[3] + near[6] * tap[6]
+                        mid = near[1] * tap[1] + near[4] * tap[4] + near[7] * tap[7]
+                        right = near[2] * tap[2] + near[5] * tap[5] + near[8] * tap[8]
+                        rows = slice(slot * ROWS + t * TILE, slot * ROWS + (t + 1) * TILE)
+                        value = mask[rows, :] * (mid + edge_l[0:TILE, :] * left + edge_r[0:TILE, :] * right)
+                        pre[m, c, rows, :] = value
+                        first = first + jnp.sum(value.reshape(TILE // 8, 8, LANES), 0)
+                        second = second + jnp.sum((value * value).reshape(TILE // 8, 8, LANES), 0)
+                stage[pl.ds(4 * c + 2 * b, 1), :] = jnp.sum(first, 0, keepdims=True)
+                stage[pl.ds(4 * c + 2 * b + 1, 1), :] = jnp.sum(second, 0, keepdims=True)
+            if m == 0:
+                save(pre.at[0, c], mixed_s.at[layer, c], c).start()
+
+        repeat(EC, body, hook)
+
+    def pooling(m, layer, hook=None):
+        tot = total_ref(m, 1, layer)
+        pool = pool_s.at[layer] if m == 0 else pool_t
+
+        def body(c):
+            if m == 0:
+                save(pre.at[0, c], mixed_s.at[layer, c], c).wait()
+            for b in range(BATCHES):
+                scale, shift = coefs(tot, 4 * c + 2 * b, cnt[b : b + 1, :], gain_e[m, layer, 2:3, lanes(c)], gain_e[m, layer, 3:4, lanes(c)])
+                scale, shift = 0.5 * scale, 0.5 * shift
+                for i in range(IMGS):
+                    slot = b * IMGS + i
+                    rows = slice(slot * ROWS, (slot + 1) * ROWS)
+                    value = act_half(mask[rows, :] * (pre[m, c, rows, :] * scale + shift))
+                    pre[m, c, rows, :] = value
+                    pool[slot : slot + 1, lanes(c)] = jnp.sum(value, 0, keepdims=True) / area[0:1, :]
+
+        repeat(EC, body, hook)
+
+    def project(m, layer):
+        pool = pool_s.at[layer] if m == 0 else pool_t
+        gate = gate_s.at[layer] if m == 0 else gate_t
+        units = matmul_bt(pool[...], squeeze[m, layer]) + gain_s[m, layer]
+        if m == 0:
+            unit_s[layer] = units
+        gate[...] = jax.nn.sigmoid(matmul(jax.nn.silu(units), excite[m, layer]) + gain_e[m, layer, 4:5, :])
+
+        def body(c):
+            for i in range(SLOTS):
+                rows = slice(i * ROWS, (i + 1) * ROWS)
+                scaled[rows, lanes(c)] = (pre[m, c, rows, :] * gate[i : i + 1, lanes(c)]).astype(BF16)
+
+        repeat(EC, body)
+        stage = stages.at[m]
+        for b in range(BATCHES):
+            rows = slice(b * HALF, (b + 1) * HALF)
+            value = contract(scaled[rows, :], wexp[m, layer, :, E : 2 * E], 1, 1)
+            out(m, layer)[rows, :] = value
+            for half in range(2):
+                put_sums(stage, half, b, value[:, half * LANES : (half + 1) * LANES])
+
+    def features(m, hook=None):
+        stage = stages.at[m]
+
+        def body(c):
+            weight = headt[m, pl.ds(pl.multiple_of(c * 256, 256), 256), :]
+            for b in range(BATCHES):
+                value = contract(low(m, L)[b * HALF : (b + 1) * HALF, :], weight, 1, 1)
+                for half in range(2):
+                    piece = value[:, half * LANES : (half + 1) * LANES]
+                    pre[m, 2 * c + half, b * HALF : (b + 1) * HALF, :] = piece
+                    put_sums(stage, 2 * c + half, b, piece)
+            if m == 0:
+                for half in range(2):
+                    save(pre.at[0, 2 * c + half], feat_s.at[2 * c + half], 2 * c + half).start()
+
+        repeat(HEAD // 256, body, hook)
+
+    def head_pool(m, hook=None):
+        tot = total_ref(m, 3, 0)
+
+        def body(c):
+            for b in range(BATCHES):
+                scale, shift = coefs(tot, 4 * c + 2 * b, cnt[b : b + 1, :], gain_h[m, 0:1, lanes(c)], gain_h[m, 1:2, lanes(c)])
+                scale, shift = 0.5 * scale, 0.5 * shift
+                for i in range(IMGS):
+                    slot = b * IMGS + i
+                    rows = slice(slot * ROWS, (slot + 1) * ROWS)
+                    value = act_half(mask[rows, :] * (pre[m, c, rows, :] * scale + shift))
+                    pooled_h[m, slot : slot + 1, lanes(c)] = jnp.sum(value, 0, keepdims=True) / area[0:1, :]
+
+        repeat(HC, body, hook)
+
+    for m in range(2):
+        stages[m] = jnp.zeros((56, LANES), F32)
+    pool_s[...] = jnp.zeros(pool_s.shape, F32)
+    pool_t[...] = jnp.zeros(pool_t.shape, F32)
+    pooled_h[...] = jnp.zeros(pooled_h.shape, F32)
+    stages[0, 48:56, :] = firstrow[...]
+    pending = None
+    for layer in range(L):
+        s_one, t_one = summer(0, 0, layer), summer(1, 0, layer)
+        s_two, t_two = summer(0, 1, layer), summer(1, 1, layer)
+        s_three, t_three = summer(0, 2, layer), summer(1, 2, layer)
+        if layer > 0:
+            update(0, layer - 1)
+        expand(0, layer, None if pending is None else (2, pending.middle))
+        s_one.start(stages.at[0])
+        if layer > 0:
+            pending.finish()
+            update(1, layer - 1)
+        expand(1, layer, (4, s_one.middle))
+        t_one.start(stages.at[1])
+        s_one.finish()
+        if layer == 0:
+            cnt[...] = tot_e[0, 0, 48:56, :]
+        depthwise(0, layer, (2, t_one.middle))
+        s_two.start(stages.at[0])
+        t_one.finish()
+        depthwise(1, layer, (5, s_two.middle))
+        t_two.start(stages.at[1])
+        s_two.finish()
+        pooling(0, layer, (5, t_two.middle))
+        project(0, layer)
+        s_three.start(stages.at[0])
+        t_two.finish()
+        pooling(1, layer, (6, s_three.middle))
+        project(1, layer)
+        t_three.start(stages.at[1])
+        s_three.finish()
+        pending = t_three
+    s_head, t_head = summer(0, 3, 0), summer(1, 3, 0)
+    update(0, L - 1)
+    features(0, (2, pending.middle))
+    s_head.start(stages.at[0])
+    pending.finish()
+    update(1, L - 1)
+    features(1, (4, s_head.middle))
+    t_head.start(stages.at[1])
+    s_head.finish()
+    head_pool(0, (3, t_head.middle))
+    t_head.finish()
+    head_pool(1)
+    for c in range(HC):
+        save(pre.at[0, c], feat_s.at[c], c).wait()
+
+
+def run_forward_all(sizes, inputs):
+    sds = jax.ShapeDtypeStruct
+    vm = pl.BlockSpec(memory_space=pltpu.VMEM)
+    hbm = pl.BlockSpec(memory_space=pl.ANY)
+    outs = [
+        (sds((L, EC, FULL, LANES), F32), hbm),
+        (sds((L, EC, FULL, LANES), F32), hbm),
+        (sds((HC, FULL, LANES), F32), hbm),
+        (sds((L, FULL, C), F32), vm),
+        (sds((L + 1, FULL, C), BF16), vm),
+        (sds((L, 16, E), F32), vm),
+        (sds((L, 16, SE), F32), vm),
+        (sds((L, 16, E), F32), vm),
+        (sds((L, 2, 56, LANES), F32), vm),
+        (sds((L, 8, LANES), F32), vm),
+        (sds((40, LANES), F32), vm),
+        (sds((2, 16, HEAD), F32), vm),
+    ]
+    scratch = [
+        pltpu.VMEM((2, EC, FULL, LANES), F32),
+        pltpu.VMEM((2, FULL, C), F32),
+        pltpu.VMEM((FULL, C), F32),
+        pltpu.VMEM((FULL, C), BF16),
+        pltpu.VMEM((FULL, E), BF16),
+        pltpu.VMEM((SLOTS, ROWS + 2 * GAP, LANES), F32),
+        pltpu.VMEM((2, 56, LANES), F32),
+        pltpu.VMEM((4, 56, LANES), F32),
+        pltpu.VMEM((8, LANES), F32),
+        pltpu.VMEM((16, E), F32),
+        pltpu.VMEM((16, E), F32),
+        pltpu.SemaphoreType.DMA((EC,)),
+    ]
+    for m in range(2):
+        for rows in (56, 48, 8, 40):
+            scratch = scratch + sum_scratch(sizes, rows)
+    return pl.pallas_call(
+        functools.partial(forward_kernel, sizes),
+        out_shape=[o[0] for o in outs],
+        in_specs=[vm] * len(inputs),
+        out_specs=[o[1] for o in outs],
+        scratch_shapes=scratch,
+        compiler_params=pltpu.CompilerParams(collective_id=1, has_side_effects=True, vmem_limit_bytes=63 * 2**20),
+        name="forward",
+    )(*inputs)
 
 
 def objective(logits, target, onehot, coef):
@@ -379,31 +815,59 @@
         (valid[index][:, None] * inside[None, :]).reshape(-1, 1) for index in range(batches)
     ]
     counts_all = [pixels[index] for index in range(batches)]
-    forward_groups = []
-    for index in range(batches):
-        forward_groups = forward_groups + [[(0, index)], [(1, index)]]
     backward_groups = [[index] for index in range(batches)]
-    targets = [None] * batches
-    main_logits = [None] * batches
-    main_blocks = [None] * batches
-    main_heads = [None] * batches
-    for group in forward_groups:
-        models = [shadow if kind == 0 else model for kind, index in group]
-        logits_all, kept_blocks, kept_heads = run_forward(
-            models,
-            [rows_all[index] for kind, index in group],
-            [masks_all[index] for kind, index in group],
-            area,
-            [counts_all[index] for kind, index in group],
-        )
-        place = 0
-        kind, index = group[place]
-        if kind == 0:
-            targets[index] = jax.nn.log_softmax(logits_all[place])
-        else:
-            main_logits[index] = logits_all[place]
-            main_blocks[index] = [kept_blocks[layer][place] for layer in range(layers)]
-            main_heads[index] = kept_heads[place]
+    sizes = (lax.axis_size("dp"), lax.axis_size("shard"))
+    both = [jnp.stack([model[item], shadow[item]]) for item in range(5)]
+    spot_l = (spot % S > 0).astype(F32)[:, None]
+    spot_r = (spot % S < S - 1).astype(F32)[:, None]
+    spread_l = jnp.broadcast_to(spot_l, (S * S, LANES))
+    spread_r = jnp.broadcast_to(spot_r, (S * S, LANES))
+    mask_all = jnp.broadcast_to(jnp.concatenate(masks_all, 0), (FULL, LANES))
+    own = jnp.concatenate([jnp.sum(valid, 1) * area_value, jnp.sum(weighted, 1), jnp.zeros((4,), F32)])
+    chan_f = both[1].astype(F32)
+    gains_f = both[4].astype(F32)
+    n_sh = sizes[1]
+    block_width = gains_f.shape[2] - 2 * (HEAD // n_sh) - CLASSES // n_sh
+    blocks = gains_f[:, :, :block_width].reshape(2, n_sh, L, -1)
+    wide = 5 * E // n_sh
+    vec_e = blocks[..., :wide].reshape(2, n_sh, L, 5, E // n_sh).transpose(0, 2, 3, 1, 4).reshape(2, L, 5, E)
+    vec_c = blocks[..., wide : wide + 2 * C // n_sh].reshape(2, n_sh, L, 2, C // n_sh).transpose(0, 2, 3, 1, 4).reshape(2, L, 2, C)
+    vec_s = blocks[..., wide + 2 * C // n_sh :].transpose(0, 2, 1, 3).reshape(2, L, 1, SE)
+    heads_f = gains_f[:, :, block_width : block_width + 2 * HEAD // n_sh]
+    vec_h = heads_f.reshape(2, n_sh, 2, HEAD // n_sh).transpose(0, 2, 1, 3).reshape(2, 2, HEAD)
+    class_bias = gains_f[:, :, block_width + 2 * HEAD // n_sh :].reshape(2, CLASSES)
+    inputs = [
+        images.reshape(FULL, C), mask_all, spread_l, spread_r, jnp.full((1, LANES), area_value),
+        jnp.broadcast_to(own[:, None], (8, LANES)), both[0], both[2].transpose(0, 2, 1),
+        chan_f[:, :, :9], chan_f[:, :, 9 : 9 + SE], chan_f[:, :, 9 + SE :], vec_e, vec_c, vec_h, vec_s,
+    ]
+    (pre_s, mixed_s, feat_s, out_s, low_s, pool_s, unit_s, gate_s, tot_e, tot_c, tot_h, pooled_h) = run_forward_all(sizes, inputs)
+    logits = [jnp.dot(pooled_h[m, :SLOTS].astype(BF16), both[3][m], preferred_element_type=F32) + class_bias[m] for m in range(2)]
+    main_logits = [logits[0][b * IMGS : (b + 1) * IMGS] for b in range(2)]
+    targets = [jax.nn.log_softmax(logits[1][b * IMGS : (b + 1) * IMGS]) for b in range(2)]
+
+    def plain(value, b):
+        return value[:, b * HALF : (b + 1) * HALF].transpose(1, 0, 2).reshape(HALF, -1)
+
+    def stats(tot, b, chunks):
+        pairs = tot[: 4 * chunks].reshape(chunks, 2, 2, LANES)[:, b]
+        mean = pairs[:, 0].reshape(-1) / counts_all[b]
+        return (mean, lax.rsqrt(pairs[:, 1].reshape(-1) / counts_all[b] - mean * mean + EPS_NORM))
+
+    main_blocks = []
+    main_heads = []
+    for b in range(2):
+        rows = slice(b * HALF, (b + 1) * HALF)
+        kept = []
+        for layer in range(layers):
+            mixed = plain(mixed_s[layer], b)
+            st = stats(tot_e[layer, 1], b, EC)
+            second = norm_apply(mixed, masks_all[b], vec_e[0, layer, 2], vec_e[0, layer, 3], st[0], st[1])
+            act = jax.nn.silu(second).reshape(IMGS, ROWS, E) * gate_s[layer, b * IMGS : (b + 1) * IMGS][:, None, :]
+            kept.append((low_s[layer, rows], plain(pre_s[layer], b), stats(tot_e[layer, 0], b, EC), mixed, st,
+                         act.reshape(HALF, E).astype(BF16), out_s[layer, rows], stats(tot_c[layer], b, 2)))
+        main_blocks.append(kept)
+        main_heads.append((low_s[layers, rows], plain(feat_s, b), stats(tot_h, b, HC), pooled_h[0, b * IMGS : (b + 1) * IMGS].astype(BF16)))
     grad_mats = jnp.zeros(model[0].shape, jnp.float32)
     grad_chan = jnp.zeros(model[1].shape, jnp.float32)
     grad_head = jnp.zeros(model[2].shape, jnp.float32)

time: 2160 us -> 1870 us (0.87)
  blocking collectives: 759 us -> 392 us
  other arithmetic: 735 us -> 515 us
  local copies, waits for them, and re-layouts: 247 us -> 451 us
  Pallas kernels: 0 us -> 129 us
  matrix products: 125 us -> 96.6 us
    psum x9 -> x0, blocking collectives: 366 us -> none  [norm_stats(): sums = lax.psum((sums_first, sums_second), ('dp', 'shard'))]
    reduce_sum x15 -> x2, other arithmetic: 204 us -> 0.4 us  [per_device(): jax.nn.log_softmax(logits[1][b * IMGS:(b + 1) * IMGS])]
    transpose x0 -> x29, local copies, waits for them, and re-layouts: none -> 143 us  [the longest x25 143 us: plain(): value[:, b * HALF:(b + 1) * HALF].transpose(1, 0, 2).reshape(HALF, -1)]
    reshape x0 -> x31, local copies, waits for them, and re-layouts: none -> 130 us  [the longest x20 125 us: plain(): value[:, b * HALF:(b + 1) * HALF].transpose(1, 0, 2).reshape(HALF, -1)]
    pallas_call x0 -> x1, Pallas kernels: none -> 129 us  [run_forward_all(): pl.pallas_call(functools.partial(forward_kernel, sizes), out_shape=[o[0]...]
    add_any x8 -> x4, other arithmetic: 112 us -> 36.6 us  [spread(): padded[:, offset // 3:offset // 3 + S, offset % 3:offset % 3 + S, :]]
    reshape x16 -> x4, local copies, waits for them, and re-layouts: 93.1 us -> 22.3 us  [spread(): return total.reshape(first.shape)]
    reduce_sum x6, other arithmetic: 183 us -> 117 us  [spread(): padded[:, offset // 3:offset // 3 + S, offset % 3:offset % 3 + S, :]]
  transfers between devices with their start and end apart: 5 -> 5, of which waited for: 1 -> 1; matrix products, arithmetic and copies ran while one was open for 23% -> 10% of each run, Pallas kernels for 0% -> 7%
where the time goes in v1:
time: 1870 us; the launch traced here: 1860 us
  other arithmetic  515 us (28%)
  local copies, waits for them, and re-layouts  451 us (24%)
  blocking collectives  392 us (21%)
  waiting for transfers between devices  256 us (14%)
  Pallas kernels  129 us (7%)
  matrix products  96.6 us (5%)
  between operations  22.3 us (1%)
    psum x1, waiting for transfers between devices, per_device(): lax.psum((loss_spread, grad_mats, grad_chan, grad_head, grad_class, grad_...  256 us
    psum x6, blocking collectives, norm_back(): sums = lax.psum((sums_first, sums_second), ('dp', 'shard'))  242 us
    transpose x25, local copies, waits for them, and re-layouts, plain(): value[:, b * HALF:(b + 1) * HALF].transpose(1, 0, 2).reshape(HALF, -1)  143 us
    pallas_call x1, Pallas kernels, run_forward_all(): pl.pallas_call(functools.partial(forward_kernel, sizes), out_shape=[o[0]...  129 us
    reduce_sum x9, other arithmetic, norm_back(): gain_grad = jnp.sum(masks[0] * grads[0] * units, 0)  129 us
    reshape x20, local copies, waits for them, and re-layouts, plain(): value[:, b * HALF:(b + 1) * HALF].transpose(1, 0, 2).reshape(HALF, -1)  125 us
    reduce_sum x6, other arithmetic, spread(): padded[:, offset // 3:offset // 3 + S, offset % 3:offset % 3 + S, :]  117 us
    mul x2, other arithmetic, spread(): padded[:, offset // 3:offset // 3 + S, offset % 3:offset % 3 + S, :]  72.6 us
  transfers between devices with their start and end apart: 5, of which 1 were waited for; matrix products, arithmetic and copies ran while one was open for 10% of the time, Pallas kernels for 7%

profile of v1, /device:TPU:0, one launch (start us, length us, event | category | flops | bytes accessed | tf_op | source)
XLA Modules:
  0.0 1862.4 jit_solution(173019818682073798)
XLA Ops:
  18.1 14.7 all_gather.34
  33.0 15.0 all_gather.35
  67.9 41.0 %all-reduce.91 = (f32[2]{0:T(128)S(1)}, f32[2]{0:T(128)S(1)}) all-reduce(f32[2]{0:T(128)S(1)} %get-tuple-element.472, f32[2]{0:T(128)S(1)} %broadcast_multiply_fusion.40), channel_id=1, replica_groups=mesh['dp'=8,'shard'=4] {'dp','shard'}, use_global_device_ids=true, to_apply=%region_1.2 | all-reduce | flops 4 | bytes 32 | tf_op jit(solution)/shard_map/psum | solution.py:806
  112.0 8.7 all_gather.32
  120.7 11.8 all_gather.33
  156.7 128.9 %forward.1 = (f32[2,12,1440,128]{3,2,1,0:T(8,128)}, f32[2,12,1440,128]{3,2,1,0:T(8,128)}, f32[10,1440,128]{2,1,0:T(8,128)}, f32[2,1440,256]{2,1,0:T(8,128)}, bf1...) custom-call(bf16[1440,256]{1,0:T(8,128)(2,1)} %reshape.3252.refs_0_,, ...), custom_call_target="tpu_custom_call" | custom-call | tf_op jit(solution)/shard_map/forward/pallas_call | solution.py:696
  285.6 10.4 slice_bitcast_fusion.3
  296.0 12.4 slice_bitcast_fusion.2
  323.2 6.3 copy.426
  335.4 7.6 slice_bitcast_fusion.10
  348.9 6.3 copy.431
  361.3 6.3 copy.451
  367.5 6.2 slice_bitcast_fusion.5
  385.7 6.3 copy.432
  397.9 7.6 slice_bitcast_fusion.4
  411.4 6.3 copy.455
  423.8 6.3 copy.435
  459.9 7.5 slice_bitcast_fusion.13
  469.6 6.7 fusion.133
  479.5 39.6 %all-reduce.90 = (f32[1280]{0:T(1024)S(1)}, f32[1,1280]{1,0:T(1,128)S(1)}, f32[1280]{0:T(1024)S(1)}, f32[1,1280]{1,0:T(1,128)S(1)}) all-reduce(f32[1280]{0:T(1024)S(1)} %bitcast.676, f32[1,1280]{1,0:T(1,128)S(1)} %bitcast.682, f32[1280]{0:T(1024)S(1)} %bitcast.677, ...), channel_id=1, replica_groups=mesh['dp'=8,'shard'=4] {'dp','shard'}, use_global_device_ids=true, to_apply=%region_30.33 | all-reduce | flops 5120 | bytes 40960 | tf_op jit(solution)/shard_map/psum | solution.py:67
  542.8 9.2 fusion.119
  558.9 39.9 %all-reduce.89 = (f32[256]{0:T(256)S(1)}, f32[1,256]{1,0:T(1,128)S(1)}, f32[256]{0:T(256)S(1)}, f32[1,256]{1,0:T(1,128)S(1)}) all-reduce(f32[256]{0:T(256)S(1)} %get-tuple-element.292, f32[1,256]{1,0:T(1,128)S(1)} %bitcast.718, f32[256]{0:T(256)S(1)} %get-tuple-element.301, ...), channel_id=1, replica_groups=mesh['dp'=8,'shard'=4] {'dp','shard'}, use_global_device_ids=true, to_apply=%region_34.37 | all-reduce | flops 1024 | bytes 8192 | tf_op jit(solution)/shard_map/psum | solution.py:67
  612.9 6.5 reshape.3270
  619.4 6.5 reshape.3286
  626.0 8.4 multiply_reduce_fusion.23
  643.4 10.0 multiply_reduce_fusion.12
  661.6 10.1 multiply_reduce_fusion.14
  671.7 40.8 %all-reduce.88 = (f32[1536]{0:T(1024)S(1)}, f32[1,1536]{1,0:T(1,128)S(1)}, f32[1536]{0:T(1024)S(1)}, f32[1,1536]{1,0:T(1,128)S(1)}) all-reduce(f32[1536]{0:T(1024)S(1)} %get-tuple-element.258, f32[1,1536]{1,0:T(1,128)S(1)} %stack.230, f32[1536]{0:T(1024)S(1)} %get-tuple-element.254, ...), channel_id=1, replica_groups=mesh['dp'=8,'shard'=4] {'dp','shard'}, use_global_device_ids=true, to_apply=%region_40.43 | all-reduce | flops 6144 | bytes 49152 | tf_op jit(solution)/shard_map/psum | solution.py:67
  727.4 17.2 multiply_reduce_fusion.16
  755.8 7.0 reshape.3277
  762.9 36.3 %broadcast_multiply_fusion.34 = (f32[5,12,12,1536]{3,2,1,0:T(8,128)}, f32[5,12,12,1536]{3,2,1,0:T(8,128)}, f32[5,12,12,1536]{3,2,1,0:T(8,128)}, f32[5,12,12,1536...) fusion(f32[5,12,12,1536]{3,2,1,0:T(8,128)} %reshape.3290, ...), kind=kLoop, calls=%fused_computation.371 | loop fusion | flops 19906560 | bytes 88528896 | tf_op jit(solution)/shard_map/transpose(jvp())/mul | solution.py:84
  799.2 10.6 pad_add_fusion.3
  809.8 24.0 %multiply_reduce_fusion.2 = (f32[1536]{0:T(1024)}, f32[1536]{0:T(1024)S(1)}, f32[1536]{0:T(1024)S(1)}, f32[1536]{0:T(1024)}, f32[5,12,12,1536]{3,2,1,0:T(8,128)}...) fusion(f32[5,12,12,1536]{3,2,1,0:T(8,128)S(1)} %copy-done, f32[1536]{0:T(1024)S(1)} %fusion.247, ...), kind=kLoop, calls=%fused_computation.154 | loop fusion | flops 32065536 | bytes 48712512 | tf_op jit(solution)/shard_map/reduce_sum | solution.py:68
  839.7 7.0 reshape.3293
  846.7 10.6 pad_add_fusion.1
  857.3 23.2 %multiply_reduce_fusion = (f32[1536]{0:T(1024)}, f32[1536]{0:T(1024)S(1)}, f32[1536]{0:T(1024)S(1)}, f32[1536]{0:T(1024)}, f32[5,12,12,1536]{3,2,1,0:T(8,128)}, ...) fusion(f32[5,12,12,1536]{3,2,1,0:T(8,128)S(1)} %copy-done.1, f32[1536]{0:T(1024)S(1)} %fusion.239, ...), kind=kLoop, calls=%fused_computation.152 | loop fusion | flops 32065536 | bytes 48712512 | tf_op jit(solution)/shard_map/reduce_sum | solution.py:68
  880.5 40.4 %all-reduce.87 = (f32[1536]{0:T(1024)S(1)}, f32[1,1536]{1,0:T(1,128)S(1)}, f32[1536]{0:T(1024)S(1)}, f32[1,1536]{1,0:T(1,128)S(1)}) all-reduce(f32[1536]{0:T(1024)S(1)} %get-tuple-element.214, f32[1,1536]{1,0:T(1,128)S(1)} %stack.232, f32[1536]{0:T(1024)S(1)} %get-tuple-element.210, ...), channel_id=1, replica_groups=mesh['dp'=8,'shard'=4] {'dp','shard'}, use_global_device_ids=true, to_apply=%region_44.47 | all-reduce | flops 6144 | bytes 49152 | tf_op jit(solution)/shard_map/psum | solution.py:67
  929.8 7.6 fusion.181
  937.6 8.1 multiply_reduce_fusion.45
  945.7 40.2 %all-reduce.86 = (f32[256]{0:T(256)S(1)}, f32[1,256]{1,0:T(1,128)S(1)}, f32[256]{0:T(256)S(1)}, f32[1,256]{1,0:T(1,128)S(1)}) all-reduce(f32[256]{0:T(256)S(1)} %get-tuple-element.296, f32[1,256]{1,0:T(1,128)S(1)} %bitcast.716, f32[256]{0:T(256)S(1)} %get-tuple-element.299, ...), channel_id=1, replica_groups=mesh['dp'=8,'shard'=4] {'dp','shard'}, use_global_device_ids=true, to_apply=%region_48.51 | all-reduce | flops 1024 | bytes 8192 | tf_op jit(solution)/shard_map/psum | solution.py:67
  997.9 6.5 reshape.3278
  1004.4 6.6 reshape.3294
  1011.1 8.6 multiply_reduce_fusion.21
  1051.4 9.3 multiply_reduce_fusion.13
  1066.7 9.4 multiply_reduce_fusion.15
  1076.1 40.7 %all-reduce.85 = (f32[1536]{0:T(1024)S(1)}, f32[1,1536]{1,0:T(1,128)S(1)}, f32[1536]{0:T(1024)S(1)}, f32[1,1536]{1,0:T(1,128)S(1)}) all-reduce(f32[1536]{0:T(1024)S(1)} %get-tuple-element.260, f32[1,1536]{1,0:T(1,128)S(1)} %stack.236, f32[1536]{0:T(1024)S(1)} %get-tuple-element.256, ...), channel_id=1, replica_groups=mesh['dp'=8,'shard'=4] {'dp','shard'}, use_global_device_ids=true, to_apply=%region_54.57 | all-reduce | flops 6144 | bytes 49152 | tf_op jit(solution)/shard_map/psum | solution.py:67
  1131.5 16.5 multiply_reduce_fusion.17
  1159.2 7.0 reshape.3299
  1166.3 36.3 %broadcast_multiply_fusion.17 = (f32[5,12,12,1536]{3,2,1,0:T(8,128)}, f32[5,12,12,1536]{3,2,1,0:T(8,128)}, f32[5,12,12,1536]{3,2,1,0:T(8,128)}, f32[5,12,12,1536...) fusion(f32[5,12,12,1536]{3,2,1,0:T(8,128)} %reshape.3282, ...), kind=kLoop, calls=%fused_computation.354 | loop fusion | flops 19906560 | bytes 88528896 | tf_op jit(solution)/shard_map/transpose(jvp())/mul | solution.py:84
  1202.6 7.7 pad_add_fusion
  1210.5 19.6 %multiply_reduce_fusion.1 = (f32[1536]{0:T(1024)S(1)}, f32[1536]{0:T(1024)S(1)}, f32[1536]{0:T(1024)S(1)}, f32[1536]{0:T(1024)S(1)}, f32[5,12,12,1536]{3,2,1,0:T(8,128)}, /*index=5*/f32[5,12,12,1536]{3,2,1,0:T(8,128)}) fusion(f32[5,12,12,1536]{3,2,1,0:T(8,128)S(1)} %copy-done.2, f32[1536]{0:T(1024)S(1)} %bitcast.661, f32[1536]{0:T(1024)S(1)} %fusion.243, ...), kind=kLoop, calls=%fused_computation.153 | loop fusion | flops 32065536 | bytes 44288832 | tf_op jit(solution)/shard_map/reduce_sum | solution.py:68
  1240.4 7.1 reshape.3283
  1247.5 7.7 pad_add_fusion.2
  1255.4 19.7 %multiply_reduce_fusion.3 = (f32[1536]{0:T(1024)S(1)}, f32[1536]{0:T(1024)S(1)}, f32[1536]{0:T(1024)S(1)}, f32[1536]{0:T(1024)S(1)}, f32[5,12,12,1536]{3,2,1,0:T(8,128)}, /*index=5*/f32[5,12,12,1536]{3,2,1,0:T(8,128)}) fusion(f32[5,12,12,1536]{3,2,1,0:T(8,128)S(1)} %copy-done.3, f32[1536]{0:T(1024)S(1)} %bitcast.658, f32[1536]{0:T(1024)S(1)} %fusion.251, ...), kind=kLoop, calls=%fused_computation.155 | loop fusion | flops 32065536 | bytes 44288832 | tf_op jit(solution)/shard_map/reduce_sum | solution.py:68
  1291.3 20.9 %fusion.33 = (f32[1536]{0:T(1024)S(1)}, f32[1536]{0:T(1024)S(1)}, f32[1536]{0:T(1024)S(1)}, f32[1536]{0:T(1024)S(1)}, f32[1536]{0:T(1024)S(1)}, /*index=5*/f32[1536]{0:T(1024)S(1)}, f32[1536]{0:T(1024)S(1)}, f32[1536]{0:T(1024)S(1)}) fusion(f32[5,12,12,1536]{3,2,1,0:T(8,128)} %reshape.3298, f32[5,12,12,1536]{3,2,1,0:T(8,128)} %get-tuple-element.490), kind=kLoop, calls=%fused_computation.85 | loop fusion | flops 17682432 | bytes 8896512 | tf_op jit(solution)/shard_map/transpose(jvp())/reduce_sum | solution.py:84
  1317.6 21.0 %fusion.49 = (f32[1536]{0:T(1024)S(1)}, f32[1536]{0:T(1024)S(1)}, f32[1536]{0:T(1024)S(1)}, f32[1536]{0:T(1024)S(1)}, f32[1536]{0:T(1024)S(1)}, /*index=5*/f32[1536]{0:T(1024)S(1)}, f32[1536]{0:T(1024)S(1)}, f32[1536]{0:T(1024)S(1)}) fusion(f32[5,12,12,1536]{3,2,1,0:T(8,128)} %reshape.3290, f32[5,12,12,1536]{3,2,1,0:T(8,128)} %get-tuple-element.491), kind=kLoop, calls=%fused_computation.101 | loop fusion | flops 17682432 | bytes 8896512 | tf_op jit(solution)/shard_map/transpose(jvp())/reduce_sum | solution.py:84
  1344.0 20.8 %fusion.1 = (f32[1536]{0:T(1024)S(1)}, f32[1536]{0:T(1024)S(1)}, f32[1536]{0:T(1024)S(1)}, f32[1536]{0:T(1024)S(1)}, f32[1536]{0:T(1024)S(1)}, /*index=5*/f32[1536]{0:T(1024)S(1)}, f32[1536]{0:T(1024)S(1)}, f32[1536]{0:T(1024)S(1)}) fusion(f32[5,12,12,1536]{3,2,1,0:T(8,128)} %reshape.3282, f32[5,12,12,1536]{3,2,1,0:T(8,128)} %get-tuple-element.492), kind=kLoop, calls=%fused_computation.53 | loop fusion | flops 17682432 | bytes 8896512 | tf_op jit(solution)/shard_map/transpose(jvp())/reduce_sum | solution.py:84
  1370.2 20.5 %fusion.17 = (f32[1536]{0:T(1024)S(1)}, f32[1536]{0:T(1024)S(1)}, f32[1536]{0:T(1024)S(1)}, f32[1536]{0:T(1024)S(1)}, f32[1536]{0:T(1024)S(1)}, /*index=5*/f32[1536]{0:T(1024)S(1)}, f32[1536]{0:T(1024)S(1)}, f32[1536]{0:T(1024)S(1)}) fusion(f32[5,12,12,1536]{3,2,1,0:T(8,128)} %reshape.3274, f32[5,12,12,1536]{3,2,1,0:T(8,128)} %get-tuple-element.493), kind=kLoop, calls=%fused_computation.69 | loop fusion | flops 17682432 | bytes 8896512 | tf_op jit(solution)/shard_map/transpose(jvp())/reduce_sum | solution.py:84
  1408.6 41.7 %all-reduce.84 = (f32[4]{0:T(128)}, f32[1536]{0:T(1024)S(1)}, f32[1,1536]{1,0:T(1,128)S(1)}, f32[1536]{0:T(1024)S(1)}, f32[1,1536]{1,0:T(1,128)S(1)}) all-reduce(f32[4]{0:T(128)S(1)} %broadcast_in_dim.179, f32[1536]{0:T(1024)S(1)} %get-tuple-element.216, ...), channel_id=1, replica_groups=mesh['dp'=8,'shard'=4] {'dp','shard'}, use_global_device_ids=true, to_apply=%region_14.17 | all-reduce | flops 6148 | bytes 49184 | tf_op jit(solution)/shard_map/psum | solution.py:935
  1451.1 12.1 multiply_convert_fusion.1
  1465.5 9.9 fusion.149
  1496.3 10.3 multiply_convert_fusion.3
  1553.7 256.2 %all-reduce.96.cloned.1.call-done = (f32[2,256,3072]{2,1,0:T(8,128)}, f32[1280,1000]{1,0:T(8,128)}, f32[256,1280]{0,1:T(8,128)}, f32[2,137,1536]{2,1,0:T(8,128)}, f32[4,5018]{1,0:T(4,128)}) async-done(((f32[2,256,3072]{2,1,0:T(8,128)}, f32[1280,1000]{1,0:T(8,128)}, f32[256,1280]{0,1:T(8,128)}, f32[2,137,1536]{2,1,0:T(8,128)}, f32[4,5018]{1,0:T(4,128)}), (f32[2,256,3072]{2,1,0:T(8,128)}, ...) | async-done | bytes 14485936 | tf_op jit(solution)/shard_map/psum | solution.py:935
  1828.3 7.0 all-reduce.93
  (1025 shorter events, 497.8 us)
Async XLA Ops:
  7.2 139.7 %all-gather.7.cloned.1.call-start = ((), (), s32[]{:S(2)}) async-start(), calls=%async_computation | async-start | bytes 3932160 | tf_op jit(solution)/shard_map/all_gather | solution.py:783
  11.0 136.0 %all-gather.9.cloned.1.call-start = ((), (), s32[]{:S(2)}) async-start(), calls=%async_computation.1 | async-start | bytes 3932160 | tf_op jit(solution)/shard_map/all_gather | solution.py:788
  13.5 416.7 %all-gather.13.cloned.1.call-start = ((), (), s32[]{:S(2)}) async-start(), calls=%async_computation.3 | async-start | bytes 3276800 | tf_op jit(solution)/shard_map/all_gather | solution.py:791
  14.5 420.4 %all-gather.11.cloned.1.call-start = ((), (), s32[]{:S(2)}) async-start(), calls=%async_computation.2 | async-start | bytes 3276800 | tf_op jit(solution)/shard_map/all_gather | solution.py:786
  16.4 1793.5 %all-reduce.96.cloned.1.call-start = ((), (), s32[]{:S(2)}) async-start(), calls=%async_computation.4 | async-start | bytes 29392896 | tf_op jit(solution)/shard_map/psum | solution.py:935
  32.8 34.9 %copy-start.18 = (bf16[2,137,1536]{2,1,0:T(8,128)(2,1)}, bf16[2,137,1536]{2,1,0:T(8,128)(2,1)S(1)}, u32[]{:S(2)}) copy-start(bf16[2,137,1536]{2,1,0:T(8,128)(2,1)S(1)} %all_gather.34) | copy-start | bytes 2525188
  33.0 23.3 %copy-start.127 = (f32[1,5018]{1,0:T(1,128)S(1)}, f32[1,5018]{1,0:T(1,128)}, u32[]{:S(2)}) copy-start(f32[1,5018]{1,0:T(1,128)} %param.53) | copy-start | bytes 60220
  48.0 63.3 %copy-start.46 = (f32[256,320]{0,1:T(8,128)S(1)}, f32[256,320]{0,1:T(8,128)}, u32[]{:S(2)}) copy-start(f32[256,320]{0,1:T(8,128)} %param.42) | copy-start | bytes 983044
  50.1 70.6 %copy-start.59 = (f32[256,320]{0,1:T(8,128)S(1)}, f32[256,320]{0,1:T(8,128)}, u32[]{:S(2)}) copy-start(f32[256,320]{0,1:T(8,128)} %param.45) | copy-start | bytes 983044
  50.1 82.5 %copy-start.62 = (bf16[2,5,12,12,256]{4,0,3,2,1:T(2,128)(2,1)S(1)}, bf16[2,5,12,12,256]{4,0,3,2,1:T(2,128)(2,1)}, u32[]{:S(2)}) copy-start(bf16[2,5,12,12,256]{4,0,3,2,1:T(2,128)(2,1)} %param.28) | copy-start | bytes 2211844
  63.2 562.7 %copy-start.83 = (f32[5,144]{1,0:T(8,128)}, f32[5,144]{1,0:T(8,128)S(1)}, u32[]{:S(2)}) copy-start(f32[5,144]{1,0:T(8,128)S(1)} %get-tuple-element.643) | copy-start | bytes 8644
  63.2 562.7 %copy-start.86 = (f32[5,144]{1,0:T(8,128)}, f32[5,144]{1,0:T(8,128)S(1)}, u32[]{:S(2)}) copy-start(f32[5,144]{1,0:T(8,128)S(1)} %get-tuple-element.644) | copy-start | bytes 8644
  64.4 478.3 %copy-start.135 = (f32[1280]{0:T(1024)}, f32[1280]{0:T(1024)S(1)}, u32[]{:S(2)}) copy-start(f32[1280]{0:T(1024)S(1)} %add.998) | copy-start | bytes 15364
  64.6 478.1 %copy-start.137 = (f32[1280]{0:T(1024)}, f32[1280]{0:T(1024)S(1)}, u32[]{:S(2)}) copy-start(f32[1280]{0:T(1024)S(1)} %mul.3152) | copy-start | bytes 15364
  66.1 69.8 %copy-start.258 = (f32[4,64]{1,0:T(4,128)S(1)}, f32[4,64]{1,0:T(4,128)}, u32[]{:S(2)}) copy-start(f32[4,64]{1,0:T(4,128)} %get-tuple-element.573) | copy-start | bytes 3076
  66.1 70.5 %copy-start.256 = (f32[4,16]{1,0:T(4,128)S(1)}, f32[4,16]{1,0:T(4,128)}, u32[]{:S(2)}) copy-start(f32[4,16]{1,0:T(4,128)} %get-tuple-element.571) | copy-start | bytes 772
  66.1 72.9 %copy-start.264 = (f32[5]{0:T(128)S(1)}, f32[5]{0:T(128)}, u32[]{:S(2)}) copy-start(f32[5]{0:T(128)} %copy-done.263) | copy-start | bytes 64
  66.2 72.9 %copy-start.266 = (f32[5]{0:T(128)S(1)}, f32[5]{0:T(128)}, u32[]{:S(2)}) copy-start(f32[5]{0:T(128)} %copy-done.265) | copy-start | bytes 64
  66.2 73.6 %copy-start.257 = (f32[4,64]{1,0:T(4,128)S(1)}, f32[4,64]{1,0:T(4,128)}, u32[]{:S(2)}) copy-start(f32[4,64]{1,0:T(4,128)} %get-tuple-element.572) | copy-start | bytes 3076
  66.2 75.5 %copy-start.255 = (f32[4,16]{1,0:T(4,128)S(1)}, f32[4,16]{1,0:T(4,128)}, u32[]{:S(2)}) copy-start(f32[4,16]{1,0:T(4,128)} %get-tuple-element.570) | copy-start | bytes 772
  120.7 431.3 %copy-start.49 = (bf16[256,1280]{0,1:T(8,128)(2,1)}, bf16[256,1280]{0,1:T(8,128)(2,1)S(1)}, u32[]{:S(2)}) copy-start(bf16[256,1280]{0,1:T(8,128)(2,1)S(1)} %all_gather.32) | copy-start | bytes 1966084
  146.1 291.6 %copy-start.259 = (f32[5]{0:T(128)}, f32[5]{0:T(128)S(1)}, u32[]{:S(2)}) copy-start(f32[5]{0:T(128)S(1)} %get-tuple-element.640) | copy-start | bytes 64
  146.1 291.9 %copy-start.261 = (f32[5]{0:T(128)}, f32[5]{0:T(128)S(1)}, u32[]{:S(2)}) copy-start(f32[5]{0:T(128)S(1)} %get-tuple-element.467) | copy-start | bytes 64
  433.6 109.1 %copy-start.139 = (f32[1280]{0:T(1024)}, f32[1280]{0:T(1024)S(1)}, u32[]{:S(2)}) copy-start(f32[1280]{0:T(1024)S(1)} %get-tuple-element.620) | copy-start | bytes 15364
  434.9 107.8 %copy-start.141 = (f32[1280]{0:T(1024)}, f32[1280]{0:T(1024)S(1)}, u32[]{:S(2)}) copy-start(f32[1280]{0:T(1024)S(1)} %fusion.259) | copy-start | bytes 15364
  442.0 100.7 %copy-start.70 = (f32[5,1280]{1,0:T(8,128)}, f32[5,1280]{1,0:T(8,128)S(1)}, u32[]{:S(2)}) copy-start(f32[5,1280]{1,0:T(8,128)S(1)} %convolution_divide_fusion.1) | copy-start | bytes 76804
  450.7 92.0 %copy-start.72 = (f32[5,1280]{1,0:T(8,128)}, f32[5,1280]{1,0:T(8,128)S(1)}, u32[]{:S(2)}) copy-start(f32[5,1280]{1,0:T(8,128)S(1)} %convolution_divide_fusion) | copy-start | bytes 76804
  459.2 83.5 %copy-start.121 = (f32[10,128]{1,0:T(8,128)}, f32[10,128]{1,0:T(8,128)S(1)}, u32[]{:S(2)}) copy-start(f32[10,128]{1,0:T(8,128)S(1)} %get-tuple-element.462) | copy-start | bytes 15364
  519.2 23.6 %copy-start.186 = (f32[1280]{0:T(1024)}, f32[1280]{0:T(1024)S(1)}, u32[]{:S(2)}) copy-start(f32[1280]{0:T(1024)S(1)} %get-tuple-element.403) | copy-start | bytes 15364
  519.2 23.6 %copy-start.188 = (f32[1280]{0:T(1024)}, f32[1280]{0:T(1024)S(1)}, u32[]{:S(2)}) copy-start(f32[1280]{0:T(1024)S(1)} %get-tuple-element.405) | copy-start | bytes 15364
  554.8 49.0 %copy-start.11 = (bf16[2,256,3072]{2,1,0:T(8,128)(2,1)S(1)}, bf16[2,256,3072]{2,1,0:T(8,128)(2,1)}, u32[]{:S(2)}) copy-start(bf16[2,256,3072]{2,1,0:T(8,128)(2,1)} %all-gather.7.cloned.1.call-done) | copy-start | bytes 9437188
  714.6 215.1 %copy-start.92 = (f32[12,128]{1,0:T(8,128)}, f32[12,128]{1,0:T(8,128)S(1)}, u32[]{:S(2)}) copy-start(f32[12,128]{1,0:T(8,128)S(1)} %get-tuple-element.359) | copy-start | bytes 18436
  715.3 222.1 %copy-start.90 = (f32[12,128]{1,0:T(8,128)}, f32[12,128]{1,0:T(8,128)S(1)}, u32[]{:S(2)}) copy-start(f32[12,128]{1,0:T(8,128)S(1)} %get-tuple-element.367) | copy-start | bytes 18436
  727.3 202.4 %copy-start.118 = (f32[1536]{0:T(1024)}, f32[1536]{0:T(1024)S(1)}, u32[]{:S(2)}) copy-start(f32[1536]{0:T(1024)S(1)} %fusion.239) | copy-start | bytes 18436
  727.3 210.1 %copy-start.116 = (f32[1536]{0:T(1024)}, f32[1536]{0:T(1024)S(1)}, u32[]{:S(2)}) copy-start(f32[1536]{0:T(1024)S(1)} %fusion.247) | copy-start | bytes 18436
  937.5 53.3 %copy-start.22 = (bf16[256,3072]{1,0:T(8,128)(2,1)S(1)}, bf16[256,3072]{1,0:T(8,128)(2,1)}, u32[]{:S(2)}) copy-start(bf16[256,3072]{1,0:T(8,128)(2,1)} %get-tuple-element.534) | copy-start | bytes 4718596
  1066.7 51.4 %copy-start.124 = (f32[1,1,48,128]{3,2,1,0:T(8,128)S(1)}, f32[1,1,48,128]{3,2,1,0:T(8,128)}, u32[]{:S(2)}) copy-start(f32[1,1,48,128]{3,2,1,0:T(8,128)} %get-tuple-element.559) | copy-start | bytes 73732
  1210.4 23.0 %copy-start.181 = (f32[1536]{0:T(1024)S(1)}, f32[1536]{0:T(1024)}, u32[]{:S(2)}) copy-start(f32[1536]{0:T(1024)} %get-tuple-element.209) | copy-start | bytes 18436
  1210.4 23.6 %copy-start.180 = (f32[1536]{0:T(1024)S(1)}, f32[1536]{0:T(1024)}, u32[]{:S(2)}) copy-start(f32[1536]{0:T(1024)} %get-tuple-element.267) | copy-start | bytes 18436
  1210.4 24.2 %copy-start.152 = (f32[1536]{0:T(1024)S(1)}, f32[1536]{0:T(1024)}, u32[]{:S(2)}) copy-start(f32[1536]{0:T(1024)} %get-tuple-element.253) | copy-start | bytes 18436
  1210.4 24.8 %copy-start.151 = (f32[1536]{0:T(1024)S(1)}, f32[1536]{0:T(1024)}, u32[]{:S(2)}) copy-start(f32[1536]{0:T(1024)} %get-tuple-element.283) | copy-start | bytes 18436
  1210.4 25.4 %copy-start.288 = (f32[64]{0:T(128)S(1)}, f32[64]{0:T(128)}, u32[]{:S(2)}) copy-start(f32[64]{0:T(128)} %get-tuple-element.671) | copy-start | bytes 772
  1210.4 26.0 %copy-start.252 = (f32[1536]{0:T(1024)S(1)}, f32[1536]{0:T(1024)}, u32[]{:S(2)}) copy-start(f32[1536]{0:T(1024)} %get-tuple-element.669) | copy-start | bytes 18436
  1210.4 26.6 %copy-start.285 = (f32[256]{0:T(256)S(1)}, f32[256]{0:T(256)}, u32[]{:S(2)}) copy-start(f32[256]{0:T(256)} %get-tuple-element.302) | copy-start | bytes 3076
  1210.4 27.3 %copy-start.284 = (f32[256]{0:T(256)S(1)}, f32[256]{0:T(256)}, u32[]{:S(2)}) copy-start(f32[256]{0:T(256)} %get-tuple-element.305) | copy-start | bytes 3076
  1210.5 27.9 %copy-start.174 = (f32[10,128]{1,0:T(8,128)S(1)}, f32[10,128]{1,0:T(8,128)}, u32[]{:S(2)}) copy-start(f32[10,128]{1,0:T(8,128)} %get-tuple-element.262) | copy-start | bytes 15364
  1210.5 28.6 %copy-start.173 = (f32[10,128]{1,0:T(8,128)S(1)}, f32[10,128]{1,0:T(8,128)}, u32[]{:S(2)}) copy-start(f32[10,128]{1,0:T(8,128)} %get-tuple-element.297) | copy-start | bytes 15364
  1210.5 29.3 %copy-start.242 = (f32[1000]{0:T(1024)S(1)}, f32[1000]{0:T(1024)}, u32[]{:S(2)}) copy-start(f32[1000]{0:T(1024)} %get-tuple-element.444) | copy-start | bytes 12004
  1255.3 26.2 %copy-start.178 = (f32[1536]{0:T(1024)S(1)}, f32[1536]{0:T(1024)}, u32[]{:S(2)}) copy-start(f32[1536]{0:T(1024)} %get-tuple-element.213) | copy-start | bytes 18436
  1255.3 26.8 %copy-start.177 = (f32[1536]{0:T(1024)S(1)}, f32[1536]{0:T(1024)}, u32[]{:S(2)}) copy-start(f32[1536]{0:T(1024)} %get-tuple-element.269) | copy-start | bytes 18436
  1255.3 26.8 %copy-start.150 = (f32[1536]{0:T(1024)S(1)}, f32[1536]{0:T(1024)}, u32[]{:S(2)}) copy-start(f32[1536]{0:T(1024)} %get-tuple-element.257) | copy-start | bytes 18436
  1255.3 27.4 %copy-start.149 = (f32[1536]{0:T(1024)S(1)}, f32[1536]{0:T(1024)}, u32[]{:S(2)}) copy-start(f32[1536]{0:T(1024)} %get-tuple-element.285) | copy-start | bytes 18436
  1255.4 33.3 %copy-start.172 = (f32[10,128]{1,0:T(8,128)S(1)}, f32[10,128]{1,0:T(8,128)}, u32[]{:S(2)}) copy-start(f32[10,128]{1,0:T(8,128)} %get-tuple-element.251) | copy-start | bytes 15364
  1255.4 33.9 %copy-start.171 = (f32[10,128]{1,0:T(8,128)S(1)}, f32[10,128]{1,0:T(8,128)}, u32[]{:S(2)}) copy-start(f32[10,128]{1,0:T(8,128)} %get-tuple-element.298) | copy-start | bytes 15364
  1317.6 25.8 %copy-start.176 = (f32[1536]{0:T(1024)S(1)}, f32[1536]{0:T(1024)}, u32[]{:S(2)}) copy-start(f32[1536]{0:T(1024)} %get-tuple-element.349) | copy-start | bytes 18436
  1399.9 51.1 %copy-start.80 = (f32[1536]{0:T(1024)S(1)}, f32[1536]{0:T(1024)}, u32[]{:S(2)}) copy-start(f32[1536]{0:T(1024)} %mul.3262) | copy-start | bytes 18436
  1399.9 51.1 %copy-start.93 = (f32[12,128]{1,0:T(8,128)S(1)}, f32[12,128]{1,0:T(8,128)}, u32[]{:S(2)}) copy-start(f32[12,128]{1,0:T(8,128)} %copy-done.92) | copy-start | bytes 18436
  1399.9 51.1 %copy-start.119 = (f32[1536]{0:T(1024)S(1)}, f32[1536]{0:T(1024)}, u32[]{:S(2)}) copy-start(f32[1536]{0:T(1024)} %copy-done.118) | copy-start | bytes 18436
  1399.9 51.1 %copy-start.185 = (f32[1536]{0:T(1024)S(1)}, f32[1536]{0:T(1024)}, u32[]{:S(2)}) copy-start(f32[1536]{0:T(1024)} %copy-done.184) | copy-start | bytes 18436
  1399.9 51.1 %copy-start.248 = (f32[1536]{0:T(1024)S(1)}, f32[1536]{0:T(1024)}, u32[]{:S(2)}) copy-start(f32[1536]{0:T(1024)} %copy-done.247) | copy-start | bytes 18436
  1550.7 259.1 %copy-start.45 = (f32[2,137,384]{2,0,1:T(2,128)S(1)}, f32[2,137,384]{2,0,1:T(2,128)}, u32[]{:S(2)}) copy-start(f32[2,137,384]{2,0,1:T(2,128)} %param.38) | copy-start | bytes 1262596
  1550.7 259.1 %copy-start.75 = (f32[2,137,384]{2,0,1:T(2,128)S(1)}, f32[2,137,384]{2,0,1:T(2,128)}, u32[]{:S(2)}) copy-start(f32[2,137,384]{2,0,1:T(2,128)} %param.40) | copy-start | bytes 1262596
  1550.7 259.1 %copy-start.76 = (f32[2,137,384]{2,0,1:T(2,128)S(1)}, f32[2,137,384]{2,0,1:T(2,128)}, u32[]{:S(2)}) copy-start(f32[2,137,384]{2,0,1:T(2,128)} %param.39) | copy-start | bytes 1262596
  1550.7 261.9 %copy-start.10 = (f32[2,64,3072]{2,1,0:T(8,128)S(1)}, f32[2,64,3072]{2,1,0:T(8,128)}, u32[]{:S(2)}) copy-start(f32[2,64,3072]{2,1,0:T(8,128)} %param.34) | copy-start | bytes 4718596
  (239 other events, 1561.8 us)
Sparse Core Ops, SparseCore 0:
  11.1 39.7 all-gather.6
  53.1 29.9 all-gather.8
  85.2 26.3 all-gather.12
  113.0 28.9 all-gather.10
  1550.9 258.9 all-reduce.95

commit v2 on v1

--- a/solution.py
+++ b/solution.py
@@ -45,231 +45,18 @@
     )
 
 
-def norm_stats(values, masks, counts):
-    sums_first = jnp.stack([jnp.sum(masks[0] * values[0], 0)])
-    sums_second = jnp.stack([jnp.sum(masks[0] * values[0] * values[0], 0)])
-    sums = lax.psum((sums_first, sums_second), ("dp", "shard"))
-    mean = sums[0][0] / counts[0]
-    scale = lax.rsqrt(sums[1][0] / counts[0] - mean * mean + EPS_NORM)
-    result = [(mean, scale)]
-    return result
-
-
-def norm_apply(value, mask, gain, shift, mean, scale):
-    return mask * (gain * ((value - mean) * scale) + shift)
-
-
-def norm_back(grads, values, masks, gains, stats, counts):
-    units = (values[0] - stats[0][0]) * stats[0][1]
-    inners = masks[0] * grads[0] * gains[0]
-    sums_first = jnp.stack([jnp.sum(inners, 0)])
-    sums_second = jnp.stack([jnp.sum(inners * units, 0)])
-    sums = lax.psum((sums_first, sums_second), ("dp", "shard"))
-    gain_grad = jnp.sum(masks[0] * grads[0] * units, 0)
-    shift_grad = jnp.sum(masks[0] * grads[0], 0)
-    back = (
-        masks[0] * stats[0][1] * (inners - sums[0][0] / counts[0] - units * sums[1][0] / counts[0])
-    )
-    result = [(back, gain_grad, shift_grad)]
-    return result
-
-
-def spread(first, taps):
-    image = jax.nn.silu(first).reshape(-1, S, S, first.shape[-1])
-    padded = jnp.pad(image, ((0, 0), (1, 1), (1, 1), (0, 0)))
-    total = jnp.zeros_like(image)
-    for offset in range(9):
-        total = (
-            total
-            + padded[:, offset // 3 : offset // 3 + S, offset % 3 : offset % 3 + S, :]
-            * taps[offset]
-        )
-    return total.reshape(first.shape)
-
-
-def pool(value, area):
-    return jnp.sum(value.reshape(area.shape[0], S * S, value.shape[-1]), 1) / area[:, None]
-
-
-def excite(second, se_part, excite_bias, squeeze_bias, area):
-    active = jax.nn.silu(second)
-    pooled = pool(active, area)
-    squeezed = jax.nn.silu(matmul_bt(pooled, se_part[:SE]) + squeeze_bias)
-    gate = jax.nn.sigmoid(matmul(squeezed, se_part[SE:]) + excite_bias)
-    shaped = active.reshape(area.shape[0], S * S, active.shape[-1])
-    return (shaped * gate[:, None, :]).reshape(second.shape)
-
-
-def unpack_gains(gains):
-    rows = gains.shape[0]
-    widths = []
-    for layer in range(L):
-        widths = widths + [E, E, E, E, E, C, C, SE]
-    widths = widths + [HEAD, HEAD, CLASSES]
-    parts = []
-    start = 0
-    for width in widths:
-        piece = width // rows
-        parts.append(gains[:, start : start + piece].reshape(-1))
-        start = start + piece
-    return parts
+def matmul_tb(left, right):
+    return lax.dot_general(
+        left,
+        right,
+        (((0,), (0,)), ((), ())),
+        precision=lax.Precision.HIGHEST,
+        preferred_element_type=jnp.float32,
+    )
 
 
 def pack_gains(vectors, rows):
     return jnp.concatenate([vector.reshape(rows, -1) for vector in vectors], 1)
-
-
-def block_forward(hiddens, mats, chans, gainsets, masks, area, counts):
-    width = mats[0].shape[1] // 2
-    hidden_lows = [h.astype(jnp.bfloat16) for h in hiddens]
-    pres = [jnp.dot(hidden_lows[0], mats[0][:, :width], preferred_element_type=jnp.float32)]
-    stats_one = norm_stats(pres, masks, counts)
-    firsts = norm_apply(
-        pres[0], masks[0], gainsets[0][0], gainsets[0][1], stats_one[0][0], stats_one[0][1]
-    )
-    mixeds = [spread(firsts, chans[0][:9].astype(jnp.float32))]
-    stats_two = norm_stats(mixeds, masks, counts)
-    seconds = norm_apply(
-        mixeds[0], masks[0], gainsets[0][2], gainsets[0][3], stats_two[0][0], stats_two[0][1]
-    )
-    scaleds = excite(
-        seconds, chans[0][9:].astype(jnp.float32), gainsets[0][4], gainsets[0][7], area
-    ).astype(jnp.bfloat16)
-    outs = [contract(scaleds, mats[0][:, width:], 1, 1)]
-    stats_three = norm_stats(outs, masks, counts)
-    fresh = [
-        hiddens[0]
-        + norm_apply(
-            outs[0], masks[0], gainsets[0][5], gainsets[0][6], stats_three[0][0], stats_three[0][1]
-        )
-    ]
-    kept = [
-        (
-            hidden_lows[0],
-            pres[0],
-            stats_one[0],
-            mixeds[0],
-            stats_two[0],
-            scaleds,
-            outs[0],
-            stats_three[0],
-        )
-    ]
-    return (fresh, kept)
-
-
-def block_backward(grad_hiddens, mats, chans, gainsets, kepts, masks, area, counts):
-    width = mats[0].shape[1] // 2
-    backs_three = norm_back(
-        grad_hiddens, [kepts[0][6]], masks, [gainsets[0][5]], [kepts[0][7]], counts
-    )
-    k = 0
-    hidden_low, pre, stats_one, mixed, stats_two, scaled, out, stats_three = kepts[k]
-    grad_out_low = backs_three[k][0].astype(jnp.bfloat16)
-    grad_project = contract(grad_out_low, scaled, 0, 0)
-    grad_scaled = jnp.dot(grad_out_low, mats[k][:, width:], preferred_element_type=jnp.float32)
-    second = norm_apply(mixed, masks[k], gainsets[k][2], gainsets[k][3], stats_two[0], stats_two[1])
-    excite_part = lambda value, se_part, bias_x, bias_r: excite(
-        value, se_part, bias_x, bias_r, area
-    )
-    unused, pull = jax.vjp(
-        excite_part, second, chans[k][9:].astype(jnp.float32), gainsets[k][4], gainsets[k][7]
-    )
-    grad_second, grad_se, grad_excite_bias, grad_squeeze_bias = pull(grad_scaled)
-    grad_seconds = [grad_second]
-    middle = [(grad_project, grad_se, grad_excite_bias, grad_squeeze_bias)]
-    backs_two = norm_back(
-        grad_seconds, [kepts[0][3]], masks, [gainsets[0][2]], [kepts[0][4]], counts
-    )
-    k = 0
-    pre = kepts[k][1]
-    stats_one = kepts[k][2]
-    first = norm_apply(pre, masks[k], gainsets[k][0], gainsets[k][1], stats_one[0], stats_one[1])
-    unused, pull = jax.vjp(spread, first, chans[k][:9].astype(jnp.float32))
-    grad_first, grad_taps = pull(backs_two[k][0])
-    grad_firsts = [grad_first]
-    taps_grads = [grad_taps]
-    backs_one = norm_back(
-        grad_firsts, [kepts[0][1]], masks, [gainsets[0][0]], [kepts[0][2]], counts
-    )
-    k = 0
-    grad_pre_low = backs_one[k][0].astype(jnp.bfloat16)
-    grad_expand = contract(kepts[k][0], grad_pre_low, 0, 0)
-    grad_below = grad_hiddens[k] + contract(grad_pre_low, mats[k][:, :width], 1, 1)
-    grad_project, grad_se, grad_excite_bias, grad_squeeze_bias = middle[k]
-    grad_mats = jnp.concatenate([grad_expand, grad_project], 1)
-    grad_chan = jnp.concatenate([taps_grads[k], grad_se], 0)
-    grad_gains = [
-        backs_one[k][1],
-        backs_one[k][2],
-        backs_two[k][1],
-        backs_two[k][2],
-        grad_excite_bias,
-        backs_three[k][1],
-        backs_three[k][2],
-        grad_squeeze_bias,
-    ]
-    result = [(grad_below, grad_mats, grad_chan, grad_gains)]
-    return result
-
-
-def run_forward(models, rows_list, masks, area, counts):
-    gainsets_all = [unpack_gains(m[4].astype(jnp.float32)) for m in models]
-    layers = models[0][0].shape[0]
-    hiddens = rows_list
-    kept_blocks = []
-    for layer in range(layers):
-        hiddens, kept = block_forward(
-            hiddens,
-            [m[0][layer] for m in models],
-            [m[1][layer] for m in models],
-            [g[8 * layer : 8 * layer + 8] for g in gainsets_all],
-            masks,
-            area,
-            counts,
-        )
-        kept_blocks.append(kept)
-    heads = [g[8 * layers : 8 * layers + 3] for g in gainsets_all]
-    hidden_lows = [h.astype(jnp.bfloat16) for h in hiddens]
-    feats = [jnp.dot(hidden_lows[0], models[0][2], preferred_element_type=jnp.float32)]
-    stats_head = norm_stats(feats, masks, counts)
-    normed = norm_apply(
-        feats[0], masks[0], heads[0][0], heads[0][1], stats_head[0][0], stats_head[0][1]
-    )
-    pooled_low = pool(jax.nn.silu(normed), area).astype(jnp.bfloat16)
-    logits_all = [
-        jnp.dot(pooled_low, models[0][3], preferred_element_type=jnp.float32) + heads[0][2]
-    ]
-    kept_heads = [(hidden_lows[0], feats[0], stats_head[0], pooled_low)]
-    return (logits_all, kept_blocks, kept_heads)
-
-
-def head_backward(grad_logits_all, model, kept_heads, masks, area, counts):
-    count_all = len(grad_logits_all)
-    layers = model[0].shape[0]
-    gains = unpack_gains(model[4].astype(jnp.float32))
-    head_gain, head_shift, class_bias = gains[8 * layers : 8 * layers + 3]
-    k = 0
-    hidden_low, feat, stats_head, pooled_low = kept_heads[k]
-    grad_low = grad_logits_all[k].astype(jnp.bfloat16)
-    grad_classes = contract(pooled_low, grad_low, 0, 0)
-    grad_class_bias = jnp.sum(grad_low.astype(jnp.float32), 0)
-    grad_pooled = contract(grad_low, model[3], 1, 1)
-    normed = norm_apply(feat, masks[k], head_gain, head_shift, stats_head[0], stats_head[1])
-    unused, pull = jax.vjp(lambda value: pool(jax.nn.silu(value), area), normed)
-    (grad_normed,) = pull(grad_pooled)
-    grad_normeds = [grad_normed]
-    partial_heads = [(grad_classes, grad_class_bias)]
-    backs = norm_back(
-        grad_normeds, [kept_heads[0][1]], masks, [head_gain] * count_all, [kept_heads[0][2]], counts
-    )
-    k = 0
-    grad_feat_low = backs[k][0].astype(jnp.bfloat16)
-    grad_head = contract(kept_heads[k][0], grad_feat_low, 0, 0)
-    grad_hidden = contract(grad_feat_low, model[2], 1, 1)
-    head_tail = [backs[k][1], backs[k][2], partial_heads[k][1]]
-    result = [(grad_hidden, grad_head, partial_heads[k][0], head_tail)]
-    return result
 
 
 IMGS = 5
@@ -283,6 +70,7 @@
 HC = HEAD // LANES
 GAP = 16
 TILE = 48
+TILE_BACK = 48
 OFFSETS = [S * (a - 1) + (c - 1) for a in range(3) for c in range(3)]
 MESH = pl.DeviceIdType.MESH
 F32 = jnp.float32
@@ -434,8 +222,6 @@
 
     def summer(m, kind, layer):
         near, far, sems, rows = sums[m][kind]
-        if kind == 0 and layer == 1:
-            pass
         return Sum(near, far, total_ref(m, kind, layer), sems, sizes, rows)
 
     def save(src, dst, index):
@@ -546,7 +332,7 @@
                     rows = slice(slot * ROWS, (slot + 1) * ROWS)
                     value = act_half(mask[rows, :] * (pre[m, c, rows, :] * scale + shift))
                     pre[m, c, rows, :] = value
-                    pool[slot : slot + 1, lanes(c)] = jnp.sum(value, 0, keepdims=True) / area[0:1, :]
+                    pool[b * 8 + i : b * 8 + i + 1, lanes(c)] = jnp.sum(value, 0, keepdims=True) / area[0:1, :]
 
         repeat(EC, body, hook)
 
@@ -559,9 +345,10 @@
         gate[...] = jax.nn.sigmoid(matmul(jax.nn.silu(units), excite[m, layer]) + gain_e[m, layer, 4:5, :])
 
         def body(c):
-            for i in range(SLOTS):
-                rows = slice(i * ROWS, (i + 1) * ROWS)
-                scaled[rows, lanes(c)] = (pre[m, c, rows, :] * gate[i : i + 1, lanes(c)]).astype(BF16)
+            for b in range(BATCHES):
+                for i in range(IMGS):
+                    rows = slice(b * HALF + i * ROWS, b * HALF + (i + 1) * ROWS)
+                    scaled[rows, lanes(c)] = (pre[m, c, rows, :] * gate[b * 8 + i : b * 8 + i + 1, lanes(c)]).astype(BF16)
 
         repeat(EC, body)
         stage = stages.at[m]
@@ -600,7 +387,7 @@
                     slot = b * IMGS + i
                     rows = slice(slot * ROWS, (slot + 1) * ROWS)
                     value = act_half(mask[rows, :] * (pre[m, c, rows, :] * scale + shift))
-                    pooled_h[m, slot : slot + 1, lanes(c)] = jnp.sum(value, 0, keepdims=True) / area[0:1, :]
+                    pooled_h[m, b * 8 + i : b * 8 + i + 1, lanes(c)] = jnp.sum(value, 0, keepdims=True) / area[0:1, :]
 
         repeat(HC, body, hook)
 
@@ -704,6 +491,354 @@
     )(*inputs)
 
 
+def backward_kernel(sizes, *refs):
+    (dpool_h, mask, edge_l, edge_r, area, wexp, headt, taps, squeeze, excite, gain_e, gain_c, gain_h,
+     pre_s, mixed_s, feat_s, out_s, low_s, pool_s, unit_s, gate_s, tot_e, tot_c, tot_h,
+     g_exp, g_taps, g_sq, g_ex, g_exb, g_sqb, g_head, back_e, back_c, back_h,
+     pre, mixed, grad, grad_hid, low_out, low_pre, pads_x, pads_g, slope, dgate, dpool, stages, load_sems) = refs[:47]
+    rest = list(refs[47:])
+    sums = []
+    for b in range(BATCHES):
+        group = []
+        for rows in (24, 24, 8, 24):
+            group.append((rest[0], rest[1], rest[2:6], rows))
+            rest = rest[6:]
+        sums.append(group)
+
+    greet(sizes)
+
+    def back_ref(b, kind, layer):
+        return (back_e.at[layer, b, 0], back_e.at[layer, b, 1], back_c.at[layer, b], back_h.at[b])[kind]
+
+    def summer(b, kind, layer):
+        near, far, sems, rows = sums[b][kind]
+        return Sum(near, far, back_ref(b, kind, layer), sems, sizes, rows)
+
+    def load(b, kind, layer):
+        rows = slice(b * HALF, (b + 1) * HALF)
+        if kind == 0:
+            return pltpu.make_async_copy(pre_s.at[layer, :, rows], pre.at[b], load_sems.at[b, 0])
+        if kind == 1:
+            return pltpu.make_async_copy(mixed_s.at[layer, :, rows], mixed.at[b], load_sems.at[b, 1])
+        return pltpu.make_async_copy(feat_s.at[:, rows], pre.at[b, 0:HC], load_sems.at[b, 0])
+
+    for b in range(BATCHES):
+        load(b, 2, 0).start()
+    for b in range(BATCHES):
+        load(b, 1, L - 1).start()
+    for slot in range(IMGS):
+        for pads in (pads_x, pads_g):
+            pads[slot, 0:GAP, :] = jnp.zeros((GAP, LANES), F32)
+            pads[slot, GAP + ROWS : 2 * GAP + ROWS, :] = jnp.zeros((GAP, LANES), F32)
+    dgate[...] = jnp.zeros(dgate.shape, F32)
+    stages[...] = jnp.zeros(stages.shape, F32)
+
+    def forward_total(kind, layer):
+        return (tot_e.at[layer, 0], tot_e.at[layer, 1], tot_c.at[layer], tot_h)[kind]
+
+    def moments(b, kind, layer, c):
+        tot = forward_total(kind, layer)
+        count = tot_e[0, 0, 48 + b : 49 + b, :]
+        mean = tot[pl.ds(4 * c + 2 * b, 1), :] / count
+        square = tot[pl.ds(4 * c + 2 * b + 1, 1), :] / count
+        return mean, lax.rsqrt(square - mean * mean + EPS_NORM)
+
+    def half_coefs(b, kind, layer, c, gain, shift):
+        mean, scale = moments(b, kind, layer, c)
+        scale = scale * gain
+        return 0.5 * scale, 0.5 * (shift - mean * scale)
+
+    def back_coefs(b, kind, layer, c, gain):
+        mean, scale = moments(b, kind, layer, c)
+        count = tot_e[0, 0, 48 + b : 49 + b, :]
+        back = back_ref(b, kind, layer)
+        plain = back[pl.ds(2 * c, 1), :]
+        cross = scale * (back[pl.ds(2 * c + 1, 1), :] - mean * plain)
+        first = scale * gain
+        third = -first * scale * cross / count
+        return first, -first * plain / count - mean * third, third
+
+    def fold(value):
+        return jnp.sum(value.reshape(value.shape[0] // 8, 8, LANES), 0)
+
+    def put(stage, c, first, second):
+        stage[pl.ds(2 * c, 1), :] = jnp.sum(first, 0, keepdims=True)
+        stage[pl.ds(2 * c + 1, 1), :] = jnp.sum(second, 0, keepdims=True)
+
+    def image(b, i):
+        return slice(i * ROWS, (i + 1) * ROWS), slice(b * HALF + i * ROWS, b * HALF + (i + 1) * ROWS)
+
+    def bend(half):
+        t = jnp.tanh(half)
+        return half + half * t, (0.5 + 0.5 * t) * (1.0 + half * (1.0 - t))
+
+    def head_first(b, hook=None):
+        stage = stages.at[b]
+
+        def body(c):
+            scale, shift = half_coefs(b, 3, 0, c, gain_h[0:1, lanes(c)], gain_h[1:2, lanes(c)])
+            first = jnp.zeros((8, LANES), F32)
+            second = jnp.zeros((8, LANES), F32)
+            for i in range(IMGS):
+                rows, full = image(b, i)
+                x = pre[b, c, rows, :]
+                half = mask[full, :] * (x * scale + shift)
+                value = mask[full, :] * dpool_h[b * 8 + i : b * 8 + i + 1, lanes(c)] * bend(half)[1]
+                grad[b, c, rows, :] = value
+                first = first + fold(value)
+                second = second + fold(value * x)
+            put(stage, c, first, second)
+
+        repeat(HC, body, hook)
+
+    def norm_back_rows(b, kind, layer, c, gain, source):
+        one, two, three = back_coefs(b, kind, layer, c, gain)
+        for i in range(IMGS):
+            rows, full = image(b, i)
+            value = mask[full, :] * (one * grad[b, c, rows, :] + two + three * source[b, c, rows, :])
+            low_pre[rows, lanes(c)] = value.astype(BF16)
+
+    def put_hidden_sums(b, layer):
+        stage = stages.at[b]
+        for half in range(2):
+            cols = slice(half * LANES, (half + 1) * LANES)
+            first = jnp.zeros((8, LANES), F32)
+            second = jnp.zeros((8, LANES), F32)
+            for i in range(IMGS):
+                full = image(b, i)[1]
+                value = grad_hid[full, cols]
+                first = first + fold(value)
+                second = second + fold(value * out_s[layer, full, cols])
+            put(stage, half, first, second)
+
+    def add(ref, index, value, b):
+        if b == 0:
+            ref[index] = value
+        else:
+            ref[index] = ref[index] + value
+
+    def head_second(b, hook=None):
+        mine = slice(b * HALF, (b + 1) * HALF)
+
+        def body(c):
+            for half in range(2):
+                norm_back_rows(b, 3, 0, 2 * c + half, gain_h[0:1, lanes(2 * c + half)], pre)
+            rows = pl.ds(pl.multiple_of(c * 256, 256), 256)
+            add(g_head, (rows, slice(None)), contract(low_pre[:, lanes(c, 256)], low_s[L, mine, :], 0, 0), b)
+
+        repeat(HEAD // 256, body, hook)
+        grad_hid[mine, :] = jnp.dot(low_pre[:, 0:HEAD], headt[...], preferred_element_type=F32)
+        put_hidden_sums(b, L - 1)
+
+    def block_gate(b, layer, hook=None):
+        mine = slice(b * HALF, (b + 1) * HALF)
+        eight = slice(b * 8, b * 8 + 8)
+        for half in range(2):
+            cols = slice(half * LANES, (half + 1) * LANES)
+            one, two, three = back_coefs(b, 2, layer, half, gain_c[layer, 0:1, cols])
+            for i in range(IMGS):
+                rows, full = image(b, i)
+                low_out[rows, cols] = (mask[full, :] * (one * grad_hid[full, cols] + two + three * out_s[layer, full, cols])).astype(BF16)
+
+        def body(c):
+            value = jnp.dot(low_out[...], wexp[layer, :, lanes(E // 256 + c, 256)], preferred_element_type=F32)
+            for part in range(2):
+                k = 2 * c + part
+                scale, shift = half_coefs(b, 1, layer, k, gain_e[layer, 2:3, lanes(k)], gain_e[layer, 3:4, lanes(k)])
+                for i in range(IMGS):
+                    rows, full = image(b, i)
+                    act = act_half(mask[full, :] * (mixed[b, k, rows, :] * scale + shift))
+                    piece = value[rows, part * LANES : (part + 1) * LANES]
+                    grad[b, k, rows, :] = piece
+                    dgate[i : i + 1, lanes(k)] = jnp.sum(fold(piece * act), 0, keepdims=True)
+                    low_pre[rows, lanes(k)] = (act * gate_s[layer, b * 8 + i : b * 8 + i + 1, lanes(k)]).astype(BF16)
+            add(g_exp, (layer, slice(None), lanes(E // 256 + c, 256)), contract(low_out[...], low_pre[:, lanes(c, 256)], 0, 0), b)
+
+        repeat(E // 256, body, hook)
+        gate = gate_s[layer, eight, :]
+        units = unit_s[layer, eight, :]
+        sig = jax.nn.sigmoid(units)
+        inner = dgate[...] * gate * (1.0 - gate)
+        add(g_exb, layer, jnp.broadcast_to(jnp.sum(inner, 0, keepdims=True), (8, E)), b)
+        add(g_ex, layer, matmul_tb(units * sig, inner), b)
+        outer = matmul_bt(inner, excite[layer]) * (sig * (1.0 + units * (1.0 - sig)))
+        add(g_sqb, layer, jnp.broadcast_to(jnp.sum(outer, 0, keepdims=True), (8, SE)), b)
+        add(g_sq, layer, matmul_tb(outer, pool_s[layer, eight, :]), b)
+        dpool[...] = matmul(outer, squeeze[layer])
+
+    def block_second(b, layer, hook=None):
+        stage = stages.at[b]
+
+        def body(c):
+            scale, shift = half_coefs(b, 1, layer, c, gain_e[layer, 2:3, lanes(c)], gain_e[layer, 3:4, lanes(c)])
+            first = jnp.zeros((8, LANES), F32)
+            second = jnp.zeros((8, LANES), F32)
+            for i in range(IMGS):
+                rows, full = image(b, i)
+                x = mixed[b, c, rows, :]
+                half = mask[full, :] * (x * scale + shift)
+                gate = gate_s[layer, b * 8 + i : b * 8 + i + 1, lanes(c)]
+                value = mask[full, :] * (grad[b, c, rows, :] * gate + dpool[i : i + 1, lanes(c)] / area[0:1, :]) * bend(half)[1]
+                grad[b, c, rows, :] = value
+                first = first + fold(value)
+                second = second + fold(value * x)
+            put(stage, c, first, second)
+
+        repeat(EC, body, hook)
+
+    def block_spread(b, layer, hook=None):
+        stage = stages.at[b]
+
+        def body(c):
+            scale, shift = half_coefs(b, 0, layer, c, gain_e[layer, 0:1, lanes(c)], gain_e[layer, 1:2, lanes(c)])
+            one, two, three = back_coefs(b, 1, layer, c, gain_e[layer, 2:3, lanes(c)])
+            tap = [taps[layer, k : k + 1, lanes(c)] for k in range(9)]
+            for i in range(IMGS):
+                rows, full = image(b, i)
+                act, der = bend(mask[full, :] * (pre[b, c, rows, :] * scale + shift))
+                pads_x[i, GAP : GAP + ROWS, :] = act
+                slope[rows, :] = mask[full, :] * der
+                pads_g[i, GAP : GAP + ROWS, :] = mask[full, :] * (one * grad[b, c, rows, :] + two + three * mixed[b, c, rows, :])
+            first = jnp.zeros((8, LANES), F32)
+            second = jnp.zeros((8, LANES), F32)
+            total = [jnp.zeros((8, LANES), F32) for k in range(9)]
+            for i in range(IMGS):
+                for t in range(ROWS // TILE_BACK):
+                    start = GAP + t * TILE_BACK
+                    rows = slice(i * ROWS + t * TILE_BACK, i * ROWS + (t + 1) * TILE_BACK)
+                    g = [pads_g[i, start - o : start - o + TILE_BACK, :] for o in OFFSETS]
+                    left, right = edge_l[0:TILE_BACK, :], edge_r[0:TILE_BACK, :]
+                    wide = (g[1] * tap[1] + g[4] * tap[4] + g[7] * tap[7]
+                            + right * (g[0] * tap[0] + g[3] * tap[3] + g[6] * tap[6])
+                            + left * (g[2] * tap[2] + g[5] * tap[5] + g[8] * tap[8]))
+                    value = wide * slope[rows, :]
+                    grad[b, c, rows, :] = value
+                    first = first + fold(value)
+                    second = second + fold(value * pre[b, c, rows, :])
+                    center = g[4]
+                    sides = (center * left, center, center * right)
+                    for k in range(9):
+                        o = OFFSETS[k]
+                        total[k] = total[k] + fold(sides[k % 3] * pads_x[i, start + o : start + o + TILE_BACK, :])
+            put(stage, c, first, second)
+            for k in range(9):
+                add(g_taps, (layer, slice(k, k + 1), lanes(c)), jnp.sum(total[k], 0, keepdims=True), b)
+
+        repeat(EC, body, hook)
+
+    def block_expand(b, layer, hook=None):
+        mine = slice(b * HALF, (b + 1) * HALF)
+
+        def body(c):
+            for part in range(2):
+                norm_back_rows(b, 0, layer, 2 * c + part, gain_e[layer, 0:1, lanes(2 * c + part)], pre)
+            add(g_exp, (layer, slice(None), lanes(c, 256)), contract(low_s[layer, mine, :], low_pre[:, lanes(c, 256)], 0, 0), b)
+
+        repeat(E // 256, body, hook)
+        if layer > 0:
+            grad_hid[mine, :] = grad_hid[mine, :] + contract(low_pre[...], wexp[layer, :, 0:E], 1, 1)
+            put_hidden_sums(b, layer - 1)
+
+    heads = [summer(b, 3, 0) for b in range(BATCHES)]
+    load(0, 2, 0).wait()
+    head_first(0)
+    heads[0].start(stages.at[0])
+    load(1, 2, 0).wait()
+    head_first(1, (5, heads[0].middle))
+    heads[1].start(stages.at[1])
+    thirds = [summer(b, 2, L - 1) for b in range(BATCHES)]
+    heads[0].finish()
+    head_second(0, (2, heads[1].middle))
+    load(0, 0, L - 1).start()
+    thirds[0].start(stages.at[0])
+    heads[1].finish()
+    head_second(1, (3, thirds[0].middle))
+    load(1, 0, L - 1).start()
+    thirds[1].start(stages.at[1])
+    for layer in reversed(range(L)):
+        twos = [summer(b, 1, layer) for b in range(BATCHES)]
+        ones = [summer(b, 0, layer) for b in range(BATCHES)]
+        thirds[0].finish()
+        load(0, 1, layer).wait()
+        block_gate(0, layer, (3, thirds[1].middle))
+        block_second(0, layer)
+        twos[0].start(stages.at[0])
+        thirds[1].finish()
+        load(1, 1, layer).wait()
+        block_gate(1, layer, (3, twos[0].middle))
+        block_second(1, layer)
+        twos[1].start(stages.at[1])
+        twos[0].finish()
+        load(0, 0, layer).wait()
+        block_spread(0, layer, (4, twos[1].middle))
+        if layer > 0:
+            load(0, 1, layer - 1).start()
+        ones[0].start(stages.at[0])
+        twos[1].finish()
+        load(1, 0, layer).wait()
+        block_spread(1, layer, (4, ones[0].middle))
+        if layer > 0:
+            load(1, 1, layer - 1).start()
+        ones[1].start(stages.at[1])
+        ones[0].finish()
+        block_expand(0, layer, (3, ones[1].middle))
+        if layer > 0:
+            load(0, 0, layer - 1).start()
+            thirds = [summer(b, 2, layer - 1) for b in range(BATCHES)]
+            thirds[0].start(stages.at[0])
+        ones[1].finish()
+        block_expand(1, layer, None if layer == 0 else (3, thirds[0].middle))
+        if layer > 0:
+            load(1, 0, layer - 1).start()
+            thirds[1].start(stages.at[1])
+
+
+def run_backward_all(sizes, inputs):
+    sds = jax.ShapeDtypeStruct
+    vm = pl.BlockSpec(memory_space=pltpu.VMEM)
+    hbm = pl.BlockSpec(memory_space=pl.ANY)
+    outs = [
+        sds((L, C, 2 * E), F32),
+        sds((L, 9, E), F32),
+        sds((L, SE, E), F32),
+        sds((L, SE, E), F32),
+        sds((L, 8, E), F32),
+        sds((L, 8, SE), F32),
+        sds((HEAD, C), F32),
+        sds((L, BATCHES, 2, 24, LANES), F32),
+        sds((L, BATCHES, 8, LANES), F32),
+        sds((BATCHES, 24, LANES), F32),
+    ]
+    scratch = [
+        pltpu.VMEM((BATCHES, EC, HALF, LANES), F32),
+        pltpu.VMEM((BATCHES, EC, HALF, LANES), F32),
+        pltpu.VMEM((BATCHES, EC, HALF, LANES), F32),
+        pltpu.VMEM((FULL, C), F32),
+        pltpu.VMEM((HALF, C), BF16),
+        pltpu.VMEM((HALF, E), BF16),
+        pltpu.VMEM((IMGS, ROWS + 2 * GAP, LANES), F32),
+        pltpu.VMEM((IMGS, ROWS + 2 * GAP, LANES), F32),
+        pltpu.VMEM((HALF, LANES), F32),
+        pltpu.VMEM((8, E), F32),
+        pltpu.VMEM((8, E), F32),
+        pltpu.VMEM((BATCHES, 24, LANES), F32),
+        pltpu.SemaphoreType.DMA((BATCHES, 2)),
+    ]
+    for b in range(BATCHES):
+        for rows in (24, 24, 8, 24):
+            scratch = scratch + sum_scratch(sizes, rows)
+    specs = [vm] * 13 + [hbm] * 3 + [vm] * 8
+    return pl.pallas_call(
+        functools.partial(backward_kernel, sizes),
+        out_shape=outs,
+        in_specs=specs,
+        out_specs=[vm] * len(outs),
+        scratch_shapes=scratch,
+        compiler_params=pltpu.CompilerParams(collective_id=2, has_side_effects=True, vmem_limit_bytes=63 * 2**20),
+        name="backward",
+    )(*inputs)
+
+
 def objective(logits, target, onehot, coef):
     logp = jax.nn.log_softmax(logits)
     per = -jnp.sum(onehot * logp, 1) + jnp.sum(jnp.exp(target) * (target - logp), 1)
@@ -779,182 +914,126 @@
     gain_v,
     gain_e,
 ):
-    full = (
-        lax.all_gather(expand_w.astype(jnp.bfloat16), "shard", axis=1, tiled=True),
-        lax.all_gather(chan_w.astype(jnp.bfloat16), "shard", axis=2, tiled=True),
-        lax.all_gather(head_w.astype(jnp.bfloat16), "shard", axis=1, tiled=True),
-        lax.all_gather(class_w.astype(jnp.bfloat16), "shard", axis=0, tiled=True),
-        lax.all_gather(gain_w.astype(jnp.bfloat16), "shard", axis=0, tiled=True),
-        lax.all_gather(expand_e.astype(jnp.bfloat16), "shard", axis=1, tiled=True),
-        lax.all_gather(chan_e.astype(jnp.bfloat16), "shard", axis=2, tiled=True),
-        lax.all_gather(head_e.astype(jnp.bfloat16), "shard", axis=1, tiled=True),
-        lax.all_gather(class_e.astype(jnp.bfloat16), "shard", axis=0, tiled=True),
-        lax.all_gather(gain_e.astype(jnp.bfloat16), "shard", axis=0, tiled=True),
-    )
-    model = full[:5]
-    shadow = full[5:]
-    batches = images.shape[0]
-    slots = images.shape[1]
+    sizes = (lax.axis_size("dp"), lax.axis_size("shard"))
+    n_sh = sizes[1]
+    weights = (expand_w, chan_w, head_w, class_w, gain_w)
+    firsts = (expand_m, chan_m, head_m, class_m, gain_m)
+    seconds = (expand_v, chan_v, head_v, class_v, gain_v)
+    averaged = (expand_e, chan_e, head_e, class_e, gain_e)
+    axes = (1, 2, 1, 0, 0)
+    both = [
+        jnp.stack(
+            [
+                lax.all_gather(item.astype(BF16), "shard", axis=axes[k], tiled=True)
+                for item in (weights[k], averaged[k])
+            ]
+        )
+        for k in range(5)
+    ]
     code = bucket[0]
     side = jnp.where(code == 0, 7, jnp.where(code == 1, 10, 12))
     spot = jnp.arange(S * S)
-    inside = ((spot // S < side) & (spot % S < side)).astype(jnp.float32)
-    area_value = (side * side).astype(jnp.float32)
-    area = jnp.full((slots,), area_value)
-    valid = (jnp.arange(slots)[None, :] < counts).astype(jnp.float32)
-    weighted = valid * balance.astype(jnp.float32)
-    pixels, weight_sums = lax.psum(
-        (jnp.sum(valid, 1) * area_value, jnp.sum(weighted, 1)), ("dp", "shard")
-    )
-    total_weight = jnp.sum(weight_sums)
-    layers = model[0].shape[0]
-    rows_all = [
-        images[index].astype(jnp.float32).reshape(-1, images.shape[-1]) for index in range(batches)
-    ]
-    masks_all = [
-        (valid[index][:, None] * inside[None, :]).reshape(-1, 1) for index in range(batches)
-    ]
-    counts_all = [pixels[index] for index in range(batches)]
-    backward_groups = [[index] for index in range(batches)]
-    sizes = (lax.axis_size("dp"), lax.axis_size("shard"))
-    both = [jnp.stack([model[item], shadow[item]]) for item in range(5)]
-    spot_l = (spot % S > 0).astype(F32)[:, None]
-    spot_r = (spot % S < S - 1).astype(F32)[:, None]
-    spread_l = jnp.broadcast_to(spot_l, (S * S, LANES))
-    spread_r = jnp.broadcast_to(spot_r, (S * S, LANES))
-    mask_all = jnp.broadcast_to(jnp.concatenate(masks_all, 0), (FULL, LANES))
-    own = jnp.concatenate([jnp.sum(valid, 1) * area_value, jnp.sum(weighted, 1), jnp.zeros((4,), F32)])
+    inside = ((spot // S < side) & (spot % S < side)).astype(F32)
+    area_value = (side * side).astype(F32)
+    valid = (jnp.arange(IMGS)[None, :] < counts).astype(F32)
+    weighted = valid * balance.astype(F32)
+    mask_all = jnp.broadcast_to(
+        (valid[:, :, None] * inside[None, None, :]).reshape(FULL, 1), (FULL, LANES)
+    )
+    spread_l = jnp.broadcast_to((spot % S > 0).astype(F32)[:, None], (ROWS, LANES))
+    spread_r = jnp.broadcast_to((spot % S < S - 1).astype(F32)[:, None], (ROWS, LANES))
+    own = jnp.concatenate(
+        [jnp.sum(valid, 1) * area_value, jnp.sum(weighted, 1), jnp.zeros((4,), F32)]
+    )
+    area = jnp.full((1, LANES), area_value)
     chan_f = both[1].astype(F32)
     gains_f = both[4].astype(F32)
-    n_sh = sizes[1]
     block_width = gains_f.shape[2] - 2 * (HEAD // n_sh) - CLASSES // n_sh
     blocks = gains_f[:, :, :block_width].reshape(2, n_sh, L, -1)
     wide = 5 * E // n_sh
-    vec_e = blocks[..., :wide].reshape(2, n_sh, L, 5, E // n_sh).transpose(0, 2, 3, 1, 4).reshape(2, L, 5, E)
-    vec_c = blocks[..., wide : wide + 2 * C // n_sh].reshape(2, n_sh, L, 2, C // n_sh).transpose(0, 2, 3, 1, 4).reshape(2, L, 2, C)
+    vec_e = (
+        blocks[..., :wide].reshape(2, n_sh, L, 5, E // n_sh).transpose(0, 2, 3, 1, 4)
+    ).reshape(2, L, 5, E)
+    vec_c = (
+        blocks[..., wide : wide + 2 * C // n_sh]
+        .reshape(2, n_sh, L, 2, C // n_sh)
+        .transpose(0, 2, 3, 1, 4)
+    ).reshape(2, L, 2, C)
     vec_s = blocks[..., wide + 2 * C // n_sh :].transpose(0, 2, 1, 3).reshape(2, L, 1, SE)
     heads_f = gains_f[:, :, block_width : block_width + 2 * HEAD // n_sh]
     vec_h = heads_f.reshape(2, n_sh, 2, HEAD // n_sh).transpose(0, 2, 1, 3).reshape(2, 2, HEAD)
     class_bias = gains_f[:, :, block_width + 2 * HEAD // n_sh :].reshape(2, CLASSES)
-    inputs = [
-        images.reshape(FULL, C), mask_all, spread_l, spread_r, jnp.full((1, LANES), area_value),
-        jnp.broadcast_to(own[:, None], (8, LANES)), both[0], both[2].transpose(0, 2, 1),
-        chan_f[:, :, :9], chan_f[:, :, 9 : 9 + SE], chan_f[:, :, 9 + SE :], vec_e, vec_c, vec_h, vec_s,
+    headt = both[2].transpose(0, 2, 1)
+    taps, squeeze, excite = chan_f[:, :, :9], chan_f[:, :, 9 : 9 + SE], chan_f[:, :, 9 + SE :]
+    saved = run_forward_all(
+        sizes,
+        [
+            images.reshape(FULL, C), mask_all, spread_l, spread_r, area,
+            jnp.broadcast_to(own[:, None], (8, LANES)), both[0], headt,
+            taps, squeeze, excite, vec_e, vec_c, vec_h, vec_s,
+        ],
+    )
+    pooled_h, kept = saved[11], saved[:11]
+    tot_e, tot_c, tot_h = kept[8:11]
+    total_weight = tot_e[0, 0, 50, 0] + tot_e[0, 0, 51, 0]
+    pooled_low = pooled_h.reshape(2, BATCHES, 8, HEAD)[:, :, :IMGS].reshape(2, SLOTS, HEAD).astype(BF16)
+    logits = [
+        jnp.dot(pooled_low[m], both[3][m], preferred_element_type=F32) + class_bias[m]
+        for m in range(2)
     ]
-    (pre_s, mixed_s, feat_s, out_s, low_s, pool_s, unit_s, gate_s, tot_e, tot_c, tot_h, pooled_h) = run_forward_all(sizes, inputs)
-    logits = [jnp.dot(pooled_h[m, :SLOTS].astype(BF16), both[3][m], preferred_element_type=F32) + class_bias[m] for m in range(2)]
-    main_logits = [logits[0][b * IMGS : (b + 1) * IMGS] for b in range(2)]
-    targets = [jax.nn.log_softmax(logits[1][b * IMGS : (b + 1) * IMGS]) for b in range(2)]
-
-    def plain(value, b):
-        return value[:, b * HALF : (b + 1) * HALF].transpose(1, 0, 2).reshape(HALF, -1)
-
-    def stats(tot, b, chunks):
-        pairs = tot[: 4 * chunks].reshape(chunks, 2, 2, LANES)[:, b]
-        mean = pairs[:, 0].reshape(-1) / counts_all[b]
-        return (mean, lax.rsqrt(pairs[:, 1].reshape(-1) / counts_all[b] - mean * mean + EPS_NORM))
-
-    main_blocks = []
-    main_heads = []
-    for b in range(2):
-        rows = slice(b * HALF, (b + 1) * HALF)
-        kept = []
-        for layer in range(layers):
-            mixed = plain(mixed_s[layer], b)
-            st = stats(tot_e[layer, 1], b, EC)
-            second = norm_apply(mixed, masks_all[b], vec_e[0, layer, 2], vec_e[0, layer, 3], st[0], st[1])
-            act = jax.nn.silu(second).reshape(IMGS, ROWS, E) * gate_s[layer, b * IMGS : (b + 1) * IMGS][:, None, :]
-            kept.append((low_s[layer, rows], plain(pre_s[layer], b), stats(tot_e[layer, 0], b, EC), mixed, st,
-                         act.reshape(HALF, E).astype(BF16), out_s[layer, rows], stats(tot_c[layer], b, 2)))
-        main_blocks.append(kept)
-        main_heads.append((low_s[layers, rows], plain(feat_s, b), stats(tot_h, b, HC), pooled_h[0, b * IMGS : (b + 1) * IMGS].astype(BF16)))
-    grad_mats = jnp.zeros(model[0].shape, jnp.float32)
-    grad_chan = jnp.zeros(model[1].shape, jnp.float32)
-    grad_head = jnp.zeros(model[2].shape, jnp.float32)
-    grad_class = jnp.zeros(model[3].shape, jnp.float32)
-    grad_gain = jnp.zeros(model[4].shape, jnp.float32)
-    loss = jnp.float32(0.0)
-    gain_list = unpack_gains(model[4].astype(jnp.float32))
-    for group in backward_groups:
-        grad_logits_all = []
-        for index in group:
-            onehot = (
-                labels[index][:, None] == jnp.arange(main_logits[index].shape[1])[None, :]
-            ).astype(jnp.float32)
-            coef = weighted[index] / total_weight
-            target = targets[index]
-            part, pull = jax.vjp(
-                lambda value: objective(value, target, onehot, coef), main_logits[index]
-            )
-            (grad_logits,) = pull(jnp.float32(1.0))
-            loss = loss + part
-            grad_logits_all.append(grad_logits)
-        masks = [masks_all[index] for index in group]
-        group_counts = [counts_all[index] for index in group]
-        head_parts = head_backward(
-            grad_logits_all,
-            model,
-            [main_heads[index] for index in group],
-            masks,
-            area,
-            group_counts,
-        )
-        grad_hiddens = [item[0] for item in head_parts]
-        mats_parts = [[None] * layers for index in group]
-        chan_parts = [[None] * layers for index in group]
-        gain_parts = [[None] * layers for index in group]
-        for layer in reversed(range(layers)):
-            size = len(group)
-            backs = block_backward(
-                grad_hiddens,
-                [model[0][layer]] * size,
-                [model[1][layer]] * size,
-                [gain_list[8 * layer : 8 * layer + 8]] * size,
-                [main_blocks[index][layer] for index in group],
-                masks,
-                area,
-                group_counts,
-            )
-            grad_hiddens = [item[0] for item in backs]
-            place = 0
-            mats_parts[place][layer] = backs[place][1]
-            chan_parts[place][layer] = backs[place][2]
-            gain_parts[place][layer] = backs[place][3]
-        place = 0
-        grad_mats = grad_mats + jnp.stack(mats_parts[place])
-        grad_chan = grad_chan + jnp.stack(chan_parts[place])
-        grad_head = grad_head + head_parts[place][1]
-        grad_class = grad_class + head_parts[place][2]
-        vectors = []
-        for layer in range(layers):
-            vectors = vectors + gain_parts[place][layer]
-        vectors = vectors + head_parts[place][3]
-        grad_gain = grad_gain + pack_gains(vectors, grad_gain.shape[0])
-    shards = lax.axis_size("shard")
-    loss_spread = jnp.full((shards,), loss)
+    onehot = (labels.reshape(SLOTS, 1) == jnp.arange(CLASSES)[None, :]).astype(F32)
+    coef = weighted.reshape(SLOTS) / total_weight
+    target = jax.nn.log_softmax(logits[1])
+    loss, pull = jax.vjp(lambda value: objective(value, target, onehot, coef), logits[0])
+    grad_low = pull(jnp.float32(1.0))[0].astype(BF16)
+    grad_class = contract(pooled_low[0], grad_low, 0, 0)
+    grad_class_bias = jnp.sum(grad_low.astype(F32), 0)
+    grad_pooled = contract(grad_low, both[3][0], 1, 1) / area_value
+    dpool_h = jnp.pad(grad_pooled.reshape(BATCHES, IMGS, HEAD), ((0, 0), (0, 3), (0, 0))).reshape(16, HEAD)
+    (g_exp, g_taps, g_sq, g_ex, g_exb, g_sqb, g_head, back_e, back_c, back_h) = run_backward_all(
+        sizes,
+        [
+            dpool_h, mask_all, spread_l, spread_r, area, both[0][0], headt[0],
+            taps[0], squeeze[0], excite[0], vec_e[0], vec_c[0], vec_h[0], *kept,
+        ],
+    )
+    g_chan = jnp.concatenate([g_taps, g_sq, g_ex], 1)
     summed = lax.psum(
-        (loss_spread, grad_mats, grad_chan, grad_head, grad_class, grad_gain), ("dp", "shard")
+        (loss, g_exp, g_chan, g_head, grad_class, g_exb[:, 0], g_sqb[:, 0], grad_class_bias),
+        ("dp", "shard"),
     )
     place = lax.axis_index("shard")
+
+    def norm_grads(tot, back, chunks):
+        count = tot_e[0, 0, 48 : 48 + BATCHES, :1]
+        forth = tot[: 4 * chunks].reshape(chunks, BATCHES, 2, LANES).transpose(1, 2, 0, 3).reshape(BATCHES, 2, -1)
+        mean = forth[:, 0] / count
+        scale = lax.rsqrt(forth[:, 1] / count - mean * mean + EPS_NORM)
+        pairs = back[:, : 2 * chunks].reshape(BATCHES, chunks, 2, LANES).transpose(0, 2, 1, 3).reshape(BATCHES, 2, -1)
+        cross = scale * (pairs[:, 1] - mean * pairs[:, 0])
+        return [jnp.sum(cross, 0), jnp.sum(pairs[:, 0], 0)]
+
+    vectors = []
+    for layer in range(L):
+        vectors = vectors + norm_grads(tot_e[layer, 0], back_e[layer, :, 0], EC)
+        vectors = vectors + norm_grads(tot_e[layer, 1], back_e[layer, :, 1], EC)
+        vectors = vectors + [summed[5][layer]]
+        vectors = vectors + norm_grads(tot_c[layer], back_c[layer], 2)
+        vectors = vectors + [summed[6][layer]]
+    vectors = vectors + norm_grads(tot_h, back_h, HC) + [summed[7]]
     owned = (
-        summed[0][0:1],
-        own_slice(summed[1], 1, shards, place),
-        own_slice(summed[2], 2, shards, place),
-        own_slice(summed[3], 1, shards, place),
-        own_slice(summed[4], 0, shards, place),
-        own_slice(summed[5], 0, shards, place),
-    )
-    total_loss = owned[0][0]
-    power = step[0].astype(jnp.float32)
+        own_slice(summed[1], 1, n_sh, place),
+        own_slice(summed[2], 2, n_sh, place),
+        own_slice(summed[3], 0, n_sh, place).T,
+        own_slice(summed[4], 0, n_sh, place),
+        own_slice(pack_gains(vectors, n_sh), 0, n_sh, place),
+    )
+    total_loss = summed[0]
+    power = step[0].astype(F32)
     first_fix = 1.0 - jnp.power(jnp.float32(BETA_ONE), power)
     second_fix = 1.0 - jnp.power(jnp.float32(BETA_TWO), power)
-    weights = (expand_w, chan_w, head_w, class_w, gain_w)
-    firsts = (expand_m, chan_m, head_m, class_m, gain_m)
-    seconds = (expand_v, chan_v, head_v, class_v, gain_v)
-    averaged = (expand_e, chan_e, head_e, class_e, gain_e)
     states = [
-        adapt(firsts[item], seconds[item], owned[item + 1], first_fix, second_fix)
-        for item in range(5)
+        adapt(firsts[item], seconds[item], owned[item], first_fix, second_fix) for item in range(5)
     ]
     updates = [states[item][2] + DECAY * weights[item] for item in range(4)]
     local_weight_sq = jnp.concatenate(
@@ -975,8 +1054,8 @@
     )
     weight_sq, update_sq = lax.psum((local_weight_sq, local_update_sq), "shard")
     ratio = jnp.sqrt(weight_sq) / jnp.sqrt(update_sq)
-    count_mats = 2 * layers
-    count_chan = 3 * layers
+    count_mats = 2 * L
+    count_chan = 3 * L
     factors = [
         mats_factor(ratio[:count_mats], expand_w),
         chan_factor(ratio[count_mats : count_mats + count_chan], chan_w),

time: 1870 us -> 708 us (0.38)
  other arithmetic: 515 us -> 57.2 us
  local copies, waits for them, and re-layouts: 451 us -> 39.5 us
  blocking collectives: 392 us -> 104 us
  Pallas kernels: 129 us -> 267 us
  matrix products: 96.6 us -> 8.54 us
  waiting for transfers between devices: 256 us -> 206 us
    psum x8 -> x1, blocking collectives: 324 us -> 41.7 us  [per_device(): lax.psum((loss, g_exp, g_chan, g_head, grad_class, g_exb[:, 0], g_sqb[:,...]
    reduce_sum x22 -> x13, other arithmetic: 264 us -> 2.34 us  [the longest x1 1.42 us: per_device(): jnp.sum(valid, 1) * area_value]
    reshape x28 -> x27, local copies, waits for them, and re-layouts: 160 us -> 4.75 us  [the longest x2 2.34 us: per_device(): vec_e = blocks[..., :wide].reshape(2, n_sh, L, 5, E // n_sh).transpose(0,...]
    transpose x27 -> x2, local copies, waits for them, and re-layouts: 143 us -> 0.62 us  [the longest x1 0.61 us: per_device(): vec_c = blocks[..., wide:wide + 2 * C // n_sh].reshape(2, n_sh, L, 2, C /...]
    pallas_call x0 -> x1, Pallas kernels: none -> 134 us  [run_backward_all(): pl.pallas_call(functools.partial(backward_kernel, sizes), out_shape=outs,...]
    mul x5 -> x1, other arithmetic: 80 us -> 0.75 us  [per_device(): valid[:, :, None] * inside[None, None, :]]
    dot_general x18 -> x2, matrix products: 62.7 us -> 3.93 us  [contract(): lax.dot_general(left, right, (((left_dim,), (right_dim,)), ((), ())), pre...]
    psum x1, waiting for transfers between devices: 256 us -> 206 us  [per_device(): lax.psum((loss, g_exp, g_chan, g_head, grad_class, g_exb[:, 0], g_sqb[:,...]
  transfers between devices with their start and end apart: 5 -> 5, of which waited for: 1 -> 1; matrix products, arithmetic and copies ran while one was open for 10% -> 9% of each run, Pallas kernels for 7% -> 19%
where the time goes in v2:
time: 708 us; the launch traced here: 702 us
  Pallas kernels  267 us (38%)
  waiting for transfers between devices  206 us (29%)
  blocking collectives  104 us (15%)
  other arithmetic  57.2 us (8%)
  local copies, waits for them, and re-layouts  39.5 us (6%)
  between operations  19.3 us (3%)
  matrix products  8.54 us (1%)
    psum x1, waiting for transfers between devices, per_device(): lax.psum((loss, g_exp, g_chan, g_head, grad_class, g_exb[:, 0], g_sqb[:,...  206 us
    pallas_call x1, Pallas kernels, run_backward_all(): pl.pallas_call(functools.partial(backward_kernel, sizes), out_shape=outs,...  134 us
    pallas_call x1, Pallas kernels, run_forward_all(): pl.pallas_call(functools.partial(forward_kernel, sizes), out_shape=[o[0]...  133 us
    all_gather x6, blocking collectives, per_device(): lax.all_gather(item.astype(BF16), 'shard', axis=axes[k], tiled=True)  56.2 us
    psum x1, blocking collectives, per_device(): lax.psum((loss, g_exp, g_chan, g_head, grad_class, g_exb[:, 0], g_sqb[:,...  41.7 us
  transfers between devices with their start and end apart: 5, of which 1 were waited for; matrix products, arithmetic and copies ran while one was open for 9% of the time, Pallas kernels for 19%

profile of v2, /device:TPU:0, one launch (start us, length us, event | category | flops | bytes accessed | tf_op | source)
XLA Modules:
  0.0 701.7 jit_solution(10703288440899230389)
XLA Ops:
  7.2 2.5 convert_element_type.96
  9.8 1.0 multiply_reduce_fusion.1
  11.4 1.0 convert_element_type.106
  12.4 1.8 multiply_reduce_fusion.3
  16.2 6.2 all-gather.1
  22.5 6.4 all-gather
  30.7 14.4 %all_gather.35 = bf16[2,137,1536]{2,1,0:T(8,128)(2,1)S(1)} all-gather(bf16[2,137,384]{2,1,0:T(8,128)(2,1)S(1)} %copy.393), channel_id=1, replica_groups=mesh['dp'=8,'shard'=4] {'shard'}, dimensions={2}, use_global_device_ids=true | all-gather | bytes 1052160 | tf_op jit(solution)/shard_map/all_gather | solution.py:927
  45.1 0.9 multiply_reduce_fusion.5
  46.1 9.3 %all_gather.34 = bf16[2,137,1536]{2,1,0:T(8,128)(2,1)S(1)} all-gather(bf16[2,137,384]{2,1,0:T(8,128)(2,1)S(1)} %copy.392), channel_id=1, replica_groups=mesh['dp'=8,'shard'=4] {'shard'}, dimensions={2}, use_global_device_ids=true | all-gather | bytes 1052160 | tf_op jit(solution)/shard_map/all_gather | solution.py:927
  56.0 1.4 convert_bitcast_fusion
  60.9 1.3 copy.391
  62.3 1.0 reshape.494.refs_0_
  63.3 0.8 fusion.42
  64.1 0.7 broadcast_multiply_fusion
  65.5 1.4 fusion.45
  67.0 11.9 %all_gather.33 = bf16[256,1280]{0,1:T(8,128)(2,1)S(1)} all-gather(bf16[256,320]{0,1:T(8,128)(2,1)S(1)} %convert_element_type.98), channel_id=1, replica_groups=mesh['dp'=8,'shard'=4] {'shard'}, dimensions={1}, use_global_device_ids=true | all-gather | bytes 819200 | tf_op jit(solution)/shard_map/all_gather | solution.py:927
  79.5 8.0 %all_gather.32 = bf16[256,1280]{0,1:T(8,128)(2,1)S(1)} all-gather(bf16[256,320]{0,1:T(8,128)(2,1)S(1)} %get-tuple-element.299), channel_id=1, replica_groups=mesh['dp'=8,'shard'=4] {'shard'}, dimensions={1}, use_global_device_ids=true | all-gather | bytes 819200 | tf_op jit(solution)/shard_map/all_gather | solution.py:927
  87.5 1.6 reshape.554.refs_11_
  89.2 1.4 reshape.499.refs_12_
  90.6 0.7 reshape.501.refs_13_
  91.3 0.7 copy.397
  92.7 1.3 eq.29
  94.0 0.8 add.216
  94.7 1.5 copy.457
  96.3 1.5 reshape.555.refs_10_
  97.8 0.7 copy.402
  99.2 0.7 copy.403
  101.4 0.8 pad_maximum_fusion.7
  102.1 0.8 maximum_convert_fusion.1.refs_8_
  103.2 0.9 slice_bitcast_fusion.refs_6_
  104.1 2.0 fusion.53
  106.2 6.1 pad_maximum_fusion.refs_6_
  112.2 1.1 broadcast_in_dim.136.refs_1_
  113.4 0.7 broadcast_in_dim.137.refs_2_
  114.1 0.7 broadcast_in_dim.138.refs_3_
  116.0 132.7 %forward.1 = (f32[2,12,1440,128]{3,2,1,0:T(8,128)}, f32[2,12,1440,128]{3,2,1,0:T(8,128)}, f32[10,1440,128]{2,1,0:T(8,128)}, f32[2,1440,256]{2,1,0:T(8,128)}, bf1...) custom-call(bf16[1440,256]{1,0:T(8,128)(2,1)} %reshape.494.refs_0_, ...), custom_call_target="tpu_custom_call" | custom-call | tf_op jit(solution)/shard_map/forward/pallas_call | solution.py:483
  248.7 0.9 convert_bitcast_fusion.3
  249.7 1.3 fusion.55
  252.4 2.3 fusion.68
  255.0 2.3 fusion.67
  257.9 3.1 fusion.69
  261.1 0.8 convolution_divide_fusion
  262.5 134.0 %backward.1 = (f32[2,256,3072]{2,1,0:T(8,128)}, f32[2,9,1536]{2,1,0:T(8,128)}, f32[2,64,1536]{2,1,0:T(8,128)}, f32[2,64,1536]{2,1,0:T(8,128)}, f32[2,8,1536]{2,1...) custom-call(f32[16,1280]{1,0:T(8,128)} %pad_bitcast_fusion.refs_0_, ...), custom_call_target="tpu_custom_call" | custom-call | tf_op jit(solution)/shard_map/backward/pallas_call | solution.py:831
  396.6 2.8 pad_maximum_fusion.1
  400.9 1.4 pad_maximum_fusion.8
  402.4 0.9 slice.386
  403.4 0.7 slice.395
  404.8 41.7 %all-reduce.1 = (f32[]{:T(128)}, f32[2,1536]{1,0:T(2,128)S(1)}, f32[2,64]{1,0:T(2,128)S(1)}, f32[4,250]{1,0:T(4,128)S(1)}) all-reduce(f32[]{:T(128)} %multiply_reduce_fusion.9, f32[2,1536]{1,0:T(2,128)S(1)} %bitcast.399, f32[2,64]{1,0:T(2,128)S(1)} %bitcast.414, ...), channel_id=1, replica_groups=mesh['dp'=8,'shard'=4] {'dp','shard'}, use_global_device_ids=true, to_apply=%region_9.10 | all-reduce | flops 4201 | bytes 33608 | tf_op jit(solution)/shard_map/psum | solution.py:1001
  449.0 205.9 %all-reduce.6.cloned.1.call-done = (f32[2,256,3072]{2,1,0:T(8,128)}, f32[1280,1000]{1,0:T(8,128)}, f32[1280,256]{1,0:T(8,128)}, f32[2,137,1536]{2,1,0:T(8,128)}) async-done(((f32[2,256,3072]{2,1,0:T(8,128)}, f32[1280,1000]{1,0:T(8,128)}, f32[1280,256]{1,0:T(8,128)}, f32[2,137,1536]{2,1,0:T(8,128)}), (f32[2,256,3072]{2,1,0:T(8,128)}, f32[1280,1000]{1,0:T(8,128)}, f32[1280,256]{1,0:T(8,128)}, ...) | async-done | bytes 14405648 | tf_op jit(solution)/shard_map/psum | solution.py:1001
  654.9 2.4 multiply_reduce_fusion.4
  657.8 5.6 multiply_reduce_fusion
  663.8 5.5 multiply_reduce_fusion.2
  669.4 2.7 multiply_reduce_fusion.6
  672.0 1.4 pad_maximum_fusion.9
  673.4 0.8 multiply_add_fusion.9
  674.2 6.3 all-reduce.3
  681.8 1.4 fusion.3
  683.2 1.0 copy.452
  684.2 1.0 copy.453
  685.2 1.0 copy.454
  686.1 1.0 copy.455
  688.6 2.1 multiply_add_fusion
  690.6 0.9 multiply_add_fusion.7
  692.2 1.9 multiply_add_fusion.3
  (269 shorter events, 22.4 us)
Async XLA Ops:
  7.2 2.6 copy-start
  7.2 98.9 %all-gather.9.cloned.1.call-start = ((), (), s32[]{:S(2)}) async-start(), calls=%async_computation.1 | async-start | bytes 3932160 | tf_op jit(solution)/shard_map/all_gather | solution.py:927
  9.8 1.6 copy-start.9
  9.8 96.4 %all-gather.7.cloned.1.call-start = ((), (), s32[]{:S(2)}) async-start(), calls=%async_computation | async-start | bytes 3932160 | tf_op jit(solution)/shard_map/all_gather | solution.py:927
  10.9 1.5 copy-start.2
  10.9 241.5 %all-gather.13.cloned.1.call-start = ((), (), s32[]{:S(2)}) async-start(), calls=%async_computation.3 | async-start | bytes 3276800 | tf_op jit(solution)/shard_map/all_gather | solution.py:927
  12.3 3.8 copy-start.30
  12.4 10.1 %copy-start.32 = (f32[1,5018]{1,0:T(1,128)S(1)}, f32[1,5018]{1,0:T(1,128)}, u32[]{:S(2)}) copy-start(f32[1,5018]{1,0:T(1,128)} %param.48) | copy-start | bytes 60220
  12.4 242.6 %all-gather.11.cloned.1.call-start = ((), (), s32[]{:S(2)}) async-start(), calls=%async_computation.2 | async-start | bytes 3276800 | tf_op jit(solution)/shard_map/all_gather | solution.py:927
  14.2 16.3 %copy-start.17 = (f32[2,137,384]{2,0,1:T(2,128)S(1)}, f32[2,137,384]{2,0,1:T(2,128)}, u32[]{:S(2)}) copy-start(f32[2,137,384]{2,0,1:T(2,128)} %param.39) | copy-start | bytes 1262596
  14.3 640.6 %all-reduce.6.cloned.1.call-start = ((), (), s32[]{:S(2)}) async-start(), calls=%async_computation.4 | async-start | bytes 29229056 | tf_op jit(solution)/shard_map/psum | solution.py:1001
  29.6 15.5 %copy-start.11 = (f32[2,137,384]{2,0,1:T(2,128)S(1)}, f32[2,137,384]{2,0,1:T(2,128)}, u32[]{:S(2)}) copy-start(f32[2,137,384]{2,0,1:T(2,128)} %param.36) | copy-start | bytes 1262596
  29.8 16.2 %copy-start.21 = (f32[2,4,2,2064]{3,2,1,0:T(2,128)}, f32[2,4,2,2064]{3,2,1,0:T(2,128)S(1)}, u32[]{:S(2)}) copy-start(f32[2,4,2,2064]{3,2,1,0:T(2,128)S(1)} %reshape.495) | copy-start | bytes 396292
  56.0 1.4 slice-start
  56.0 2.8 slice-start.1
  60.9 6.0 copy-start.18
  63.3 15.6 %copy-start.12 = (f32[256,320]{0,1:T(8,128)S(1)}, f32[256,320]{0,1:T(8,128)}, u32[]{:S(2)}) copy-start(f32[256,320]{0,1:T(8,128)} %param.40) | copy-start | bytes 983044
  101.3 1.8 copy-start.5
  106.1 6.1 copy-start.34
  106.1 7.2 %copy-start.43 = (f32[144]{0:T(256)S(1)}, f32[144]{0:T(256)}, u32[]{:S(2)}) copy-start(f32[144]{0:T(256)} %get-tuple-element.360) | copy-start | bytes 1732
  106.1 7.9 %copy-start.42 = (f32[144]{0:T(256)S(1)}, f32[144]{0:T(256)}, u32[]{:S(2)}) copy-start(f32[144]{0:T(256)} %get-tuple-element.359) | copy-start | bytes 1732
  116.0 136.3 %copy-start.40 = (s32[2,5]{1,0:T(2,128)S(1)}, s32[2,5]{1,0:T(2,128)}, u32[]{:S(2)}) copy-start(s32[2,5]{1,0:T(2,128)} %param.29) | copy-start | bytes 124
  116.0 136.3 %copy-start.41 = (s32[2,1]{0,1:T(1,128)S(1)}, s32[2,1]{0,1:T(1,128)}, u32[]{:S(2)}) copy-start(s32[2,1]{0,1:T(1,128)} %param.28) | copy-start | bytes 28
  254.7 2.8 copy-start.44
  257.9 3.2 copy-start.4
  399.4 0.9 copy-start.27
  399.4 47.1 %copy-start.28 = (f32[2,2,2,24,128]{4,3,2,1,0:T(8,128)S(1)}, f32[2,2,2,24,128]{4,3,2,1,0:T(8,128)}, u32[]{:S(2)}) copy-start(f32[2,2,2,24,128]{4,3,2,1,0:T(8,128)} %get-tuple-element.61) | copy-start | bytes 294916
  399.4 47.1 %copy-start.24 = (f32[2,2,56,128]{3,2,1,0:T(8,128)S(1)}, f32[2,2,56,128]{3,2,1,0:T(8,128)}, u32[]{:S(2)}) copy-start(f32[2,2,56,128]{3,2,1,0:T(8,128)} %get-tuple-element.44.refs_21_) | copy-start | bytes 344068
  399.4 48.1 %copy-start.39 = (f32[2,2,8,128]{3,2,1,0:T(8,128)S(1)}, f32[2,2,8,128]{3,2,1,0:T(8,128)}, u32[]{:S(2)}) copy-start(f32[2,2,8,128]{3,2,1,0:T(8,128)} %get-tuple-element.63) | copy-start | bytes 49156
  399.4 48.1 %copy-start.35 = (f32[2,8,128]{2,1,0:T(8,128)S(1)}, f32[2,8,128]{2,1,0:T(8,128)}, u32[]{:S(2)}) copy-start(f32[2,8,128]{2,1,0:T(8,128)} %get-tuple-element.54.refs_22_) | copy-start | bytes 24580
  399.5 49.0 %copy-start.36 = (f32[2,24,128]{2,1,0:T(8,128)S(1)}, f32[2,24,128]{2,1,0:T(8,128)}, u32[]{:S(2)}) copy-start(f32[2,24,128]{2,1,0:T(8,128)} %get-tuple-element.65) | copy-start | bytes 73732
  399.5 49.0 %copy-start.29 = (f32[40,128]{1,0:T(8,128)S(1)}, f32[40,128]{1,0:T(8,128)}, u32[]{:S(2)}) copy-start(f32[40,128]{1,0:T(8,128)} %get-tuple-element.55.refs_23_) | copy-start | bytes 61444
  400.9 254.0 %copy-start.22 = (f32[2,137,384]{2,0,1:T(2,128)S(1)}, f32[2,137,384]{2,0,1:T(2,128)}, u32[]{:S(2)}) copy-start(f32[2,137,384]{2,0,1:T(2,128)} %param.38) | copy-start | bytes 1262596
  400.9 254.0 %copy-start.23 = (f32[2,137,384]{2,0,1:T(2,128)S(1)}, f32[2,137,384]{2,0,1:T(2,128)}, u32[]{:S(2)}) copy-start(f32[2,137,384]{2,0,1:T(2,128)} %param.37) | copy-start | bytes 1262596
  448.9 208.9 %copy-start.1 = (f32[2,64,3072]{2,1,0:T(8,128)S(1)}, f32[2,64,3072]{2,1,0:T(8,128)}, u32[]{:S(2)}) copy-start(f32[2,64,3072]{2,1,0:T(8,128)} %param.32) | copy-start | bytes 4718596
  657.8 6.0 copy-start.3
  663.8 5.6 copy-start.13
  663.8 5.6 copy-start.25
  663.8 5.6 copy-start.26
  669.3 4.1 copy-start.31
  669.3 4.1 copy-start.33
  669.3 4.1 copy-start.37
  669.3 4.1 copy-start.38
  681.5 2.7 copy-start.16
  681.8 3.3 copy-start.15
  683.2 5.3 copy-start.6
  683.2 5.3 copy-start.7
  688.5 2.1 copy-start.14
  688.5 2.1 copy-start.19
  688.5 2.1 copy-start.20
  688.5 3.0 copy-start.10
  690.6 1.6 copy-start.8
Sparse Core Ops, SparseCore 0:
  10.2 36.3 all-gather.8
  48.8 32.1 all-gather.6
  82.5 25.5 all-gather.12
  109.5 26.7 all-gather.10
  399.6 255.2 all-reduce.5

commit v3 on v2

--- a/solution.py
+++ b/solution.py
@@ -491,16 +491,39 @@
     )(*inputs)
 
 
+CLASS_PAD = 1024
+FACT = CLASS_PAD + 384
+BACK_ROWS = ((24, 24, 8, 24), (40, 24, 8, 40))
+
+
+def round_up(value, unit):
+    return -(-value // unit) * unit
+
+
+CHUNKS = 6
+MATS = 2 * E // LANES * 8
+CHAN = 3 * 18
+AT_CHAN = L * MATS
+AT_HEAD = AT_CHAN + L * CHAN
+AT_END = AT_HEAD + 2 * HEAD // 4 // 8
+
+
+def packed_blocks(sizes):
+    return round_up(AT_END, CHUNKS * 2 * sizes[0])
+
+
 def backward_kernel(sizes, *refs):
-    (dpool_h, mask, edge_l, edge_r, area, wexp, headt, taps, squeeze, excite, gain_e, gain_c, gain_h,
+    (dpool_h, extra, mask, edge_l, edge_r, area, wexp, headt, taps, squeeze, excite, gain_e, gain_c, gain_h,
      pre_s, mixed_s, feat_s, out_s, low_s, pool_s, unit_s, gate_s, tot_e, tot_c, tot_h,
-     g_exp, g_taps, g_sq, g_ex, g_exb, g_sqb, g_head, back_e, back_c, back_h,
-     pre, mixed, grad, grad_hid, low_out, low_pre, pads_x, pads_g, slope, dgate, dpool, stages, load_sems) = refs[:47]
-    rest = list(refs[47:])
+     packed, back_e, back_c, back_h,
+     pre, mixed, grad, grad_hid, low_out, low_pre, pads_x, pads_g, slope, dgate, dpool, stages, load_sems,
+     held, held_chan, held_exb, held_sqb, out_v, low_v, row_sems) = refs[:49]
+    rest = list(refs[49:])
+    n_dp, n_sh = sizes
     sums = []
     for b in range(BATCHES):
         group = []
-        for rows in (24, 24, 8, 24):
+        for rows in BACK_ROWS[b]:
             group.append((rest[0], rest[1], rest[2:6], rows))
             rest = rest[6:]
         sums.append(group)
@@ -522,8 +545,16 @@
             return pltpu.make_async_copy(mixed_s.at[layer, :, rows], mixed.at[b], load_sems.at[b, 1])
         return pltpu.make_async_copy(feat_s.at[:, rows], pre.at[b, 0:HC], load_sems.at[b, 0])
 
+    def load_out(layer):
+        return pltpu.make_async_copy(out_s.at[layer], out_v, row_sems.at[0])
+
+    def load_low(layer):
+        return pltpu.make_async_copy(low_s.at[layer], low_v, row_sems.at[1])
+
     for b in range(BATCHES):
         load(b, 2, 0).start()
+    load_low(L).start()
+    load_out(L - 1).start()
     for b in range(BATCHES):
         load(b, 1, L - 1).start()
     for slot in range(IMGS):
@@ -532,6 +563,22 @@
             pads[slot, GAP + ROWS : 2 * GAP + ROWS, :] = jnp.zeros((GAP, LANES), F32)
     dgate[...] = jnp.zeros(dgate.shape, F32)
     stages[...] = jnp.zeros(stages.shape, F32)
+    stages[1, 24:40, :] = extra[...]
+    held_chan[...] = jnp.zeros(held_chan.shape, F32)
+    spare = packed.shape[1] - AT_END
+    if spare:
+        packed[:, AT_END:] = jnp.zeros((n_sh, spare, 8, LANES), F32)
+
+    def pack(first, c, value):
+        for t in range(n_sh):
+            for half in range(2):
+                piece = value[64 * t : 64 * t + 64, half * LANES : (half + 1) * LANES]
+                packed[t, pl.ds(first + 16 * c + 8 * half, 8)] = piece.reshape(8, 8, LANES)
+
+    def pack_chan(layer):
+        for k in range(EC):
+            first = AT_CHAN + CHAN * layer + 18 * (k % 3)
+            packed[k // 3, first : first + 18] = held_chan[:, k * LANES : (k + 1) * LANES].reshape(18, 8, LANES)
 
     def forward_total(kind, layer):
         return (tot_e.at[layer, 0], tot_e.at[layer, 1], tot_c.at[layer], tot_h)[kind]
@@ -608,14 +655,8 @@
                 full = image(b, i)[1]
                 value = grad_hid[full, cols]
                 first = first + fold(value)
-                second = second + fold(value * out_s[layer, full, cols])
+                second = second + fold(value * out_v[full, cols])
             put(stage, half, first, second)
-
-    def add(ref, index, value, b):
-        if b == 0:
-            ref[index] = value
-        else:
-            ref[index] = ref[index] + value
 
     def head_second(b, hook=None):
         mine = slice(b * HALF, (b + 1) * HALF)
@@ -623,8 +664,15 @@
         def body(c):
             for half in range(2):
                 norm_back_rows(b, 3, 0, 2 * c + half, gain_h[0:1, lanes(2 * c + half)], pre)
-            rows = pl.ds(pl.multiple_of(c * 256, 256), 256)
-            add(g_head, (rows, slice(None)), contract(low_pre[:, lanes(c, 256)], low_s[L, mine, :], 0, 0), b)
+            value = contract(low_pre[:, lanes(c, 256)], low_v[mine, :], 0, 0)
+            if b == 0:
+                held[c] = value
+            else:
+                value = value + held[c]
+                for i in range(32):
+                    row = 32 * c + i
+                    for half in range(2):
+                        packed[row // 40, AT_HEAD + 40 * half + lax.rem(row, 40)] = value[8 * i : 8 * i + 8, half * LANES : (half + 1) * LANES]
 
         repeat(HEAD // 256, body, hook)
         grad_hid[mine, :] = jnp.dot(low_pre[:, 0:HEAD], headt[...], preferred_element_type=F32)
@@ -638,7 +686,7 @@
             one, two, three = back_coefs(b, 2, layer, half, gain_c[layer, 0:1, cols])
             for i in range(IMGS):
                 rows, full = image(b, i)
-                low_out[rows, cols] = (mask[full, :] * (one * grad_hid[full, cols] + two + three * out_s[layer, full, cols])).astype(BF16)
+                low_out[rows, cols] = (mask[full, :] * (one * grad_hid[full, cols] + two + three * out_v[full, cols])).astype(BF16)
 
         def body(c):
             value = jnp.dot(low_out[...], wexp[layer, :, lanes(E // 256 + c, 256)], preferred_element_type=F32)
@@ -652,18 +700,34 @@
                     grad[b, k, rows, :] = piece
                     dgate[i : i + 1, lanes(k)] = jnp.sum(fold(piece * act), 0, keepdims=True)
                     low_pre[rows, lanes(k)] = (act * gate_s[layer, b * 8 + i : b * 8 + i + 1, lanes(k)]).astype(BF16)
-            add(g_exp, (layer, slice(None), lanes(E // 256 + c, 256)), contract(low_out[...], low_pre[:, lanes(c, 256)], 0, 0), b)
+            value = contract(low_out[...], low_pre[:, lanes(c, 256)], 0, 0)
+            if b == 0:
+                held[c] = value
+            else:
+                pack(MATS * layer + MATS // 2, c, value + held[c])
 
         repeat(E // 256, body, hook)
         gate = gate_s[layer, eight, :]
         units = unit_s[layer, eight, :]
         sig = jax.nn.sigmoid(units)
         inner = dgate[...] * gate * (1.0 - gate)
-        add(g_exb, layer, jnp.broadcast_to(jnp.sum(inner, 0, keepdims=True), (8, E)), b)
-        add(g_ex, layer, matmul_tb(units * sig, inner), b)
+        bias_x = jnp.sum(inner, 0, keepdims=True)
+        grad_x = matmul_tb(units * sig, inner)
         outer = matmul_bt(inner, excite[layer]) * (sig * (1.0 + units * (1.0 - sig)))
-        add(g_sqb, layer, jnp.broadcast_to(jnp.sum(outer, 0, keepdims=True), (8, SE)), b)
-        add(g_sq, layer, matmul_tb(outer, pool_s[layer, eight, :]), b)
+        bias_r = jnp.sum(outer, 0, keepdims=True)
+        grad_r = matmul_tb(outer, pool_s[layer, eight, :])
+        if b == 0:
+            held_exb[0:1, :] = bias_x
+            held_chan[9 + SE : 9 + 2 * SE, :] = grad_x
+            held_sqb[0:1, 0:SE] = bias_r
+            held_chan[9 : 9 + SE, :] = grad_r
+        else:
+            bias_x = bias_x + held_exb[0:1, :]
+            for k in range(EC):
+                stages[1, 24 + k : 25 + k, :] = bias_x[:, k * LANES : (k + 1) * LANES]
+            stages[1, 24 + EC : 25 + EC, 0:SE] = bias_r + held_sqb[0:1, 0:SE]
+            held_chan[9 : 9 + SE, :] = held_chan[9 : 9 + SE, :] + grad_r
+            held_chan[9 + SE : 9 + 2 * SE, :] = held_chan[9 + SE : 9 + 2 * SE, :] + grad_x
         dpool[...] = matmul(outer, squeeze[layer])
 
     def block_second(b, layer, hook=None):
@@ -722,9 +786,15 @@
                         total[k] = total[k] + fold(sides[k % 3] * pads_x[i, start + o : start + o + TILE_BACK, :])
             put(stage, c, first, second)
             for k in range(9):
-                add(g_taps, (layer, slice(k, k + 1), lanes(c)), jnp.sum(total[k], 0, keepdims=True), b)
+                row = jnp.sum(total[k], 0, keepdims=True)
+                if b == 0:
+                    held_chan[k : k + 1, lanes(c)] = row
+                else:
+                    held_chan[k : k + 1, lanes(c)] = held_chan[k : k + 1, lanes(c)] + row
 
         repeat(EC, body, hook)
+        if b == 1:
+            pack_chan(layer)
 
     def block_expand(b, layer, hook=None):
         mine = slice(b * HALF, (b + 1) * HALF)
@@ -732,7 +802,11 @@
         def body(c):
             for part in range(2):
                 norm_back_rows(b, 0, layer, 2 * c + part, gain_e[layer, 0:1, lanes(2 * c + part)], pre)
-            add(g_exp, (layer, slice(None), lanes(c, 256)), contract(low_s[layer, mine, :], low_pre[:, lanes(c, 256)], 0, 0), b)
+            value = contract(low_v[mine, :], low_pre[:, lanes(c, 256)], 0, 0)
+            if b == 0:
+                held[c] = value
+            else:
+                pack(MATS * layer, c, value + held[c])
 
         repeat(E // 256, body, hook)
         if layer > 0:
@@ -748,6 +822,8 @@
     heads[1].start(stages.at[1])
     thirds = [summer(b, 2, L - 1) for b in range(BATCHES)]
     heads[0].finish()
+    load_low(L).wait()
+    load_out(L - 1).wait()
     head_second(0, (2, heads[1].middle))
     load(0, 0, L - 1).start()
     thirds[0].start(stages.at[0])
@@ -755,6 +831,7 @@
     head_second(1, (3, thirds[0].middle))
     load(1, 0, L - 1).start()
     thirds[1].start(stages.at[1])
+    load_low(L - 1).start()
     for layer in reversed(range(L)):
         twos = [summer(b, 1, layer) for b in range(BATCHES)]
         ones = [summer(b, 0, layer) for b in range(BATCHES)]
@@ -766,48 +843,49 @@
         thirds[1].finish()
         load(1, 1, layer).wait()
         block_gate(1, layer, (3, twos[0].middle))
+        if layer > 0:
+            load_out(layer - 1).start()
         block_second(1, layer)
         twos[1].start(stages.at[1])
         twos[0].finish()
         load(0, 0, layer).wait()
         block_spread(0, layer, (4, twos[1].middle))
+        ones[0].start(stages.at[0])
         if layer > 0:
             load(0, 1, layer - 1).start()
-        ones[0].start(stages.at[0])
         twos[1].finish()
         load(1, 0, layer).wait()
         block_spread(1, layer, (4, ones[0].middle))
+        ones[1].start(stages.at[1])
         if layer > 0:
             load(1, 1, layer - 1).start()
-        ones[1].start(stages.at[1])
         ones[0].finish()
+        load_low(layer).wait()
+        if layer > 0:
+            load_out(layer - 1).wait()
         block_expand(0, layer, (3, ones[1].middle))
         if layer > 0:
-            load(0, 0, layer - 1).start()
             thirds = [summer(b, 2, layer - 1) for b in range(BATCHES)]
             thirds[0].start(stages.at[0])
+            load(0, 0, layer - 1).start()
         ones[1].finish()
         block_expand(1, layer, None if layer == 0 else (3, thirds[0].middle))
         if layer > 0:
+            thirds[1].start(stages.at[1])
             load(1, 0, layer - 1).start()
-            thirds[1].start(stages.at[1])
+            load_low(layer - 1).start()
 
 
 def run_backward_all(sizes, inputs):
     sds = jax.ShapeDtypeStruct
     vm = pl.BlockSpec(memory_space=pltpu.VMEM)
     hbm = pl.BlockSpec(memory_space=pl.ANY)
+    n_dp, n_sh = sizes
     outs = [
-        sds((L, C, 2 * E), F32),
-        sds((L, 9, E), F32),
-        sds((L, SE, E), F32),
-        sds((L, SE, E), F32),
-        sds((L, 8, E), F32),
-        sds((L, 8, SE), F32),
-        sds((HEAD, C), F32),
-        sds((L, BATCHES, 2, 24, LANES), F32),
+        sds((n_sh, packed_blocks(sizes), 8, LANES), F32),
+        sds((L, BATCHES, 2, 40, LANES), F32),
         sds((L, BATCHES, 8, LANES), F32),
-        sds((BATCHES, 24, LANES), F32),
+        sds((BATCHES, 40, LANES), F32),
     ]
     scratch = [
         pltpu.VMEM((BATCHES, EC, HALF, LANES), F32),
@@ -821,13 +899,20 @@
         pltpu.VMEM((HALF, LANES), F32),
         pltpu.VMEM((8, E), F32),
         pltpu.VMEM((8, E), F32),
-        pltpu.VMEM((BATCHES, 24, LANES), F32),
+        pltpu.VMEM((BATCHES, 40, LANES), F32),
         pltpu.SemaphoreType.DMA((BATCHES, 2)),
+        pltpu.VMEM((E // 256, 256, 256), F32),
+        pltpu.VMEM((144, E), F32),
+        pltpu.VMEM((8, E), F32),
+        pltpu.VMEM((8, LANES), F32),
+        pltpu.VMEM((FULL, C), F32),
+        pltpu.VMEM((FULL, C), BF16),
+        pltpu.SemaphoreType.DMA((2,)),
     ]
     for b in range(BATCHES):
-        for rows in (24, 24, 8, 24):
+        for rows in BACK_ROWS[b]:
             scratch = scratch + sum_scratch(sizes, rows)
-    specs = [vm] * 13 + [hbm] * 3 + [vm] * 8
+    specs = [vm] * 14 + [hbm] * 5 + [vm] * 6
     return pl.pallas_call(
         functools.partial(backward_kernel, sizes),
         out_shape=outs,
@@ -839,6 +924,427 @@
     )(*inputs)
 
 
+GROUPS = 12
+
+
+def update_kernel(sizes, *refs):
+    (packed, facts, fixes, *state) = refs[:19]
+    state_in = [state[4 * k : 4 * k + 4] for k in range(4)]
+    outs = refs[19:36]
+    out_refs = [outs[4 * k : 4 * k + 4] for k in range(4)]
+    norms = outs[16]
+    peers = refs[36]
+    (own, near, cross, side, line, full, gathered, g_class, turned, sums_near, ratios) = refs[37:48]
+    boxes = [refs[48 + 5 * k : 53 + 5 * k] for k in range(4)]
+    (core_s, core_r, x_s, x_r, y_s, y_r, z_s, z_r, zz_s, zz_r, yy_s, yy_r,
+     fn_s, fn_r, ff_s, ff_r, nn_s, nn_r, load_sems, store_sems, misc) = refs[68:89]
+    n_dp, n_sh = sizes
+    d, s = lax.axis_index("dp"), lax.axis_index("shard")
+    count = packed_blocks(sizes)
+    chunk = count // CHUNKS
+    half = chunk // 2
+    n_z = n_dp // 2
+    piece = half // n_z
+    bit0, bit1 = lax.rem(s, 2), s // 2
+    near_peer = s + 1 - 2 * bit0
+    far_peer = s + 2 - 4 * bit1
+    yb, zi = lax.rem(d, 2), d // 2
+    y_peer = d + 1 - 2 * yb
+
+    greet(sizes)
+
+    def load_own(t):
+        return pltpu.make_async_copy(packed.at[t], own.at[t], load_sems.at[16 + t])
+
+    def load(k, i):
+        return pltpu.make_async_copy(state_in[k][i], boxes[k][i], load_sems.at[4 * k + i])
+
+    def store(k, i):
+        source = boxes[k][(4, 1, 2, 3)[i]]
+        return pltpu.make_async_copy(source, out_refs[k][i], store_sems.at[4 * k + i])
+
+    def core_copy(k, i):
+        rows = pl.ds(k * chunk, chunk)
+        return pltpu.make_async_remote_copy(
+            packed.at[2 * i + 1 - bit0, rows], near.at[i, rows], core_s.at[k, i], core_r.at[k, i],
+            device_id=(d, near_peer), device_id_type=MESH)
+
+    def x_copy(k):
+        rows = pl.ds(k * chunk, chunk)
+        return pltpu.make_async_remote_copy(
+            own.at[far_peer, rows], cross.at[rows], x_s.at[k], x_r.at[k],
+            device_id=(d, far_peer), device_id_type=MESH)
+
+    def y_copy(k):
+        rows = pl.ds(k * chunk + (1 - yb) * half, half)
+        return pltpu.make_async_remote_copy(
+            own.at[s, rows], side.at[k], y_s.at[k], y_r.at[k],
+            device_id=(y_peer, s), device_id_type=MESH)
+
+    def z_copy(k, step, source, target):
+        rows = pl.ds(k * chunk + yb * half + target * piece, piece)
+        return pltpu.make_async_remote_copy(
+            own.at[s, rows], line.at[k, source], z_s.at[k, step], z_r.at[k, source],
+            device_id=(2 * target + yb, s), device_id_type=MESH)
+
+    def zz_copy(k, step, source, target):
+        rows = pl.ds(k * (chunk // 2) + yb * (half // 2) + source * (piece // 2), piece // 2)
+        return pltpu.make_async_remote_copy(
+            full.at[rows], full.at[rows], zz_s.at[k, step], zz_r.at[k, source],
+            device_id=(2 * target + yb, s), device_id_type=MESH)
+
+    def yy_copy(k, b):
+        rows = pl.ds(k * (chunk // 2) + b * (half // 2), half // 2)
+        return pltpu.make_async_remote_copy(
+            full.at[rows], full.at[rows], yy_s.at[k], yy_r.at[k],
+            device_id=(y_peer, s), device_id_type=MESH)
+
+    def over_z(action):
+        def step(j, carry):
+            action(j, lax.rem(zi + j, n_z))
+            return carry
+
+        lax.fori_loop(1, n_z, step, 0)
+
+    def add_into(t, low, length, other, low_other, unit=8):
+        def step(i, carry):
+            rows = pl.ds(low + i * unit, unit)
+            own[t, rows] = own[t, rows] + other(pl.ds(low_other + i * unit, unit))
+            return carry
+
+        lax.fori_loop(0, length // unit, step, 0)
+
+    def stage_core(k):
+        for i in range(2):
+            core_copy(k, i).start()
+
+    def stage_x(k):
+        for i in range(2):
+            core_copy(k, i).wait_recv()
+        low = k * chunk
+        add_into(far_peer, low, chunk, lambda rows: near[1 - bit1, rows], low)
+        x_copy(k).start()
+        add_into(s, low, chunk, lambda rows: near[bit1, rows], low)
+
+    def stage_y(k):
+        x_copy(k).wait_recv()
+        low = k * chunk
+        give = low + (1 - yb) * half
+        keep = low + yb * half
+        add_into(s, give, half, lambda rows: cross[rows], give)
+        y_copy(k).start()
+        add_into(s, keep, half, lambda rows: cross[rows], keep)
+
+    def stage_z(k):
+        y_copy(k).wait_recv()
+        add_into(s, k * chunk + yb * half, half, lambda rows: side[k, rows], 0)
+        over_z(lambda j, t: z_copy(k, j, zi, t).start())
+
+    def stage_zz(k):
+        over_z(lambda j, t: z_copy(k, j, t, zi).wait_recv())
+        low = k * chunk + yb * half + zi * piece
+
+        def step(i, carry):
+            total = own[s, pl.ds(low + 2 * i, 2)]
+            for j in range(1, n_z):
+                total = total + line[k, lax.rem(zi + j, n_z), pl.ds(2 * i, 2)]
+            full[low // 2 + i] = total.reshape(16, LANES).astype(BF16)
+            return carry
+
+        lax.fori_loop(0, piece // 2, step, 0)
+        over_z(lambda j, t: zz_copy(k, j, zi, t).start())
+
+    def stage_yy(k):
+        over_z(lambda j, t: zz_copy(k, j, t, zi).wait_recv())
+        yy_copy(k, yb).start()
+
+    def stage_done(k):
+        yy_copy(k, 1 - yb).wait_recv()
+
+    def settle(k):
+        for i in range(2):
+            core_copy(k, i).wait_send()
+        x_copy(k).wait_send()
+        y_copy(k).wait_send()
+        over_z(lambda j, t: z_copy(k, j, zi, t).wait_send())
+        over_z(lambda j, t: zz_copy(k, j, zi, t).wait_send())
+        yy_copy(k, yb).wait_send()
+
+    def own_facts():
+        return pltpu.make_async_copy(facts.at[s], peers.at[d, s], misc.at[0])
+
+    def fact_near(step, source, target):
+        return pltpu.make_async_remote_copy(
+            facts.at[target], peers.at[d, source], fn_s.at[step], fn_r.at[source],
+            device_id=(d, target), device_id_type=MESH)
+
+    def fact_far(step, source, target):
+        return pltpu.make_async_remote_copy(
+            peers.at[source], peers.at[source], ff_s.at[step], ff_r.at[source],
+            device_id=(target, s), device_id_type=MESH)
+
+    def over_dp(action):
+        def step(j, carry):
+            action(j, lax.rem(d + j, n_dp))
+            return carry
+
+        lax.fori_loop(1, n_dp, step, 0)
+
+    def facts_begin():
+        own_facts().start()
+        for j in range(1, n_sh):
+            fact_near(j, s, lax.rem(s + j, n_sh)).start()
+
+    def facts_second():
+        for j in range(1, n_sh):
+            fact_near(j, lax.rem(s + j, n_sh), s).wait_recv()
+            fact_near(j, s, s).wait_send()
+        own_facts().wait()
+        over_dp(lambda j, t: fact_far(j, d, t).start())
+
+    def facts_third():
+        def arrive(j, t):
+            fact_far(j, t, d).wait_recv()
+            fact_far(j, d, d).wait_send()
+
+        over_dp(arrive)
+        for first in range(0, n_dp, 8):
+            copy = pltpu.make_async_copy(peers.at[pl.ds(first, 8)], gathered, misc.at[1])
+            copy.start()
+            copy.wait()
+            value = gathered[...].reshape(8 * n_sh * 16, FACT)
+            product = contract(value[:, CLASS_PAD:], value[:, :CLASS_PAD], 0, 0)
+            g_class[...] = product if first == 0 else g_class[...] + product
+
+    sums_near[s] = jnp.zeros((24, LANES), F32)
+    first_fix, second_fix = fixes[0:1, 0:1], fixes[1:2, 0:1]
+
+    def note(row, value):
+        square = value * value
+        width = square.shape[1]
+        line_sum = jnp.sum(square, 0, keepdims=True)
+        total = jnp.zeros((1, LANES), F32)
+        for low in range(0, width - width % LANES, LANES):
+            total = total + line_sum[:, low : low + LANES]
+        tail = width % LANES
+        if tail:
+            total = total + jnp.concatenate([line_sum[:, width - tail :], jnp.zeros((1, LANES - tail), F32)], 1)
+        sums_near[s, row : row + 1, :] = sums_near[s, row : row + 1, :] + total
+
+    def moments(k, index, grad):
+        weight, first, second, unused, update = boxes[k]
+        new_first = BETA_ONE * first[index] + (1.0 - BETA_ONE) * grad
+        new_second = BETA_TWO * second[index] + (1.0 - BETA_TWO) * grad * grad
+        first[index] = new_first
+        second[index] = new_second
+        value = new_first / first_fix / (jnp.sqrt(new_second / second_fix) + EPS_ADAM) + DECAY * weight[index]
+        update[index] = value
+        return value
+
+    every = slice(None)
+
+    def mats_index(layer, c):
+        return (layer, every, lanes(c))
+
+    def weights_squares():
+        for layer in range(L):
+            for part in range(2):
+
+                def body(c):
+                    note(2 * layer + part, boxes[0][0][mats_index(layer, c + part * EC)])
+
+                repeat(EC, body)
+            for kk in range(3):
+                cols = slice(kk * LANES, (kk + 1) * LANES)
+                note(2 * L + 3 * layer, boxes[1][0][layer, 0:9, cols])
+                note(2 * L + 3 * layer + 1, boxes[1][0][layer, 9 : 9 + SE, cols])
+                note(2 * L + 3 * layer + 2, boxes[1][0][layer, 9 + SE : 9 + 2 * SE, cols])
+        note(5 * L, boxes[2][0][...])
+
+        def body(i):
+            note(5 * L + 1, boxes[3][0][pl.ds(pl.multiple_of(i * 40, 40), 40), :])
+
+        repeat(8, body)
+
+    def mats_moments(layer):
+        for part in range(2):
+
+            def body(c):
+                panel = c + part * EC
+                grad = full[pl.ds(layer * (MATS // 2) + 4 * panel, 4)].astype(F32).reshape(64, LANES)
+                note(GROUPS + 2 * layer + part, moments(0, mats_index(layer, panel), grad))
+
+            repeat(EC, body)
+
+    def chan_moments():
+        for layer in range(L):
+            for kk in range(3):
+                low = (AT_CHAN + CHAN * layer + 18 * kk) // 2
+                grad = full[low : low + 9].astype(F32).reshape(144, LANES)[:137]
+                value = moments(1, (layer, every, slice(kk * LANES, (kk + 1) * LANES)), grad)
+                note(GROUPS + 2 * L + 3 * layer, value[0:9])
+                note(GROUPS + 2 * L + 3 * layer + 1, value[9 : 9 + SE])
+                note(GROUPS + 2 * L + 3 * layer + 2, value[9 + SE :])
+
+    def head_moments():
+        rows = HEAD // 4
+        turned[rows:, :] = jnp.zeros((turned.shape[0] - rows, C), F32)
+        for part in range(2):
+            low = (AT_HEAD + part * (rows // 8)) // 2
+            turned[0:rows, part * LANES : (part + 1) * LANES] = full[low : low + rows // 16].astype(F32).reshape(rows, LANES)
+        grad = turned[...].T
+        note(GROUPS + 5 * L, moments(2, (every, every), grad[:, :rows]))
+
+    def class_moments():
+        def body(i):
+            rows = pl.ds(pl.multiple_of(i * 40, 40), 40)
+            note(GROUPS + 5 * L + 1, moments(3, (rows, every), g_class[rows, :CLASSES]))
+
+        repeat(8, body)
+
+    def norm_copy(step, source, target):
+        return pltpu.make_async_remote_copy(
+            sums_near.at[source], sums_near.at[source], nn_s.at[step], nn_r.at[source],
+            device_id=(d, target), device_id_type=MESH)
+
+    def finish(k, index, factor):
+        weight, unused, unused_two, average, update = boxes[k]
+        fresh = weight[index] - RATE * factor * update[index]
+        update[index] = fresh
+        average[index] = KEEP * average[index] + (1.0 - KEEP) * fresh
+
+    for k in range(CHUNKS):
+        stage_core(k)
+    for t in range(n_sh):
+        load_own(t).start()
+    facts_begin()
+    for i in range(4):
+        for k in range(4):
+            load(k, i).start()
+    for t in range(n_sh):
+        load_own(t).wait()
+    for tau in range(1, CHUNKS + 6):
+        stages = (stage_x, stage_y, stage_z, stage_zz, stage_yy, stage_done)
+        for age, stage in enumerate(stages):
+            k = tau - 1 - age
+            if 0 <= k < CHUNKS:
+                stage(k)
+        if tau == 1:
+            facts_second()
+            for k in range(4):
+                load(k, 0).wait()
+            weights_squares()
+        if tau == 2:
+            for i in range(1, 4):
+                for k in range(4):
+                    load(k, i).wait()
+        if tau == CHUNKS:
+            facts_third()
+            class_moments()
+            for i in (1, 2):
+                store(3, i).start()
+        if tau == CHUNKS + 2:
+            mats_moments(0)
+        if tau == CHUNKS + 4:
+            mats_moments(1)
+            for i in (1, 2):
+                store(0, i).start()
+    chan_moments()
+    head_moments()
+    for j in range(1, n_sh):
+        norm_copy(j, s, lax.rem(s + j, n_sh)).start()
+    for k in (1, 2):
+        for i in (1, 2):
+            store(k, i).start()
+    for k in range(CHUNKS):
+        settle(k)
+    for j in range(1, n_sh):
+        norm_copy(j, lax.rem(s + j, n_sh), s).wait_recv()
+        norm_copy(j, s, s).wait_send()
+    total = sums_near[0]
+    for j in range(1, n_sh):
+        total = total + sums_near[j]
+    root = jnp.broadcast_to(jnp.sqrt(jnp.sum(total, 1, keepdims=True)), (24, LANES))
+    norms[...] = root
+    ratios[0:GROUPS, :] = root[0:GROUPS] / root[GROUPS : 2 * GROUPS]
+
+    def ratio(row):
+        return ratios[row : row + 1, 0:1]
+
+    for layer in range(L):
+        for part in range(2):
+
+            def body(c):
+                finish(0, mats_index(layer, c + part * EC), ratio(2 * layer + part))
+
+            repeat(EC, body)
+    for i in (0, 3):
+        store(0, i).start()
+
+    def body(i):
+        finish(3, (pl.ds(pl.multiple_of(i * 40, 40), 40), every), ratio(5 * L + 1))
+
+    repeat(8, body)
+    for i in (0, 3):
+        store(3, i).start()
+    row = lax.broadcasted_iota(jnp.int32, (137, LANES), 0)
+    for layer in range(L):
+        low = 2 * L + 3 * layer
+        factor = jnp.where(row < 9, ratio(low), jnp.where(row < 9 + SE, ratio(low + 1), ratio(low + 2)))
+        for kk in range(3):
+            finish(1, (layer, every, slice(kk * LANES, (kk + 1) * LANES)), factor)
+    finish(2, (every, every), ratio(5 * L))
+    for k in (1, 2):
+        for i in (0, 3):
+            store(k, i).start()
+    for k in range(4):
+        for i in range(4):
+            store(k, i).wait()
+
+
+def run_update(sizes, packed, facts, fixes, states):
+    sds = jax.ShapeDtypeStruct
+    vm = pl.BlockSpec(memory_space=pltpu.VMEM)
+    hbm = pl.BlockSpec(memory_space=pl.ANY)
+    n_dp, n_sh = sizes
+    count = packed_blocks(sizes)
+    chunk = count // CHUNKS
+    n_z = n_dp // 2
+    sem = pltpu.SemaphoreType.DMA
+    outs = [sds(item.shape, F32) for group in states for item in group]
+    outs = outs + [sds((2 * GROUPS, LANES), F32), sds((n_dp, n_sh, 16, FACT), BF16)]
+    scratch = [
+        pltpu.VMEM((n_sh, count, 8, LANES), F32),
+        pltpu.VMEM((2, count, 8, LANES), F32),
+        pltpu.VMEM((count, 8, LANES), F32),
+        pltpu.VMEM((CHUNKS, chunk // 2, 8, LANES), F32),
+        pltpu.VMEM((CHUNKS, n_z, chunk // 2 // n_z, 8, LANES), F32),
+        pltpu.VMEM((count // 2, 16, LANES), BF16),
+        pltpu.VMEM((8, n_sh, 16, FACT), BF16),
+        pltpu.VMEM((FACT - CLASS_PAD, CLASS_PAD), F32),
+        pltpu.VMEM((FACT - CLASS_PAD, C), F32),
+        pltpu.VMEM((n_sh, 2 * GROUPS, LANES), F32),
+        pltpu.VMEM((16, LANES), F32),
+    ]
+    for group in states:
+        scratch = scratch + [pltpu.VMEM(group[0].shape, F32)] * 5
+    scratch = scratch + [
+        sem((CHUNKS, 2)), sem((CHUNKS, 2)), sem((CHUNKS,)), sem((CHUNKS,)), sem((CHUNKS,)), sem((CHUNKS,)),
+        sem((CHUNKS, n_z)), sem((CHUNKS, n_z)), sem((CHUNKS, n_z)), sem((CHUNKS, n_z)), sem((CHUNKS,)), sem((CHUNKS,)),
+        sem((n_sh,)), sem((n_sh,)), sem((n_dp,)), sem((n_dp,)), sem((n_sh,)), sem((n_sh,)),
+        sem((20,)), sem((16,)), sem((2,)),
+    ]
+    return pl.pallas_call(
+        functools.partial(update_kernel, sizes),
+        out_shape=outs,
+        in_specs=[hbm, hbm, vm] + [hbm] * 16,
+        out_specs=[hbm] * 16 + [vm, hbm],
+        scratch_shapes=scratch,
+        compiler_params=pltpu.CompilerParams(collective_id=3, has_side_effects=True, vmem_limit_bytes=63 * 2**20),
+        name="update",
+    )(packed, facts, fixes, *[item for group in states for item in group])
+
+
 def objective(logits, target, onehot, coef):
     logp = jax.nn.log_softmax(logits)
     per = -jnp.sum(onehot * logp, 1) + jnp.sum(jnp.exp(target) * (target - logp), 1)
@@ -848,35 +1354,6 @@
 def own_slice(value, dim, parts, place):
     width = value.shape[dim] // parts
     return lax.dynamic_slice_in_dim(value, place * width, width, dim)
-
-
-def mats_groups(value):
-    rows = jnp.sum(value * value, 1)
-    half = rows.shape[1] // 2
-    return jnp.stack([jnp.sum(rows[:, :half], 1), jnp.sum(rows[:, half:], 1)], 1).reshape(-1)
-
-
-def chan_groups(value):
-    rows = jnp.sum(value * value, 2)
-    return jnp.stack(
-        [jnp.sum(rows[:, :9], 1), jnp.sum(rows[:, 9 : 9 + SE], 1), jnp.sum(rows[:, 9 + SE :], 1)], 1
-    ).reshape(-1)
-
-
-def mats_factor(ratio, value):
-    paired = ratio.reshape(-1, 2)
-    column = jnp.arange(value.shape[2])
-    return jnp.where(column[None, :] < value.shape[2] // 2, paired[:, 0:1], paired[:, 1:2])[
-        :, None, :
-    ]
-
-
-def chan_factor(ratio, value):
-    triple = ratio.reshape(-1, 3)
-    row = jnp.arange(value.shape[1])[None, :]
-    return jnp.where(
-        row < 9, triple[:, 0:1], jnp.where(row < 9 + SE, triple[:, 1:2], triple[:, 2:3])
-    )[:, :, None]
 
 
 def adapt(first, second, grad, first_fix, second_fix):
@@ -986,21 +1463,32 @@
     target = jax.nn.log_softmax(logits[1])
     loss, pull = jax.vjp(lambda value: objective(value, target, onehot, coef), logits[0])
     grad_low = pull(jnp.float32(1.0))[0].astype(BF16)
-    grad_class = contract(pooled_low[0], grad_low, 0, 0)
     grad_class_bias = jnp.sum(grad_low.astype(F32), 0)
     grad_pooled = contract(grad_low, both[3][0], 1, 1) / area_value
     dpool_h = jnp.pad(grad_pooled.reshape(BATCHES, IMGS, HEAD), ((0, 0), (0, 3), (0, 0))).reshape(16, HEAD)
-    (g_exp, g_taps, g_sq, g_ex, g_exb, g_sqb, g_head, back_e, back_c, back_h) = run_backward_all(
+    extra = jnp.concatenate(
+        [
+            jnp.pad(grad_class_bias, (0, CLASS_PAD - CLASSES)).reshape(8, LANES),
+            jnp.broadcast_to(loss, (8, LANES)),
+        ]
+    )
+    pooled_parts = pooled_low[0].reshape(SLOTS, n_sh, HEAD // n_sh).transpose(1, 0, 2)
+    pooled_parts = jnp.pad(pooled_parts, ((0, 0), (0, 6), (0, FACT - CLASS_PAD - HEAD // n_sh)))
+    facts = jnp.concatenate(
+        [
+            jnp.broadcast_to(
+                jnp.pad(grad_low, ((0, 6), (0, CLASS_PAD - CLASSES)))[None], (n_sh, 16, CLASS_PAD)
+            ),
+            pooled_parts,
+        ],
+        2,
+    )
+    (packed, back_e, back_c, back_h) = run_backward_all(
         sizes,
         [
-            dpool_h, mask_all, spread_l, spread_r, area, both[0][0], headt[0],
+            dpool_h, extra, mask_all, spread_l, spread_r, area, both[0][0], headt[0],
             taps[0], squeeze[0], excite[0], vec_e[0], vec_c[0], vec_h[0], *kept,
         ],
-    )
-    g_chan = jnp.concatenate([g_taps, g_sq, g_ex], 1)
-    summed = lax.psum(
-        (loss, g_exp, g_chan, g_head, grad_class, g_exb[:, 0], g_sqb[:, 0], grad_class_bias),
-        ("dp", "shard"),
     )
     place = lax.axis_index("shard")
 
@@ -1017,65 +1505,28 @@
     for layer in range(L):
         vectors = vectors + norm_grads(tot_e[layer, 0], back_e[layer, :, 0], EC)
         vectors = vectors + norm_grads(tot_e[layer, 1], back_e[layer, :, 1], EC)
-        vectors = vectors + [summed[5][layer]]
+        vectors = vectors + [back_e[layer, 1, 0, 24 : 24 + EC].reshape(E)]
         vectors = vectors + norm_grads(tot_c[layer], back_c[layer], 2)
-        vectors = vectors + [summed[6][layer]]
-    vectors = vectors + norm_grads(tot_h, back_h, HC) + [summed[7]]
-    owned = (
-        own_slice(summed[1], 1, n_sh, place),
-        own_slice(summed[2], 2, n_sh, place),
-        own_slice(summed[3], 0, n_sh, place).T,
-        own_slice(summed[4], 0, n_sh, place),
-        own_slice(pack_gains(vectors, n_sh), 0, n_sh, place),
-    )
-    total_loss = summed[0]
+        vectors = vectors + [back_e[layer, 1, 0, 24 + EC, :SE]]
+    vectors = vectors + norm_grads(tot_h, back_h, HC) + [back_h[1, 24:32].reshape(CLASS_PAD)[:CLASSES]]
+    total_loss = back_h[1, 32, 0]
     power = step[0].astype(F32)
     first_fix = 1.0 - jnp.power(jnp.float32(BETA_ONE), power)
     second_fix = 1.0 - jnp.power(jnp.float32(BETA_TWO), power)
-    states = [
-        adapt(firsts[item], seconds[item], owned[item], first_fix, second_fix) for item in range(5)
-    ]
-    updates = [states[item][2] + DECAY * weights[item] for item in range(4)]
-    local_weight_sq = jnp.concatenate(
-        [
-            mats_groups(expand_w),
-            chan_groups(chan_w),
-            jnp.sum(head_w * head_w)[None],
-            jnp.sum(class_w * class_w)[None],
-        ]
+    fixes = jnp.broadcast_to(jnp.stack([first_fix, second_fix])[:, None], (2, LANES))
+    new = run_update(
+        sizes,
+        packed,
+        facts,
+        fixes,
+        [(weights[k], firsts[k], seconds[k], averaged[k]) for k in range(4)],
     )
-    local_update_sq = jnp.concatenate(
-        [
-            mats_groups(updates[0]),
-            chan_groups(updates[1]),
-            jnp.sum(updates[2] * updates[2])[None],
-            jnp.sum(updates[3] * updates[3])[None],
-        ]
-    )
-    weight_sq, update_sq = lax.psum((local_weight_sq, local_update_sq), "shard")
-    ratio = jnp.sqrt(weight_sq) / jnp.sqrt(update_sq)
-    count_mats = 2 * L
-    count_chan = 3 * L
-    factors = [
-        mats_factor(ratio[:count_mats], expand_w),
-        chan_factor(ratio[count_mats : count_mats + count_chan], chan_w),
-        ratio[count_mats + count_chan],
-        ratio[count_mats + count_chan + 1],
-    ]
-    result = [total_loss]
-    for item in range(5):
-        if item < 4:
-            fresh = weights[item] - RATE * factors[item] * updates[item]
-        else:
-            fresh = weights[item] - RATE * states[item][2]
-        result = result + [
-            fresh,
-            states[item][0],
-            states[item][1],
-            KEEP * averaged[item] + (1.0 - KEEP) * fresh,
-        ]
-    norms = jnp.stack([jnp.sqrt(weight_sq), jnp.sqrt(update_sq)])
-    return tuple(result + [norms])
+    gain_grad = own_slice(pack_gains(vectors, n_sh), 0, n_sh, place)
+    gain_first, gain_second, gain_update = adapt(gain_m, gain_v, gain_grad, first_fix, second_fix)
+    gain_new = gain_w - RATE * gain_update
+    gains_out = [gain_new, gain_first, gain_second, KEEP * gain_e + (1.0 - KEEP) * gain_new]
+    norms = new[16][:, 0].reshape(2, GROUPS)
+    return tuple([total_loss] + list(new[:16]) + gains_out + [norms])
 
 
 def solution(mesh):

time: 708 us -> 555 us (0.78)
  waiting for transfers between devices: 206 us -> 0.11 us
  Pallas kernels: 267 us -> 363 us
  blocking collectives: 104 us -> 60.6 us
  local copies, waits for them, and re-layouts: 39.5 us -> 77.5 us
  other arithmetic: 57.2 us -> 24.5 us
    psum x1 -> x0, waiting for transfers between devices: 206 us -> none  [per_device(): lax.psum((loss, g_exp, g_chan, g_head, grad_class, g_exb[:, 0], g_sqb[:,...]
    pallas_call x0 -> x1, Pallas kernels: none -> 97.5 us  [run_update(): pl.pallas_call(functools.partial(update_kernel, sizes), out_shape=outs, i...]
    psum x2 -> x0, blocking collectives: 47.9 us -> none  [the longest x1 41.7 us: per_device(): lax.psum((loss, g_exp, g_chan, g_head, grad_class, g_exb[:, 0], g_sqb[:,...]
    unnamed x98 -> x125, local copies, waits for them, and re-layouts: 6.49 us -> 38.6 us
    reduce_sum x14 -> x1, other arithmetic: 21.4 us -> 0.24 us  [objective(): jnp.sum(onehot * logp, 1)]
  transfers between devices with their start and end apart: 5 -> 4, of which waited for: 1 -> 0; matrix products, arithmetic and copies ran while one was open for 9% -> 12% of each run, Pallas kernels for 19% -> 24%
where the time goes in v3:
time: 555 us; the launch traced here: 549 us
  Pallas kernels  363 us (65%)
  local copies, waits for them, and re-layouts  77.5 us (14%)
  blocking collectives  60.6 us (11%)
  other arithmetic  24.5 us (4%)
  between operations  17.6 us (3%)
    pallas_call x1, Pallas kernels, run_backward_all(): pl.pallas_call(functools.partial(backward_kernel, sizes), out_shape=outs,...  135 us
    pallas_call x1, Pallas kernels, run_forward_all(): pl.pallas_call(functools.partial(forward_kernel, sizes), out_shape=[o[0]...  131 us
    pallas_call x1, Pallas kernels, run_update(): pl.pallas_call(functools.partial(update_kernel, sizes), out_shape=outs, i...  97.5 us
    all_gather x6, blocking collectives, per_device(): lax.all_gather(item.astype(BF16), 'shard', axis=axes[k], tiled=True)  60.6 us
    unnamed x125, local copies, waits for them, and re-layouts  38.6 us
  transfers between devices with their start and end apart: 4, of which 0 were waited for; matrix products, arithmetic and copies ran while one was open for 12% of the time, Pallas kernels for 24%

profile of v3, /device:TPU:0, one launch (start us, length us, event | category | flops | bytes accessed | tf_op | source)
XLA Modules:
  0.0 549.3 jit_solution(5547648914291992602)
XLA Ops:
  7.2 2.5 convert_element_type.102
  9.8 1.0 convert_element_type.101
  11.4 1.0 convert_element_type.112
  12.5 0.9 convert_element_type.111
  14.7 6.3 %all-gather.1 = bf16[4,1,5018]{2,1,0:T(2,128)(2,1)S(1)} all-gather(bf16[1,1,5018]{2,1,0:T(2,128)(2,1)S(1)} %convert_bitcast_fusion.4), channel_id=1, replica_groups=mesh['dp'=8,'shard'=4] {'shard'}, dimensions={0}, use_global_device_ids=true | all-gather | bytes 50180 | tf_op jit(solution)/shard_map/all_gather | solution.py:1404
  21.1 6.0 %all-gather = bf16[4,1,5018]{2,1,0:T(2,128)(2,1)S(1)} all-gather(bf16[1,1,5018]{2,1,0:T(2,128)(2,1)S(1)} %convert_bitcast_fusion.5), channel_id=1, replica_groups=mesh['dp'=8,'shard'=4] {'shard'}, dimensions={0}, use_global_device_ids=true | all-gather | bytes 50180 | tf_op jit(solution)/shard_map/all_gather | solution.py:1404
  28.2 14.4 %all_gather.35 = bf16[2,137,1536]{2,1,0:T(8,128)(2,1)S(1)} all-gather(bf16[2,137,384]{2,1,0:T(8,128)(2,1)S(1)} %copy.347), channel_id=1, replica_groups=mesh['dp'=8,'shard'=4] {'shard'}, dimensions={2}, use_global_device_ids=true | all-gather | bytes 1052160 | tf_op jit(solution)/shard_map/all_gather | solution.py:1404
  42.8 9.3 %all_gather.34 = bf16[2,137,1536]{2,1,0:T(8,128)(2,1)S(1)} all-gather(bf16[2,137,384]{2,1,0:T(8,128)(2,1)S(1)} %copy.346), channel_id=1, replica_groups=mesh['dp'=8,'shard'=4] {'shard'}, dimensions={2}, use_global_device_ids=true | all-gather | bytes 1052160 | tf_op jit(solution)/shard_map/all_gather | solution.py:1404
  52.1 0.8 maximum_convert_fusion.1.refs_8_
  53.5 1.4 convert_bitcast_fusion
  55.2 12.0 %all_gather.33 = bf16[256,1280]{0,1:T(8,128)(2,1)} all-gather(bf16[256,320]{0,1:T(8,128)(2,1)S(1)} %convert_element_type.104), channel_id=1, replica_groups=mesh['dp'=8,'shard'=4] {'shard'}, dimensions={1}, use_global_device_ids=true | all-gather | bytes 819200 | tf_op jit(solution)/shard_map/all_gather | solution.py:1404
  67.2 12.5 %all_gather.32 = bf16[256,1280]{0,1:T(8,128)(2,1)} all-gather(bf16[256,320]{0,1:T(8,128)(2,1)S(1)} %convert_element_type.103), channel_id=1, replica_groups=mesh['dp'=8,'shard'=4] {'shard'}, dimensions={1}, use_global_device_ids=true | all-gather | bytes 819200 | tf_op jit(solution)/shard_map/all_gather | solution.py:1404
  82.0 1.4 maximum_bitcast_fusion.refs_7_
  85.4 1.7 reshape.359
  87.1 1.6 copy.414
  88.7 1.5 slice.360
  92.3 0.8 copy.358.refs_7_
  93.1 1.9 copy.361.refs_10_
  95.0 1.9 copy.362.refs_11_
  96.8 0.9 copy.365.refs_14_
  97.9 2.3 copy.345
  100.1 2.3 reshape.357.refs_0_
  106.0 0.8 eq.29
  106.8 0.8 add.120
  107.6 1.5 copy.415
  109.1 1.5 reshape.418.refs_11_
  113.4 1.8 copy.359.refs_8_
  115.2 0.8 copy.360.refs_9_
  116.0 1.9 copy.363.refs_12_
  117.9 1.9 copy.364.refs_13_
  120.0 0.9 slice_bitcast_fusion.refs_7_
  120.9 2.0 fusion.42
  123.0 6.0 %pad_maximum_fusion.refs_6_ = bf16[2,2,256,3072]{3,2,1,0:T(8,128)(2,1)} fusion(bf16[1,2,256,3072]{3,2,1,0:T(8,128)(2,1)} %bitcast.345, bf16[1,2,256,3072]{3,2,1,0:T(8,128)(2,1)} %bitcast.344), kind=kLoop, calls=%fused_computation | loop fusion | flops 3145728 | bytes 12582912 | tf_op jit(solution)/shard_map/stack | solution.py:1402
  129.0 1.1 broadcast_in_dim.34.refs_1_.refs_2_
  132.7 131.1 %forward.1 = (f32[2,12,1440,128]{3,2,1,0:T(8,128)}, f32[2,12,1440,128]{3,2,1,0:T(8,128)}, f32[10,1440,128]{2,1,0:T(8,128)}, f32[2,1440,256]{2,1,0:T(8,128)}, bf1...) custom-call(bf16[1440,256]{1,0:T(8,128)(2,1)} %reshape.357.refs_0_, ...), custom_call_target="tpu_custom_call" | custom-call | tf_op jit(solution)/shard_map/forward/pallas_call | solution.py:483
  263.8 0.9 convert_bitcast_fusion.3
  265.0 2.3 fusion.55
  268.2 2.5 fusion.56
  272.8 0.8 convolution_divide_fusion
  275.0 1.2 concatenate.13.refs_1_
  276.2 134.7 %backward.1 = (f32[4,576,8,128]{3,2,1,0:T(8,128)}, f32[2,2,2,40,128]{4,3,2,1,0:T(8,128)}, f32[2,2,8,128]{3,2,1,0:T(8,128)}, f32[2,40,128]{2,1,0:T(8,128)}) custom-call(f32[16,1280]{1,0:T(8,128)} %pad_bitcast_fusion.refs_0_, f32[16,128]{1,0:T(8,128)} %concatenate.13.refs_1_, f32[1440,128]{1,0:T(8,128)} %broadcast_in_dim.34.refs_1_.refs_2_, ...), custom_call_target="tpu_custom_call" | custom-call | tf_op jit(solution)/shard_map/backward/pallas_call | solution.py:916
  411.0 0.9 slice_bitcast_fusion.4
  413.2 1.2 slice.295
  417.2 97.5 %update.1 = (f32[2,64,3072]{2,1,0:T(8,128)}, f32[2,64,3072]{2,1,0:T(8,128)}, f32[2,64,3072]{2,1,0:T(8,128)}, f32[2,64,3072]{2,1,0:T(8,128)}, f32[2,137,384]{2,1,...) custom-call(f32[4,576,8,128]{3,2,1,0:T(8,128)} %get-tuple-element.68, ...), custom_call_target="tpu_custom_call" | custom-call | tf_op jit(solution)/shard_map/update/pallas_call | solution.py:1337
  514.8 2.1 copy.406
  516.9 2.0 copy.407
  518.9 1.0 copy.408
  519.9 1.0 copy.409
  520.9 0.9 copy.410
  521.7 0.9 copy.411
  522.6 0.9 copy.412
  523.5 0.9 copy.413
  527.5 0.8 multiply_add_fusion
  528.3 1.1 copy.671
  529.4 0.8 copy-done.9
  530.3 1.1 copy.672
  531.4 0.8 copy-done.8
  532.2 1.1 copy.673
  533.4 0.8 copy-done.7
  534.2 1.1 copy.674
  536.1 1.1 copy.675
  537.9 1.1 copy.676
  539.7 1.1 copy.677
  541.5 1.1 copy.678
  (260 shorter events, 31.5 us)
Async XLA Ops:
  7.2 2.6 copy-start.2
  7.2 115.8 %all-gather.9.cloned.1.call-start = ((), (), s32[]{:S(2)}) async-start(), calls=%async_computation.1 | async-start | bytes 3932160 | tf_op jit(solution)/shard_map/all_gather | solution.py:1404
  9.8 1.6 copy-start.3
  9.8 113.2 %all-gather.7.cloned.1.call-start = ((), (), s32[]{:S(2)}) async-start(), calls=%async_computation | async-start | bytes 3932160 | tf_op jit(solution)/shard_map/all_gather | solution.py:1404
  10.8 1.7 copy-start.4
  10.8 254.1 %all-gather.13.cloned.1.call-start = ((), (), s32[]{:S(2)}) async-start(), calls=%async_computation.3 | async-start | bytes 3276800 | tf_op jit(solution)/shard_map/all_gather | solution.py:1404
  12.4 2.3 copy-start.30
  12.4 8.7 %copy-start.32 = (f32[1,5018]{1,0:T(1,128)S(1)}, f32[1,5018]{1,0:T(1,128)}, u32[]{:S(2)}) copy-start(f32[1,5018]{1,0:T(1,128)} %param.48) | copy-start | bytes 60220
  12.4 15.6 %copy-start.6 = (f32[2,137,384]{2,0,1:T(2,128)S(1)}, f32[2,137,384]{2,0,1:T(2,128)}, u32[]{:S(2)}) copy-start(f32[2,137,384]{2,0,1:T(2,128)} %param.39) | copy-start | bytes 1262596
  12.4 255.8 %all-gather.11.cloned.1.call-start = ((), (), s32[]{:S(2)}) async-start(), calls=%async_computation.2 | async-start | bytes 3276800 | tf_op jit(solution)/shard_map/all_gather | solution.py:1404
  14.7 27.9 %copy-start.5 = (f32[2,137,384]{2,0,1:T(2,128)S(1)}, f32[2,137,384]{2,0,1:T(2,128)}, u32[]{:S(2)}) copy-start(f32[2,137,384]{2,0,1:T(2,128)} %param.36) | copy-start | bytes 1262596
  53.5 1.4 copy-start.44
  53.5 1.4 copy-start.42
  53.5 1.6 copy-start.16
  53.5 13.6 %copy-start.15 = (f32[256,320]{0,1:T(8,128)S(1)}, f32[256,320]{0,1:T(8,128)}, u32[]{:S(2)}) copy-start(f32[256,320]{0,1:T(8,128)} %param.40) | copy-start | bytes 983044
  79.9 2.1 copy-start.18
  82.0 2.8 copy-start.19
  82.0 8.3 %slice-start = ((f32[2,4,2,2064]{3,2,1,0:T(2,128)}), f32[2,4,2,128]{3,2,1,0:T(2,128)S(1)}, s32[]{:S(2)}) async-start(f32[2,4,2,2064]{3,2,1,0:T(2,128)} %copy-done.18), calls=%async_computation.4 | async-start | bytes 16384 | tf_op jit(solution)/shard_map/slice | solution.py:1435
  83.4 36.6 %copy-start.1 = (bf16[2,1280,256]{2,1,0:T(8,128)(2,1)}, bf16[2,1280,256]{2,1,0:T(8,128)(2,1)S(1)}, u32[]{:S(2)}) copy-start(bf16[2,1280,256]{2,1,0:T(8,128)(2,1)S(1)} %maximum_bitcast_fusion.refs_7_) | copy-start | bytes 3932164
  92.3 5.5 copy-start.39
  93.1 3.8 copy-start.17
  97.8 4.6 copy-start.34
  97.8 4.7 copy-start.20
  97.9 5.4 copy-start.35
  103.3 11.9 %copy-start.23 = (f32[2,137,384]{2,0,1:T(2,128)S(1)}, f32[2,137,384]{2,0,1:T(2,128)}, u32[]{:S(2)}) copy-start(f32[2,137,384]{2,0,1:T(2,128)} %param.38) | copy-start | bytes 1262596
  123.0 7.2 %copy-start.47 = (f32[144]{0:T(256)S(1)}, f32[144]{0:T(256)}, u32[]{:S(2)}) copy-start(f32[144]{0:T(256)} %compare_convert_fusion.1) | copy-start | bytes 1732
  123.0 9.1 %copy-start.46 = (f32[8]{0:T(128)S(1)}, f32[8]{0:T(128)}, u32[]{:S(2)}) copy-start(f32[8]{0:T(128)} %pad_maximum_fusion.1) | copy-start | bytes 100
  264.8 2.8 copy-start.24
  267.3 4.9 copy-start.43
  267.3 4.9 copy-start.45
  268.2 4.6 copy-start
  276.2 136.3 %copy-start.36 = (f32[2,8,128]{2,1,0:T(8,128)S(1)}, f32[2,8,128]{2,1,0:T(8,128)}, u32[]{:S(2)}) copy-start(f32[2,8,128]{2,1,0:T(8,128)} %get-tuple-element.65.refs_23_) | copy-start | bytes 24580
  276.2 140.4 %copy-start.48 = (f32[2]{0:T(128)S(1)}, f32[2]{0:T(128)}, u32[]{:S(2)}) copy-start(f32[2]{0:T(128)} %pad_maximum_fusion.2) | copy-start | bytes 28
  514.8 4.2 copy-start.22
  514.8 5.1 copy-start.21
  514.8 6.1 %copy-start.28 = (f32[256,320]{1,0:T(8,128)S(1)}, f32[256,320]{1,0:T(8,128)}, u32[]{:S(2)}) copy-start(f32[256,320]{1,0:T(8,128)} %get-tuple-element.207) | copy-start | bytes 983044
  516.9 4.9 copy-start.27
  518.9 3.7 copy-start.26
  519.9 3.6 copy-start.25
  522.6 2.6 copy-start.40
  523.5 2.6 copy-start.29
  523.5 3.1 copy-start.41
  524.4 3.1 copy-start.31
  524.4 3.1 copy-start.33
  524.4 3.1 copy-start.37
  524.4 3.1 copy-start.38
  524.4 3.9 copy-start.10
  528.3 2.0 copy-start.9
  530.3 2.0 copy-start.8
  532.2 2.0 copy-start.7
  534.2 1.9 copy-start.14
  536.1 1.8 copy-start.13
  537.9 1.8 copy-start.12
  539.7 1.8 copy-start.11
Sparse Core Ops, SparseCore 0:
  10.2 36.3 all-gather.8
  48.8 35.5 all-gather.6
  85.9 25.7 all-gather.12
  113.1 25.5 all-gather.10
